TPU v7x, 32 devices: a whole 2x2x4 slice. The times are simulated.
32 devices in a mesh: group: 2 (over x), seq: 4 (over y, core), tp: 4 (over z).
Axes of the slice: x: 2, y: 2, z: 4, core: 2. Of those that a mesh axis runs over, the one named last changes fastest.
Arguments:
- queries: bfloat16 [4096, 4096], P(('group', 'seq'), 'tp'), parts along dimension 0, may hold values from -32 to 32
- key_value: bfloat16 [4096, 2, 2048], P(('group', 'seq'), None, 'tp'), parts along dimension 0, may hold values from -32 to 32
- window_cache: bfloat16 [2048, 2, 2048], P('group', None, 'tp'), parts along dimension 0, may hold values from -5 to 5
- span_start: int32 [2], P('group'), parts along dimension 0, may hold values from 1024 to 30720
- hidden: bfloat16 [4096, 21504], P(('group', 'seq'), 'tp'), parts along dimension 0, may hold values from -6 to 6
- down_codes: int32 [21504, 2688], P('tp', 'seq'), may hold values from 0 to 15
- down_scales: int32 [168, 2688], P('tp', 'seq'), may hold values from 1 to 15
- out_weight: bfloat16 [4096, 2688], P('tp', 'seq'), may hold values from -0.375 to 0.375
Outputs:
- layer_update: bfloat16 [4096, 2688], P(('group', 'seq', 'tp')), parts along dimension 0
There are 2 independent parts, one for each index of `group`. A program takes and returns all parts, laid end to end along the dimension named above; an argument that names none is the same for every part. Nothing has to cross between parts.
All inputs are finite; a program needn't handle non-finite values.
Results may differ from a plain program's by a relative error of at most 0.02.
Values may be sent and summed in bfloat16 or wider, within the bound.
No kernel may reach another device: no remote copies, remote signals or barrier semaphores. Data moves between devices by JAX's collectives and lax.ppermute only.
A program may use at most 192 MiB of HBM per device.

v0:
```python
import jax
import jax.numpy as jnp
import numpy as np
from jax import lax
from jax.experimental import pallas as pl
from jax.experimental.pallas import tpu as pltpu
from jax.sharding import PartitionSpec as P

HD = 128
WINDOW = 1024
GROUP = 128


ROPE_BASE = 10000.0
SCORE_SCALE = 168.0 ** (-0.5)
CODE_STEP = 2.0 ** (-14)
INV_ROOT = 1344.0 ** (-0.5)


def shifted(value, axis, steps):
    count = lax.axis_size(axis)
    first, last = (max(0, -steps), min(count, count - steps))
    return lax.ppermute(value, axis, [(source, source + steps) for source in range(first, last)])


def swapped(x, axis, stride):
    return lax.ppermute(x, axis, [(i, i ^ 1 << stride) for i in range(lax.axis_size(axis))])


def bit_total(value_now):
    return (value_now & 1) + (value_now >> 1 & 1) + (value_now >> 2 & 1)


def build_tables():
    prime_order = 167
    residues = set((value_now * value_now % prime_order for value_now in range(1, prime_order)))
    legendre = [0] + [1 if value_now in residues else -1 for value_now in range(1, prime_order)]
    paley_table = np.eye(prime_order + 1)
    paley_table[0, 1:] += 1.0
    paley_table[1:, 0] -= 1.0
    for row_index in range(prime_order):
        for col_index in range(prime_order):
            paley_table[row_index + 1, col_index + 1] += legendre[
                (col_index - row_index) % prime_order
            ]
    sylvester = np.array(
        [
            [(-1.0) ** bit_total(left_bit & right_bit) for right_bit in range(8)]
            for left_bit in range(8)
        ]
    )
    return (paley_table, sylvester)


def rotary(values, cosine, sine_part):
    half_dim = values.shape[-1] // 2
    first_half = values[..., :half_dim]
    second_half = values[..., half_dim:]
    return jnp.concatenate(
        [
            first_half * cosine - second_half * sine_part,
            second_half * cosine + first_half * sine_part,
        ],
        axis=-1,
    )


def section_pairs(blocks_now, section_level):
    row_count, block_count, width_cols = blocks_now.shape
    paired = blocks_now.reshape(
        row_count, block_count >> section_level + 1, 2, 1 << section_level, width_cols
    ).astype(jnp.float32)
    upper_half = paired[:, :, 0]
    lower_half = paired[:, :, 1]
    mixed = jnp.stack([upper_half + lower_half, upper_half - lower_half], axis=2)
    return mixed.astype(jnp.bfloat16).reshape(row_count, block_count, width_cols)


def per_device(
    queries, key_value, window_cache, span_start, hidden, down_codes, down_scales, out_weight
):
    tok_rows = queries.shape[0]
    tp_count = lax.axis_size("tp")
    seq_index = lax.axis_index("seq")
    tp_index = lax.axis_index("tp")
    heads_dev = queries.shape[1] // HD
    kv_dev = key_value.shape[2] // HD
    group_size = heads_dev // kv_dev
    first_pos = span_start[0]
    positions = first_pos + seq_index * tok_rows + jnp.arange(tok_rows, dtype=jnp.int32)
    inv_freq = ROPE_BASE ** (-(2.0 * jnp.arange(HD // 2, dtype=jnp.float32)) / HD)
    angles = positions.astype(jnp.float32)[:, None] * inv_freq[None, :]
    cosine = jnp.cos(angles)[:, None, :]
    sine_part = jnp.sin(angles)[:, None, :]
    query_rot = rotary(
        queries.reshape(tok_rows, heads_dev, HD).astype(jnp.float32), cosine, sine_part
    ).astype(jnp.bfloat16)
    key_rot = rotary(
        key_value[:, 0].reshape(tok_rows, kv_dev, HD).astype(jnp.float32), cosine, sine_part
    ).astype(jnp.bfloat16)
    own_pairs = jnp.stack([key_rot.reshape(tok_rows, kv_dev * HD), key_value[:, 1]], axis=1)
    reach_blocks = WINDOW // tok_rows
    earlier = []
    moving = own_pairs
    for hop_count in range(reach_blocks):
        moving = shifted(moving, "seq", 1)
        earlier.insert(0, moving)
    halo_rows = jnp.concatenate(earlier, axis=0)
    doubled = jnp.concatenate([window_cache, window_cache], axis=0)
    ordered = lax.dynamic_slice_in_dim(doubled, first_pos % WINDOW, WINDOW, 0)
    padded_cache = jnp.concatenate([ordered, jnp.zeros_like(ordered)], axis=0)
    from_cache = lax.dynamic_slice_in_dim(
        padded_cache, jnp.minimum(seq_index * tok_rows, WINDOW), WINDOW, 0
    )
    halo_rows = halo_rows + from_cache
    all_rows = jnp.concatenate([halo_rows, own_pairs], axis=0)
    key_count = all_rows.shape[0]
    key_rows = all_rows[:, 0].reshape(key_count, kv_dev, HD)
    value_rows = all_rows[:, 1].reshape(key_count, kv_dev, HD)
    grouped = query_rot.reshape(tok_rows, kv_dev, group_size, HD)
    scores = (
        jnp.einsum("qkgd,skd->kgqs", grouped, key_rows, preferred_element_type=jnp.float32)
        * SCORE_SCALE
    )
    query_ids = jnp.arange(tok_rows)[:, None]
    key_ids = jnp.arange(key_count)[None, :]
    allowed = (key_ids > query_ids) & (key_ids <= query_ids + WINDOW)
    scores = jnp.where(allowed, scores, -jnp.inf)
    top_score = jnp.max(scores, axis=-1, keepdims=True)
    weights_soft = jnp.exp(scores - top_score)
    weights_soft = (weights_soft / jnp.sum(weights_soft, axis=-1, keepdims=True)).astype(
        jnp.bfloat16
    )
    attended = jnp.einsum(
        "kgqs,skd->qkgd", weights_soft, value_rows, preferred_element_type=jnp.float32
    )
    attended = attended.astype(jnp.bfloat16).reshape(tok_rows, heads_dev * HD)
    paley_np, sylvester_np = build_tables()
    paley_table = jnp.asarray(paley_np, dtype=jnp.bfloat16)
    sylvester = jnp.asarray(sylvester_np, dtype=jnp.float32)
    local_blocks = hidden.shape[1] // 1344
    local_levels = local_blocks.bit_length() - 1
    parts_now = hidden.reshape(tok_rows, local_blocks, 8, 168)
    mixed = jnp.einsum("nbac,cd->nbad", parts_now, paley_table, preferred_element_type=jnp.float32)
    mixed = (
        jnp.einsum("nbad,ae->nbed", mixed, sylvester, precision=lax.Precision.HIGHEST) * INV_ROOT
    )
    blocks_now = mixed.reshape(tok_rows, local_blocks, 1344).astype(jnp.bfloat16)
    for section_level in range(local_levels):
        blocks_now = section_pairs(blocks_now, section_level)
    for bit_index in range(tp_count.bit_length() - 1):
        partner = swapped(blocks_now, "tp", bit_index)
        high_side = jnp.right_shift(tp_index, bit_index) % 2
        own_values = blocks_now.astype(jnp.float32)
        other_values = partner.astype(jnp.float32)
        blocks_now = jnp.where(
            high_side == 0, own_values + other_values, other_values - own_values
        ).astype(jnp.bfloat16)
    rotated = blocks_now.reshape(tok_rows, local_blocks * 1344)
    joined = jnp.concatenate([rotated, attended], axis=1)
    group_count = down_scales.shape[0]
    col_count = down_codes.shape[1]
    down_weight = (
        (down_codes.reshape(group_count, GROUP, col_count) - 8) * down_scales[:, None, :]
    ).astype(jnp.float32) * CODE_STEP
    down_rows = down_weight.astype(jnp.bfloat16).reshape(group_count * GROUP, col_count)
    stacked = jnp.concatenate([down_rows, out_weight], axis=0)
    partials = jnp.dot(
        joined,
        lax.all_gather(stacked, "seq", axis=1, tiled=True),
        preferred_element_type=jnp.float32,
    )
    layer_update = lax.psum_scatter(
        partials.astype(jnp.bfloat16), "tp", scatter_dimension=0, tiled=True
    )
    return layer_update


BLOCK = 1344
PADDED = 1408
CHUNKS = ((0, 192), (192, 192), (384, 144), (528, 144))
NT = (((1,), (1,)), ((), ()))
ANYWHERE = pl.BlockSpec(memory_space=pl.ANY)


def cost(microseconds):
    return pl.CostEstimate(
        flops=1 + int(microseconds * 1.15e9), bytes_accessed=1, transcendentals=0
    )


def fits(mesh):
    return dict(mesh.shape) == {"group": 2, "seq": 4, "tp": 4}


def mix_tables():
    paley_np, sylvester_np = build_tables()
    mix_np = np.kron(sylvester_np, paley_np)
    low = np.zeros((PADDED, PADDED), np.float32)
    high = np.zeros((PADDED, PADDED), np.float32)
    low[:BLOCK, :BLOCK] = mix_np
    high[PADDED - BLOCK :, :BLOCK] = mix_np
    return jnp.asarray(np.stack([low, high]), dtype=jnp.bfloat16)


def mix_kernel(hidden_ref, table_ref, *refs):
    out_ref = refs[-1]
    gap = PADDED - BLOCK
    pair = 2 * BLOCK

    def product(first, table):
        return jnp.dot(
            hidden_ref[:, first : first + PADDED],
            table_ref[table],
            preferred_element_type=jnp.float32,
        )

    sums, differences = [], []
    for half in range(2):
        even = product(half * pair, 0)
        odd = product(half * pair + BLOCK - gap, 1)
        sums.append(even + odd)
        differences.append(even - odd)
    for half in range(2):
        if half == 0:
            even, odd = sums[0] + sums[1], differences[0] + differences[1]
        else:
            even, odd = sums[0] - sums[1], differences[0] - differences[1]
        even, odd = even * INV_ROOT, pltpu.roll(odd * INV_ROOT, gap, 1)
        first, edge = half * pair, BLOCK - gap
        out_ref[:, first : first + edge] = even[:, :edge].astype(jnp.bfloat16)
        out_ref[:, first + edge : first + PADDED] = (even[:, edge:] + odd[:, : 2 * gap]).astype(
            jnp.bfloat16
        )
        out_ref[:, first + PADDED : first + pair] = odd[:, 2 * gap :].astype(jnp.bfloat16)


def mix_hidden(hidden, *earlier):
    rows, width = hidden.shape
    step = 256
    return pl.pallas_call(
        mix_kernel,
        grid=(rows // step,),
        in_specs=[
            pl.BlockSpec((step, width), lambda i: (i, 0)),
            pl.BlockSpec((2, PADDED, PADDED), lambda i: (0, 0, 0)),
        ]
        + [ANYWHERE] * len(earlier),
        out_specs=pl.BlockSpec((step, width), lambda i: (i, 0)),
        out_shape=jax.ShapeDtypeStruct((rows, width), jnp.bfloat16),
        compiler_params=pltpu.CompilerParams(vmem_limit_bytes=56 << 20),
        cost_estimate=cost(16),
    )(hidden, mix_tables(), *earlier)


def dequant_kernel(first, half_ref, codes_ref, scales_ref, spread_ref, *refs):
    out_ref, wide = refs[-2:]
    step = codes_ref.shape[0]

    @pl.when(pl.program_id(0) == 0)
    def _():
        scales = scales_ref[:, first : first + wide.shape[0]].astype(jnp.bfloat16)
        wide[...] = lax.dot_general(
            scales, spread_ref[...], (((0,), (0,)), ((), ())), preferred_element_type=jnp.float32
        )

    rows = pl.ds(pl.multiple_of(pl.program_id(0) * step, step), step)
    out_ref[...] = ((codes_ref[...] - 8).astype(jnp.float32) * wide[rows, :]).astype(jnp.bfloat16)


def dequant(half_id, codes, scales, chunk, earlier=()):
    width = codes.shape[1] // 2
    first, size = CHUNKS[chunk]
    step = 48
    groups = scales.shape[0]
    spread = np.repeat(np.eye(groups, dtype=np.float32) * CODE_STEP, GROUP, axis=1)
    return pl.pallas_call(
        lambda *refs: dequant_kernel(first, *refs),
        grid_spec=pltpu.PrefetchScalarGridSpec(
            num_scalar_prefetch=1,
            grid=(size // step,),
            in_specs=[
                pl.BlockSpec((step, width), lambda i, half: (first // step + i, half[0])),
                pl.BlockSpec(scales.shape, lambda i, half: (0, 0)),
                pl.BlockSpec((groups, width), lambda i, half: (0, half[0])),
            ]
            + [ANYWHERE] * len(earlier),
            out_specs=pl.BlockSpec((step, width), lambda i, half: (i, 0)),
            scratch_shapes=[pltpu.VMEM((size, width), jnp.float32)],
        ),
        out_shape=jax.ShapeDtypeStruct((size, width), jnp.bfloat16),
        cost_estimate=cost(3),
    )(half_id, codes, scales, jnp.asarray(spread, dtype=jnp.bfloat16), *earlier)


def level_kernel(sign_ref, own_ref, partner_ref, *refs):
    out_ref = refs[-1]
    sign = sign_ref[0].astype(jnp.float32).astype(jnp.bfloat16)
    out_ref[...] = own_ref[...] * sign + partner_ref[...]


def level_step(value, bit, earlier=()):
    partner = flipped(value, "tp", bit)
    sign = jnp.where(lax.axis_index("tp") & bit == 0, 1, -1).reshape(1)
    size, width = value.shape
    step = 96 if size % 96 == 0 else 48
    spec = pl.BlockSpec((step, width), lambda i, sign: (i, 0))
    return pl.pallas_call(
        level_kernel,
        grid_spec=pltpu.PrefetchScalarGridSpec(
            num_scalar_prefetch=1,
            grid=(size // step,),
            in_specs=[spec, spec] + [ANYWHERE] * len(earlier),
            out_specs=spec,
        ),
        out_shape=jax.ShapeDtypeStruct(value.shape, jnp.bfloat16),
        cost_estimate=cost(3),
    )(sign, value, partner, *earlier)


def gate_kernel(*refs):
    pass


def gate(value, *earlier):
    return pl.pallas_call(
        gate_kernel,
        in_specs=[ANYWHERE] * (1 + len(earlier)),
        out_specs=ANYWHERE,
        out_shape=jax.ShapeDtypeStruct(value.shape, value.dtype),
        input_output_aliases={0: 0},
        cost_estimate=cost(0),
    )(value, *earlier)


def project_kernel(chunks, count, place_ref, *refs):
    row_refs, attn_refs, out_side = refs[:count], refs[count : 2 * count], refs[2 * count]
    weights = refs[2 * count + 1 : 2 * count + 1 + 2 * len(chunks)]
    out_ref, total = refs[-2:]
    step = pl.program_id(0)
    steps = pl.num_programs(0)
    rows = row_refs[0].shape[0]
    shards = out_ref.shape[0]
    kept = rows // shards

    def add(parts, sources, first):
        part = jnp.concatenate(parts, axis=0)
        for place, ref in enumerate(sources):
            lanes = slice(place * rows, (place + 1) * rows)
            value = lax.dot_general(part, ref[...], NT, preferred_element_type=jnp.float32)
            total[:, lanes] = value if first else total[:, lanes] + value

    @pl.when(step == 0)
    def _():
        add([out_side[first : first + size, :] for first, size in chunks], attn_refs, True)

    @pl.when(step < steps // 2)
    def _():
        add([ref[...] for ref in weights[0::2]], row_refs, False)

    @pl.when(step >= steps // 2)
    def _():
        add([ref[...] for ref in weights[1::2]], row_refs, False)

    @pl.when(step == steps - 1)
    def _():
        for shard in range(shards):
            for place in range(count):
                first = place * rows + shard * kept
                out_ref[shard, :, place * kept : (place + 1) * kept] = total[
                    :, first : first + kept
                ].astype(jnp.bfloat16)


def project(place, shards, row_parts, attn, flips, out_side, weights, chunks, earlier=()):
    count = len(row_parts)
    rows, width = row_parts[0].shape
    steps = 6
    depth = width // steps
    last = steps // 2 - 1
    columns = sum(size for _, size in chunks)
    weight_specs = []
    for _, size in chunks:
        weight_specs += [
            pl.BlockSpec((size, depth), lambda i, h: (0, jnp.minimum(i, last))),
            pl.BlockSpec((size, depth), lambda i, h: (0, jnp.maximum(i - last - 1, 0))),
        ]
    row_spec = pl.BlockSpec((rows, depth), lambda i, h: (0, lax.rem(i + h[0] * (last + 1), steps)))

    def attn_spec(flip):
        return pl.BlockSpec((rows, attn.shape[1]), lambda i, h: (h[1] ^ flip, 0))

    shape = (shards, columns, count * rows // shards)
    return pl.pallas_call(
        lambda *refs: project_kernel(chunks, count, *refs),
        grid_spec=pltpu.PrefetchScalarGridSpec(
            num_scalar_prefetch=1,
            grid=(steps,),
            in_specs=[row_spec] * count
            + [attn_spec(flip) for flip in flips]
            + [pl.BlockSpec(out_side.shape, lambda i, h: (0, 0))]
            + weight_specs
            + [ANYWHERE] * len(earlier),
            out_specs=pl.BlockSpec(shape, lambda i, h: (0, 0, 0)),
            scratch_shapes=[pltpu.VMEM((columns, count * rows), jnp.float32)],
        ),
        out_shape=jax.ShapeDtypeStruct(shape, jnp.bfloat16),
        compiler_params=pltpu.CompilerParams(vmem_limit_bytes=56 << 20),
        cost_estimate=cost(10),
    )(place, *row_parts, *[attn] * count, out_side, *weights, *earlier)


def turned(head, cosine, signed_sine):
    head = head.astype(jnp.float32)
    return (head * cosine + pltpu.roll(head, HD // 2, 1) * signed_sine).astype(jnp.bfloat16)


def attend_kernel(
    place_ref,
    query_ref,
    cosine_ref,
    sine_ref,
    key0,
    value0,
    key1,
    value1,
    cached_key1,
    cached_value1,
    key2,
    value2,
    cached_key2,
    cached_value2,
    out_ref,
):
    rows = query_ref.shape[0]

    def chosen(block, halo, cached):
        return jnp.where(place_ref[0] >= block, halo[...], cached[...])

    key1, value1 = chosen(1, key1, cached_key1), chosen(1, value1, cached_value1)
    key2, value2 = chosen(2, key2, cached_key2), chosen(2, value2, cached_value2)
    keys = [
        turned(
            key,
            cosine_ref[block * rows : (block + 1) * rows, :],
            sine_ref[block * rows : (block + 1) * rows, :],
        )
        for block, key in enumerate((key0[...], key1, key2))
    ]
    half = rows // 2
    heads = query_ref.shape[1] // HD
    for part in range(2):
        low = part * half
        here = slice(low, low + half)
        own = slice(0, low + half)
        old = slice(low, rows)
        query = jnp.concatenate(
            [
                turned(
                    query_ref[here, head * HD : (head + 1) * HD],
                    cosine_ref[here, :],
                    sine_ref[here, :],
                )
                for head in range(heads)
            ],
            axis=0,
        )

        def score(block):
            return (
                lax.dot_general(query, block, NT, preferred_element_type=jnp.float32) * SCORE_SCALE
            )

        def places(count, first):
            query_at = lax.broadcasted_iota(jnp.int32, (heads, half, count), 1) + low
            key_at = lax.broadcasted_iota(jnp.int32, (heads, half, count), 2) + first
            shape = (heads * half, count)
            return query_at.reshape(shape), key_at.reshape(shape)

        score0, score1, score2 = score(keys[0][own, :]), score(keys[1]), score(keys[2][old, :])
        query_at, key_at = places(low + half, 0)
        score0 = jnp.where(key_at <= query_at, score0, -jnp.inf)
        query_at, key_at = places(rows - low, low)
        score2 = jnp.where(key_at > query_at, score2, -jnp.inf)
        top = jnp.maximum(
            jnp.max(score0, axis=1, keepdims=True),
            jnp.maximum(
                jnp.max(score1, axis=1, keepdims=True), jnp.max(score2, axis=1, keepdims=True)
            ),
        )
        mass = jnp.zeros_like(top)
        total = jnp.zeros((heads * half, HD), jnp.float32)
        for scores, values in (
            (score0, value0[own, :]),
            (score1, value1),
            (score2, value2[old, :]),
        ):
            weight = jnp.exp(scores - top)
            mass += jnp.sum(weight, axis=1, keepdims=True)
            total += jnp.dot(
                weight.astype(jnp.bfloat16), values, preferred_element_type=jnp.float32
            )
        total = (total / mass).astype(jnp.bfloat16)
        for head in range(heads):
            out_ref[here, head * HD : (head + 1) * HD] = total[head * half : (head + 1) * half]


def attend(place, queries, cosine, signed_sine, pairs, all_pairs, cached1, cached2):
    rows, width = queries.shape
    kv_heads = pairs.shape[1] // (2 * HD)
    wide = width // kv_heads

    def specs(back):
        def row(p):
            return 0 if back is None else jnp.maximum(p[0] - back, 0)

        return [
            pl.BlockSpec((rows, HD), lambda i, p: (row(p), i)),
            pl.BlockSpec((rows, HD), lambda i, p: (row(p), kv_heads + i)),
        ]

    table_spec = pl.BlockSpec(cosine.shape, lambda i, p: (0, 0))
    query_spec = pl.BlockSpec((rows, wide), lambda i, p: (0, i))
    return pl.pallas_call(
        attend_kernel,
        grid_spec=pltpu.PrefetchScalarGridSpec(
            num_scalar_prefetch=1,
            grid=(kv_heads,),
            in_specs=[query_spec, table_spec, table_spec]
            + specs(None)
            + specs(1)
            + specs(None)
            + specs(2)
            + specs(None),
            out_specs=query_spec,
        ),
        out_shape=jax.ShapeDtypeStruct(queries.shape, jnp.bfloat16),
        compiler_params=pltpu.CompilerParams(vmem_limit_bytes=56 << 20),
        cost_estimate=cost(13),
    )(
        place,
        queries,
        cosine,
        signed_sine,
        pairs,
        pairs,
        all_pairs,
        all_pairs,
        cached1,
        cached1,
        all_pairs,
        all_pairs,
        cached2,
        cached2,
    )


def flipped(value, axis, bit):
    return lax.ppermute(value, axis, [(i, i ^ bit) for i in range(lax.axis_size(axis))])


def planned(
    queries, key_value, window_cache, span_start, hidden, down_codes, down_scales, out_weight
):
    half_id = lax.axis_index("group").reshape(1)
    seq_index = lax.axis_index("seq")
    core = seq_index & 1
    side = seq_index >> 1
    tok_rows = queries.shape[0]

    pairs = key_value.reshape(tok_rows, -1)
    all_pairs = lax.all_gather(pairs, "seq", axis=0, tiled=True)

    codes = down_codes.T
    out_own = out_weight.T
    piece_a = dequant(half_id, codes, down_scales, 0)
    piece_c = dequant(half_id, codes, down_scales, 1, (piece_a, pairs))
    rotated = mix_hidden(hidden, piece_c)
    piece_b = dequant(half_id, codes, down_scales, 2, (rotated,))
    piece_d = dequant(half_id, codes, down_scales, 3, (piece_b,))

    def both_cores(value):
        return [value, flipped(value, "seq", 1)]

    own_rows = both_cores(rotated)
    piece_a = level_step(piece_a, 2)
    piece_c = level_step(piece_c, 1, (piece_a,))
    first_pos = gate(span_start, piece_c)[0]

    block_first = first_pos + (seq_index - jnp.arange(3, dtype=jnp.int32)) * tok_rows
    positions = block_first[:, None] + jnp.arange(tok_rows, dtype=jnp.int32)[None, :]
    inv_freq = ROPE_BASE ** (-(2.0 * jnp.arange(HD // 2, dtype=jnp.float32)) / HD)
    angles = positions.astype(jnp.float32)[:, :, None] * inv_freq
    turn = (seq_index >= jnp.arange(3))[:, None, None]
    cosine, sine = jnp.where(turn, jnp.cos(angles), 1.0), jnp.where(turn, jnp.sin(angles), 0.0)
    cosine = jnp.concatenate([cosine, cosine], axis=2).reshape(-1, HD)
    signed_sine = jnp.concatenate([-sine, sine], axis=2).reshape(-1, HD)
    cache = gate(window_cache, piece_c).reshape(WINDOW, -1)
    doubled = jnp.concatenate([cache, cache], axis=0)
    first1 = (first_pos + tok_rows) % WINDOW
    first2 = (first_pos + jnp.minimum(seq_index, 1) * tok_rows) % WINDOW
    cached1 = lax.dynamic_slice_in_dim(doubled, first1, tok_rows, 0)
    cached2 = lax.dynamic_slice_in_dim(doubled, first2, tok_rows, 0)
    attended = attend(
        seq_index.reshape(1), queries, cosine, signed_sine, pairs, all_pairs, cached1, cached2
    )

    piece_b = level_step(piece_b, 2, (piece_c, attended))
    piece_d = level_step(piece_d, 1, (piece_b, own_rows[1]))
    piece_a = level_step(piece_a, 1, (piece_d,))
    across_a = flipped(piece_a, "group", 1)
    piece_c = level_step(piece_c, 2, (piece_a,))
    across_c = flipped(piece_c, "group", 1)
    piece_b = level_step(piece_b, 1, (piece_c, across_a))
    across_b = flipped(piece_b, "group", 1)
    piece_d = level_step(piece_d, 2, (piece_b, across_c))
    across_d = flipped(piece_d, "group", 1)

    shards = lax.axis_size("tp")
    place = jnp.stack([half_id[0], seq_index])
    all_attended = lax.all_gather(attended, "seq", axis=0, tiled=True)

    def reduced(rows, flips, weights, chunks, earlier=()):
        partial = project(
            place, shards, rows, all_attended, flips, out_own, weights, chunks, earlier
        )
        return lax.psum_scatter(partial, "tp", scatter_dimension=0, tiled=True)[0], partial

    early, late = [piece_a, across_a, piece_c, across_c], [piece_b, across_b, piece_d, across_d]
    own_early, own_done = reduced(own_rows, (0, 1), early, CHUNKS[:2], (piece_d,))
    far_rows = both_cores(gate(flipped(rotated, "seq", 2), own_done, across_b))
    far_early, far_done = reduced(far_rows, (2, 3), early, CHUNKS[:2], (across_d,))
    all_late, _ = reduced(own_rows + far_rows, (0, 1, 2, 3), late, CHUNKS[2:], (far_done,))
    kept = tok_rows // shards
    sums = jnp.concatenate([own_early, far_early], axis=1)
    sums = jnp.concatenate([sums, all_late], axis=0)
    strips = [sums[:, i * kept : (i + 1) * kept] for i in range(4)]
    strips = strips[:1] + [flipped(strips[i], "seq", i) for i in (1, 2, 3)]
    strips = [jnp.where(core == 0, strips[i], strips[i ^ 1]) for i in range(4)]
    strips = [jnp.where(side == 0, strips[i], strips[i ^ 2]) for i in range(4)]
    return jnp.concatenate(strips, axis=0).T


def solution(mesh):
    return jax.shard_map(
        planned if fits(mesh) else per_device,
        mesh=mesh,
        in_specs=(
            P(("group", "seq"), "tp"),
            P(("group", "seq"), None, "tp"),
            P("group", None, "tp"),
            P("group"),
            P(("group", "seq"), "tp"),
            P("tp", "seq"),
            P("tp", "seq"),
            P("tp", "seq"),
        ),
        out_specs=P(("group", "seq", "tp"), None),
        check_vma=False,
    )
```

profile of v0, /device:TPU:0, one launch (start us, length us, event | category | flops | bytes accessed | tf_op | source)
XLA Modules:
  0.0 364.6 jit_solution(9291615286722615223)
XLA Ops:
  6.5 4.4 %copy.27.refs_0_ = bf16[1024,2,512]{2,1,0:T(2,128)(2,1)} copy(bf16[1024,2,512]{2,1,0:T(2,128)(2,1)} %param.15) | data formatting | bytes 4194304
  11.0 1.2 copy.18
  12.3 4.3 %shard_map.127.refs_4_.own_ref = bf16[192,2688]{1,0:T(8,128)(2,1)} custom-call(s32[1]{0:T(128)} %bitcast.refs_0_, s32[672,5376]{1,0:T(8,128)} %bitcast.16, s32[42,672]{1,0:T(8,128)} %refs_2_.7, bf16[42,5376]{1,0:T(8,128)(2,1)} %constant.57.clone.refs_3_), custom_call_target="tpu_custom_call" | custom-call | flops 3450000128 | bytes 1 | tf_op jit(solution)/shard_map/pallas_call | solution.py:277
  16.5 4.0 %collective-permute-start.2 = (bf16[192,2688]{1,0:T(8,128)(2,1)}, bf16[192,2688]{1,0:T(8,128)(2,1)S(1)}, u32[]{:S(2)}, u32[]{:S(2)}) collective-permute-start(bf16[192,2688]{1,0:T(8,128)(2,1)} %shard_map.127.refs_4_.own_ref), channel_id=1, source_target_pairs={{0,2},{1,3},{2,0},{3,1},{4,6},{5,7},{6,4},{7,5},{8,10},{9,11},{10,... | collective-permute-start | bytes 3096584 | tf_op jit(solution)/shard_map/ppermute | solution.py:559
  20.6 4.5 %shard_map.128.refs_0_.own_ref = bf16[192,2688]{1,0:T(8,128)(2,1)} custom-call(s32[1]{0:T(128)} %bitcast.refs_0_, s32[672,5376]{1,0:T(8,128)} %bitcast.17, s32[42,672]{1,0:T(8,128)} %refs_2_.7, bf16[42,5376]{1,0:T(8,128)(2,1)} %constant.57.clone.refs_3_, bf16[192,2688]{1,0:T(8,128)(2,1)} %shard_map.127.refs_4_.own_ref, bf16[512,1024]{1,0:T(8,128)(2,1)} %bitcast.24), custom_call_target="tpu_custom_call" | custom-call | flops 3450000128 | bytes 1 | tf_op jit(solution)/shard_map/pallas_call | solution.py:277
  25.1 1.5 collective-permute-start.1
  26.6 16.5 %shard_map.129.refs_4_.refs_1_ = bf16[512,5376]{1,0:T(8,128)(2,1)} custom-call(bf16[512,5376]{1,0:T(8,128)(2,1)} %hidden_ref.1, bf16[2,1408,1408]{2,1,0:T(8,128)(2,1)} %constant.58.clone.table_ref, bf16[192,2688]{1,0:T(8,128)(2,1)} %shard_map.128.refs_0_.own_ref), custom_call_target="tpu_custom_call" | custom-call | flops 18400000000 | bytes 1 | tf_op jit(solution)/shard_map/pallas_call | solution.py:241
  43.9 21.9 %collective-permute-done.2.partner_ref = bf16[192,2688]{1,0:T(8,128)(2,1)S(1)} collective-permute-done((bf16[192,2688]{1,0:T(8,128)(2,1)}, bf16[192,2688]{1,0:T(8,128)(2,1)S(1)}, u32[]{:S(2)}, u32[]{:S(2)}) %collective-permute-start.2) | collective-permute-done | bytes 1032224 | tf_op jit(solution)/shard_map/ppermute | solution.py:559
  65.8 1.0 copy-done.8
  66.8 2.4 shard_map.130.refs_0_.own_ref
  69.1 1.3 collective-permute-done.1.partner_ref
  71.4 2.3 shard_map.131.refs_1_.refs_0_.own_ref
  76.1 2.1 copy.19
  78.6 2.9 fusion.2
  81.5 1.6 pad_maximum_fusion
  83.2 1.9 constant_dynamic-slice_fusion
  85.0 14.2 %shard_map.134.refs_1_ = bf16[512,1024]{1,0:T(8,128)(2,1)} custom-call(s32[1]{0:T(128)} %bitcast.1.place_ref, bf16[512,1024]{1,0:T(8,128)(2,1)} %query_ref.1, f32[1536,128]{1,0:T(8,128)} %get-tuple-element.17.cosine_ref, f32[1536,128]{1,0:T(8,128)} %get-tuple-element.18.sine_ref, bf16[512,1024]{1,0:T(8,128)(2,1)} %bitcast.25, bf16[512,1024]{1,0:T(8,128)(2,1)} %bitcast.26, ...), custom_call_target="tpu_custom_call" | custom-call | flops 14949999616 | bytes 1 | tf_op jit(solution)/shard_map/pallas_call | solution.py:524
  99.3 1.6 collective-permute-start.11
  100.9 3.7 %shard_map.135.refs_4_.own_ref = bf16[144,2688]{1,0:T(8,128)(2,1)} custom-call(s32[1]{0:T(128)} %bitcast.refs_0_, s32[672,5376]{1,0:T(8,128)} %bitcast.18, s32[42,672]{1,0:T(8,128)} %refs_2_.7, bf16[42,5376]{1,0:T(8,128)(2,1)} %constant.57.clone.refs_3_, bf16[512,5376]{1,0:T(8,128)(2,1)} %shard_map.129.refs_4_.refs_1_), custom_call_target="tpu_custom_call" | custom-call | flops 3450000128 | bytes 1 | tf_op jit(solution)/shard_map/pallas_call | solution.py:277
  105.1 4.2 %shard_map.136.own_ref = bf16[144,2688]{1,0:T(8,128)(2,1)} custom-call(s32[1]{0:T(128)} %bitcast.refs_0_, s32[672,5376]{1,0:T(8,128)} %bitcast.19, s32[42,672]{1,0:T(8,128)} %refs_2_.7, bf16[42,5376]{1,0:T(8,128)(2,1)} %constant.57.clone.refs_3_, bf16[144,2688]{1,0:T(8,128)(2,1)} %shard_map.135.refs_4_.own_ref), custom_call_target="tpu_custom_call" | custom-call | flops 3450000128 | bytes 1 | tf_op jit(solution)/shard_map/pallas_call | solution.py:277
  109.3 2.1 collective-permute-start.4
  111.5 28.5 %collective-permute-done.5.partner_ref = bf16[144,2688]{1,0:T(8,128)(2,1)} collective-permute-done((bf16[144,2688]{1,0:T(8,128)(2,1)}, bf16[144,2688]{1,0:T(8,128)(2,1)}, u32[]{:S(2)}, u32[]{:S(2)}) %collective-permute-start.5) | collective-permute-done | bytes 774176 | tf_op jit(solution)/shard_map/ppermute | solution.py:559
  139.9 3.1 shard_map.137.refs_0_.own_ref
  143.1 22.9 %collective-permute-done.4.partner_ref = bf16[144,2688]{1,0:T(8,128)(2,1)} collective-permute-done((bf16[144,2688]{1,0:T(8,128)(2,1)}, bf16[144,2688]{1,0:T(8,128)(2,1)}, u32[]{:S(2)}, u32[]{:S(2)}) %collective-permute-start.4) | collective-permute-done | bytes 774176 | tf_op jit(solution)/shard_map/ppermute | solution.py:559
  166.0 3.2 shard_map.138.refs_0_.own_ref
  169.2 18.8 %collective-permute-done.3.partner_ref = bf16[192,2688]{1,0:T(8,128)(2,1)S(1)} collective-permute-done((bf16[192,2688]{1,0:T(8,128)(2,1)S(1)}, bf16[192,2688]{1,0:T(8,128)(2,1)S(1)}, u32[]{:S(2)}, u32[]{:S(2)}) %collective-permute-start.3) | collective-permute-done | bytes 1032224 | tf_op jit(solution)/shard_map/ppermute | solution.py:559
  188.0 1.0 copy-done.9
  189.0 2.4 shard_map.139.refs_0_.refs_6_
  191.4 1.5 collective-permute-start.6
  192.9 2.4 shard_map.140.refs_0_.refs_8_
  195.8 3.1 collective-permute-start.9
  199.5 22.0 %collective-permute-done.10.partner_ref = bf16[144,2688]{1,0:T(8,128)(2,1)} collective-permute-done((bf16[144,2688]{1,0:T(8,128)(2,1)}, bf16[144,2688]{1,0:T(8,128)(2,1)}, u32[]{:S(2)}, u32[]{:S(2)}) %collective-permute-start.10) | collective-permute-done | bytes 774176 | tf_op jit(solution)/shard_map/ppermute | solution.py:559
  222.4 3.1 shard_map.141.refs_0_.refs_10_
  225.6 3.5 collective-permute-done.9.partner_ref
  229.1 10.5 %collective-permute-done.8.refs_1_.refs_9_ = bf16[192,2688]{1,0:T(8,128)(2,1)} collective-permute-done((bf16[192,2688]{1,0:T(8,128)(2,1)}, bf16[192,2688]{1,0:T(8,128)(2,1)}, u32[]{:S(2)}, u32[]{:S(2)}) %collective-permute-start.8) | collective-permute-done | bytes 1032224 | tf_op jit(solution)/shard_map/ppermute | solution.py:559
  239.6 3.1 shard_map.142.refs_10_.refs_12_
  242.7 13.7 %shard_map.143.refs_1_ = bf16[4,384,256]{2,1,0:T(8,128)(2,1)} custom-call(s32[2]{0:T(128)} %pad_add_fusion.refs_0_, bf16[512,5376]{1,0:T(8,128)(2,1)} %shard_map.129.refs_4_.refs_1_, bf16[512,5376]{1,0:T(8,128)(2,1)} %collective-permute-done.refs_1_.refs_2_, bf16[2048,1024]{1,0:T(8,128)(2,1)} %all-gather.5.cloned.1.call-done.refs_3_.refs_4_.refs_5_.refs_6_.refs_7_.refs_8_, ...), custom_call_target="tpu_custom_call" | custom-call | flops 11500000256 | bytes 1 | tf_op jit(solution)/shard_map/pallas_call | solution.py:394
  257.8 1.5 collective-permute-start.14
  259.4 17.7 %collective-permute-done.14.refs_10_.refs_13_ = bf16[144,2688]{1,0:T(8,128)(2,1)S(1)} collective-permute-done((bf16[144,2688]{1,0:T(8,128)(2,1)S(1)}, bf16[144,2688]{1,0:T(8,128)(2,1)S(1)}, u32[]{:S(2)}, u32[]{:S(2)}) %collective-permute-start.14) | collective-permute-done | bytes 774176 | tf_op jit(solution)/shard_map/ppermute | solution.py:559
  277.9 13.7 %shard_map.145.refs_14_ = bf16[4,384,256]{2,1,0:T(8,128)(2,1)} custom-call(s32[2]{0:T(128)} %pad_add_fusion.refs_0_, bf16[512,5376]{1,0:T(8,128)(2,1)} %shard_map.144.refs_1_.refs_3_, bf16[512,5376]{1,0:T(8,128)(2,1)} %collective-permute-done.13.refs_2_.refs_4_, ...), custom_call_target="tpu_custom_call" | custom-call | flops 11500000256 | bytes 1 | tf_op jit(solution)/shard_map/pallas_call | solution.py:394
  291.7 18.7 %shard_map.146 = bf16[4,288,512]{2,1,0:T(8,128)(2,1)} custom-call(s32[2]{0:T(128)} %pad_add_fusion.refs_0_, bf16[512,5376]{1,0:T(8,128)(2,1)} %shard_map.129.refs_4_.refs_1_, bf16[512,5376]{1,0:T(8,128)(2,1)} %collective-permute-done.refs_1_.refs_2_, bf16[512,5376]{1,0:T(8,128)(2,1)} %shard_map.144.refs_1_.refs_3_, ...), custom_call_target="tpu_custom_call" | custom-call | flops 11500000256 | bytes 1 | tf_op jit(solution)/shard_map/pallas_call | solution.py:394
  310.5 3.9 %reduce-scatter.6.cloned.1.call-done = bf16[1,384,256]{2,1,0:T(8,128)(2,1)} async-done(((bf16[4,384,256]{2,1,0:T(8,128)(2,1)}), bf16[1,384,256]{2,1,0:T(8,128)(2,1)}) %reduce-scatter.6.cloned.1.call-update) | async-done | bytes 196624 | tf_op jit(solution)/shard_map/reduce_scatter | solution.py:627
  314.4 30.6 %reduce-scatter.8.cloned.1.call-done = bf16[1,288,512]{2,1,0:T(8,128)(2,1)} async-done(((bf16[4,288,512]{2,1,0:T(8,128)(2,1)}), bf16[1,288,512]{2,1,0:T(8,128)(2,1)}) %reduce-scatter.8.cloned.1.call-update) | async-done | bytes 294928 | tf_op jit(solution)/shard_map/reduce_scatter | solution.py:627
  345.0 1.2 pad_maximum_fusion.2
  346.3 1.6 collective-permute-start.17
  348.5 4.2 %collective-permute-done.17 = bf16[672,128]{1,0:T(8,128)(2,1)S(1)} collective-permute-done((bf16[672,128]{1,0:T(8,128)(2,1)S(1)}, bf16[672,128]{1,0:T(8,128)(2,1)S(1)}, u32[]{:S(2)}, u32[]{:S(2)}) %collective-permute-start.17) | collective-permute-done | bytes 172064 | tf_op jit(solution)/shard_map/ppermute | solution.py:559
  352.7 4.1 %collective-permute-done.16 = bf16[672,128]{1,0:T(8,128)(2,1)S(1)} collective-permute-done((bf16[672,128]{1,0:T(8,128)(2,1)S(1)}, bf16[672,128]{1,0:T(8,128)(2,1)S(1)}, u32[]{:S(2)}, u32[]{:S(2)}) %collective-permute-start.16) | collective-permute-done | bytes 172064 | tf_op jit(solution)/shard_map/ppermute | solution.py:559
  356.9 1.1 copy.17
  (68 shorter events, 8.7 us)
Async XLA Ops:
  6.5 4.4 %copy-start.2 = (bf16[512,2,512]{2,1,0:T(2,128)(2,1)S(1)}, bf16[512,2,512]{2,1,0:T(2,128)(2,1)}, u32[]{:S(2)}) copy-start(bf16[512,2,512]{2,1,0:T(2,128)(2,1)} %param.14) | copy-start | bytes 3145732
  6.5 78.5 %all-gather.3.cloned.1.call-start = ((), (), s32[]{:S(2)}) async-start(), calls=%async_computation.3 | async-start | bytes 5242880 | tf_op jit(solution)/shard_map/all_gather | solution.py:572
  12.2 230.5 %all-gather.5.cloned.1.call-start = ((), (), s32[]{:S(2)}) async-start(), calls=%async_computation.4 | async-start | bytes 5242880 | tf_op jit(solution)/shard_map/all_gather | solution.py:621
  16.5 49.3 %collective-permute-start.2 = (bf16[192,2688]{1,0:T(8,128)(2,1)}, bf16[192,2688]{1,0:T(8,128)(2,1)S(1)}, u32[]{:S(2)}, u32[]{:S(2)}) collective-permute-start(bf16[192,2688]{1,0:T(8,128)(2,1)} %shard_map.127.refs_4_.own_ref), channel_id=1, source_target_pairs={{0,2},{1,3},{2,0},{3,1},{4,6},{5,7},{6,4},{7,5},{8,10},{9,11},{10,... | collective-permute-start | bytes 3096584 | tf_op jit(solution)/shard_map/ppermute | solution.py:559
  25.1 45.4 %collective-permute-start.1 = (bf16[192,2688]{1,0:T(8,128)(2,1)}, bf16[192,2688]{1,0:T(8,128)(2,1)S(1)}, u32[]{:S(2)}, u32[]{:S(2)}) collective-permute-start(bf16[192,2688]{1,0:T(8,128)(2,1)} %shard_map.128.refs_0_.own_ref), channel_id=1, source_target_pairs={{0,1},{1,0},{2,3},{3,2},{4,5},{5,4},{6,7},{7,6},{8,9},{9,8},{10,11... | collective-permute-start | bytes 3096584 | tf_op jit(solution)/shard_map/ppermute | solution.py:559
  43.1 122.9 %collective-permute-start = (bf16[512,5376]{1,0:T(8,128)(2,1)}, bf16[512,5376]{1,0:T(8,128)(2,1)}, u32[]{:S(2)}, u32[]{:S(2)}) collective-permute-start(bf16[512,5376]{1,0:T(8,128)(2,1)} %shard_map.129.refs_4_.refs_1_), channel_id=1, source_target_pairs={{0,4},{4,0},{8,12},{12,8},{1,5},{5,1},{9,13},{13,9},{2,6},{6,2},{1... | collective-permute-start | bytes 16515080 | tf_op jit(solution)/shard_map/ppermute | solution.py:559
  65.8 1.0 copy-start.8
  70.4 1.0 copy-start.7
  99.2 211.2 %reduce-scatter.4.cloned.1.call-start = ((), (), s32[]{:S(2)}) async-start(), calls=%async_computation.5 | async-start | bytes 983040 | tf_op jit(solution)/shard_map/reduce_scatter | solution.py:627
  99.3 157.1 %collective-permute-start.11 = (bf16[512,5376]{1,0:T(8,128)(2,1)}, bf16[512,5376]{1,0:T(8,128)(2,1)}, u32[]{:S(2)}, u32[]{:S(2)}) collective-permute-start(bf16[512,5376]{1,0:T(8,128)(2,1)} %shard_map.129.refs_4_.refs_1_), channel_id=1, source_target_pairs={{0,8},{4,12},{8,0},{12,4},{1,9},{5,13},{9,1},{13,5},{2,10},{6,14},... | collective-permute-start | bytes 16515080 | tf_op jit(solution)/shard_map/ppermute | solution.py:559
  104.6 6.8 %copy-start.5 = (bf16[192,2688]{1,0:T(8,128)(2,1)S(1)}, bf16[192,2688]{1,0:T(8,128)(2,1)}, u32[]{:S(2)}) copy-start(bf16[192,2688]{1,0:T(8,128)(2,1)} %shard_map.130.refs_0_.own_ref) | copy-start | bytes 3096580
  104.6 35.4 %copy-start = (bf16[192,2688]{1,0:T(8,128)(2,1)S(1)}, bf16[192,2688]{1,0:T(8,128)(2,1)}, u32[]{:S(2)}) copy-start(bf16[192,2688]{1,0:T(8,128)(2,1)} %shard_map.131.refs_1_.refs_0_.own_ref) | copy-start | bytes 3096580
  104.6 35.4 %collective-permute-start.5 = (bf16[144,2688]{1,0:T(8,128)(2,1)}, bf16[144,2688]{1,0:T(8,128)(2,1)}, u32[]{:S(2)}, u32[]{:S(2)}) collective-permute-start(bf16[144,2688]{1,0:T(8,128)(2,1)} %shard_map.135.refs_4_.own_ref), channel_id=1, source_target_pairs={{0,2},{1,3},{2,0},{3,1},{4,6},{5,7},{6,4},{7,5},{8,10},{9,11},{10,... | collective-permute-start | bytes 2322440 | tf_op jit(solution)/shard_map/ppermute | solution.py:559
  109.3 56.8 %collective-permute-start.4 = (bf16[144,2688]{1,0:T(8,128)(2,1)}, bf16[144,2688]{1,0:T(8,128)(2,1)}, u32[]{:S(2)}, u32[]{:S(2)}) collective-permute-start(bf16[144,2688]{1,0:T(8,128)(2,1)} %shard_map.136.own_ref), channel_id=1, source_target_pairs={{0,1},{1,0},{2,3},{3,2},{4,5},{5,4},{6,7},{7,6},{8,9},{9,8},{10,11... | collective-permute-start | bytes 2322440 | tf_op jit(solution)/shard_map/ppermute | solution.py:559
  111.4 76.6 %collective-permute-start.3 = (bf16[192,2688]{1,0:T(8,128)(2,1)S(1)}, bf16[192,2688]{1,0:T(8,128)(2,1)S(1)}, u32[]{:S(2)}, u32[]{:S(2)}) collective-permute-start(bf16[192,2688]{1,0:T(8,128)(2,1)S(1)} %copy-done.5), channel_id=1, source_target_pairs={{0,1},{1,0},{2,3},{3,2},{4,5},{5,4},{6,7},{7,6},{8,9},{9,8},{10,11... | collective-permute-start | bytes 3096584 | tf_op jit(solution)/shard_map/ppermute | solution.py:559
  139.9 52.9 %collective-permute-start.7 = (bf16[192,2688]{1,0:T(8,128)(2,1)S(1)}, bf16[192,2688]{1,0:T(8,128)(2,1)}, u32[]{:S(2)}, u32[]{:S(2)}) collective-permute-start(bf16[192,2688]{1,0:T(8,128)(2,1)S(1)} %copy-done), channel_id=1, source_target_pairs={{0,2},{1,3},{2,0},{3,1},{4,6},{5,7},{6,4},{7,5},{8,10},{9,11},{10,... | collective-permute-start | bytes 3096584 | tf_op jit(solution)/shard_map/ppermute | solution.py:559
  188.0 1.0 copy-start.9
  191.4 4.4 %copy-start.10 = (bf16[144,2688]{1,0:T(8,128)(2,1)S(1)}, bf16[144,2688]{1,0:T(8,128)(2,1)}, u32[]{:S(2)}) copy-start(bf16[144,2688]{1,0:T(8,128)(2,1)} %shard_map.138.refs_0_.own_ref) | copy-start | bytes 2322436
  191.4 30.1 %collective-permute-start.6 = (bf16[192,2688]{1,0:T(8,128)(2,1)}, bf16[192,2688]{1,0:T(8,128)(2,1)S(1)}, u32[]{:S(2)}, u32[]{:S(2)}) collective-permute-start(bf16[192,2688]{1,0:T(8,128)(2,1)} %shard_map.139.refs_0_.refs_6_), channel_id=1, source_target_pairs={{0,16},{16,0},{1,17},{17,1},{2,18},{18,2},{3,19},{19,3},{4,20},{20... | collective-permute-start | bytes 3096584 | tf_op jit(solution)/shard_map/ppermute | solution.py:559
  192.9 28.6 %collective-permute-start.10 = (bf16[144,2688]{1,0:T(8,128)(2,1)}, bf16[144,2688]{1,0:T(8,128)(2,1)}, u32[]{:S(2)}, u32[]{:S(2)}) collective-permute-start(bf16[144,2688]{1,0:T(8,128)(2,1)} %shard_map.137.refs_0_.own_ref), channel_id=1, source_target_pairs={{0,1},{1,0},{2,3},{3,2},{4,5},{5,4},{6,7},{7,6},{8,9},{9,8},{10,11... | collective-permute-start | bytes 2322440 | tf_op jit(solution)/shard_map/ppermute | solution.py:559
  195.2 44.3 %collective-permute-start.8 = (bf16[192,2688]{1,0:T(8,128)(2,1)}, bf16[192,2688]{1,0:T(8,128)(2,1)}, u32[]{:S(2)}, u32[]{:S(2)}) collective-permute-start(bf16[192,2688]{1,0:T(8,128)(2,1)} %shard_map.140.refs_0_.refs_8_), channel_id=1, source_target_pairs={{0,16},{16,0},{1,17},{17,1},{2,18},{18,2},{3,19},{19,3},{4,20},{20... | collective-permute-start | bytes 3096584 | tf_op jit(solution)/shard_map/ppermute | solution.py:559
  195.8 33.3 %collective-permute-start.9 = (bf16[144,2688]{1,0:T(8,128)(2,1)S(1)}, bf16[144,2688]{1,0:T(8,128)(2,1)S(1)}, u32[]{:S(2)}, u32[]{:S(2)}) collective-permute-start(bf16[144,2688]{1,0:T(8,128)(2,1)S(1)} %copy-done.10), channel_id=1, source_target_pairs={{0,2},{1,3},{2,0},{3,1},{4,6},{5,7},{6,4},{7,5},{8,10},{9,11},{10,... | collective-permute-start | bytes 2322440 | tf_op jit(solution)/shard_map/ppermute | solution.py:559
  221.5 1.0 copy-start.6
  225.6 30.8 %collective-permute-start.12 = (bf16[144,2688]{1,0:T(8,128)(2,1)}, bf16[144,2688]{1,0:T(8,128)(2,1)S(1)}, u32[]{:S(2)}, u32[]{:S(2)}) collective-permute-start(bf16[144,2688]{1,0:T(8,128)(2,1)} %shard_map.141.refs_0_.refs_10_), channel_id=1, source_target_pairs={{0,16},{16,0},{1,17},{17,1},{2,18},{18,2},{3,19},{19,3},{4,20},{20... | collective-permute-start | bytes 2322440 | tf_op jit(solution)/shard_map/ppermute | solution.py:559
  229.1 10.5 %copy-start.11 = (bf16[144,2688]{1,0:T(8,128)(2,1)}, bf16[144,2688]{1,0:T(8,128)(2,1)S(1)}, u32[]{:S(2)}) copy-start(bf16[144,2688]{1,0:T(8,128)(2,1)S(1)} %collective-permute-done.9.partner_ref) | copy-start | bytes 2322436
  256.4 1.4 copy-start.3
  256.4 0.9 copy-start.1
  257.3 19.7 %collective-permute-start.13 = (bf16[512,5376]{1,0:T(8,128)(2,1)}, bf16[512,5376]{1,0:T(8,128)(2,1)}, u32[]{:S(2)}, u32[]{:S(2)}) collective-permute-start(bf16[512,5376]{1,0:T(8,128)(2,1)} %shard_map.144.refs_1_.refs_3_), channel_id=1, source_target_pairs={{0,4},{4,0},{8,12},{12,8},{1,5},{5,1},{9,13},{13,9},{2,6},{6,2},{1... | collective-permute-start | bytes 16515080 | tf_op jit(solution)/shard_map/ppermute | solution.py:559
  257.8 19.2 %collective-permute-start.14 = (bf16[144,2688]{1,0:T(8,128)(2,1)S(1)}, bf16[144,2688]{1,0:T(8,128)(2,1)S(1)}, u32[]{:S(2)}, u32[]{:S(2)}) collective-permute-start(bf16[144,2688]{1,0:T(8,128)(2,1)S(1)} %copy-done.3), channel_id=1, source_target_pairs={{0,16},{16,0},{1,17},{17,1},{2,18},{18,2},{3,19},{19,3},{4,20},{20... | collective-permute-start | bytes 2322440 | tf_op jit(solution)/shard_map/ppermute | solution.py:559
  259.3 55.1 %reduce-scatter.6.cloned.1.call-start = ((), (), s32[]{:S(2)}) async-start(), calls=%async_computation.6 | async-start | bytes 983040 | tf_op jit(solution)/shard_map/reduce_scatter | solution.py:627
  277.0 0.9 copy-start.4
  291.7 53.3 %reduce-scatter.8.cloned.1.call-start = ((), (), s32[]{:S(2)}) async-start(), calls=%async_computation.7 | async-start | bytes 1474560 | tf_op jit(solution)/shard_map/reduce_scatter | solution.py:627
  346.3 2.2 collective-permute-start.15
  346.3 6.3 %collective-permute-start.17 = (bf16[672,128]{1,0:T(8,128)(2,1)S(1)}, bf16[672,128]{1,0:T(8,128)(2,1)S(1)}, u32[]{:S(2)}, u32[]{:S(2)}) collective-permute-start(bf16[672,128]{1,0:T(8,128)(2,1)S(1)} %get-tuple-element.12), channel_id=1, source_target_pairs={{0,12},{4,8},{8,4},{12,0},{1,13},{5,9},{9,5},{13,1},{2,14},{6,10},... | collective-permute-start | bytes 516104 | tf_op jit(solution)/shard_map/ppermute | solution.py:559
  348.0 8.8 %collective-permute-start.16 = (bf16[672,128]{1,0:T(8,128)(2,1)S(1)}, bf16[672,128]{1,0:T(8,128)(2,1)S(1)}, u32[]{:S(2)}, u32[]{:S(2)}) collective-permute-start(bf16[672,128]{1,0:T(8,128)(2,1)S(1)} %get-tuple-element.13), channel_id=1, source_target_pairs={{0,8},{4,12},{8,0},{12,4},{1,9},{5,13},{9,1},{13,5},{2,10},{6,14},... | collective-permute-start | bytes 516104 | tf_op jit(solution)/shard_map/ppermute | solution.py:559
Sparse Core Ops, SparseCore 0:
  12.3 40.3 all-gather.2
  99.3 57.0 all-gather.4
  259.4 21.6 reduce-scatter.3
  291.8 22.4 reduce-scatter.5
  316.5 28.4 reduce-scatter.7
where the time goes:
time: 366 us; the launch traced here: 365 us
  waiting for transfers between devices  190 us (52%)
  Pallas kernels  116 us (32%)
  starting transfers between devices  18.9 us (5%)
  local copies, waits for them, and re-layouts  17.5 us (5%)
  between operations  15.1 us (4%)
  other arithmetic  7.1 us (2%)
    ppermute x18, waiting for transfers between devices, flipped(): lax.ppermute(value, axis, [(i, i ^ bit) for i in range(lax.axis_size(axis...  155 us
    pallas_call x3, Pallas kernels, project(): pl.pallas_call(lambda *refs: project_kernel(chunks, count, *refs), grid_s...  46.1 us
    reduce_scatter x3, waiting for transfers between devices, reduced(): lax.psum_scatter(partial, 'tp', scatter_dimension=0, tiled=True)[0]  34.6 us
    pallas_call x8, Pallas kernels, level_step(): pl.pallas_call(level_kernel, grid_spec=pltpu.PrefetchScalarGridSpec(num_s...  22 us
    ppermute x18, starting transfers between devices, flipped(): lax.ppermute(value, axis, [(i, i ^ bit) for i in range(lax.axis_size(axis...  18.8 us
    pallas_call x4, Pallas kernels, dequant(): pl.pallas_call(lambda *refs: dequant_kernel(first, *refs), grid_spec=pltp...  16.6 us
    pallas_call x1, Pallas kernels, mix_hidden(): pl.pallas_call(mix_kernel, grid=(rows // step,), in_specs=[pl.BlockSpec((...  16.5 us
    unnamed x28, local copies, waits for them, and re-layouts  14.2 us
  transfers between devices with their start and end apart: 23, of which 13 were waited for; matrix products, arithmetic and copies ran while one was open for 3% of the time, Pallas kernels for 32%

commit v1 on v0

--- a/solution.py
+++ b/solution.py
@@ -176,9 +176,13 @@
     return layer_update
 
 
-BLOCK = 1344
-PADDED = 1408
-CHUNKS = ((0, 192), (192, 192), (384, 144), (528, 144))
+PIECE = 672
+SHIFT = 96
+WINDOWED = PIECE + SHIFT
+HALF = 336
+WIDE = 192
+EARLY = ((0, WIDE), (HALF, WIDE))
+LATE = ((WIDE, HALF - WIDE), (HALF + WIDE, HALF - WIDE))
 NT = (((1,), (1,)), ((), ()))
 ANYWHERE = pl.BlockSpec(memory_space=pl.ANY)
 
@@ -195,44 +199,45 @@
 
 def mix_tables():
     paley_np, sylvester_np = build_tables()
-    mix_np = np.kron(sylvester_np, paley_np)
-    low = np.zeros((PADDED, PADDED), np.float32)
-    high = np.zeros((PADDED, PADDED), np.float32)
-    low[:BLOCK, :BLOCK] = mix_np
-    high[PADDED - BLOCK :, :BLOCK] = mix_np
-    return jnp.asarray(np.stack([low, high]), dtype=jnp.bfloat16)
+    table = np.zeros((WINDOWED + SHIFT, WINDOWED), np.float32)
+    table[SHIFT : SHIFT + PIECE, :PIECE] = np.kron(sylvester_np[:4, :4], paley_np)
+    return jnp.asarray(table, dtype=jnp.bfloat16)
 
 
 def mix_kernel(hidden_ref, table_ref, *refs):
     out_ref = refs[-1]
-    gap = PADDED - BLOCK
-    pair = 2 * BLOCK
-
-    def product(first, table):
-        return jnp.dot(
-            hidden_ref[:, first : first + PADDED],
-            table_ref[table],
-            preferred_element_type=jnp.float32,
+    rows = hidden_ref.shape[0]
+    pair = 4 * PIECE
+    pieces = []
+    for place in range(4):
+        shift = place * PIECE % 128
+        first = place * PIECE - shift
+        stacked = jnp.concatenate(
+            [
+                hidden_ref[:, start + first : start + first + WINDOWED] for start in (0, pair)
+            ],
+            axis=0,
         )
-
-    sums, differences = [], []
+        table = table_ref[SHIFT - shift : SHIFT - shift + WINDOWED, :]
+        pieces.append(jnp.dot(stacked, table, preferred_element_type=jnp.float32) * INV_ROOT)
+    for bit in (1, 2):
+        pieces = [
+            pieces[i] + pieces[i ^ bit] if i & bit == 0 else pieces[i ^ bit] - pieces[i]
+            for i in range(4)
+        ]
     for half in range(2):
-        even = product(half * pair, 0)
-        odd = product(half * pair + BLOCK - gap, 1)
-        sums.append(even + odd)
-        differences.append(even - odd)
-    for half in range(2):
-        if half == 0:
-            even, odd = sums[0] + sums[1], differences[0] + differences[1]
-        else:
-            even, odd = sums[0] - sums[1], differences[0] - differences[1]
-        even, odd = even * INV_ROOT, pltpu.roll(odd * INV_ROOT, gap, 1)
-        first, edge = half * pair, BLOCK - gap
-        out_ref[:, first : first + edge] = even[:, :edge].astype(jnp.bfloat16)
-        out_ref[:, first + edge : first + PADDED] = (even[:, edge:] + odd[:, : 2 * gap]).astype(
-            jnp.bfloat16
-        )
-        out_ref[:, first + PADDED : first + pair] = odd[:, 2 * gap :].astype(jnp.bfloat16)
+        carried = None
+        for place in range(4):
+            upper, lower = pieces[place][:rows], pieces[place][rows:]
+            value = upper + lower if half == 0 else upper - lower
+            shift = place * PIECE % 128
+            first = half * pair + place * PIECE - shift
+            if shift:
+                value = pltpu.roll(value, shift, 1)
+                value = jnp.concatenate([value[:, :128] + carried, value[:, 128:]], axis=1)
+            keep = WINDOWED if place == 3 else WINDOWED - 128
+            out_ref[:, first : first + keep] = value[:, :keep].astype(jnp.bfloat16)
+            carried = value[:, keep:]
 
 
 def mix_hidden(hidden, *earlier):
@@ -243,13 +248,14 @@
         grid=(rows // step,),
         in_specs=[
             pl.BlockSpec((step, width), lambda i: (i, 0)),
-            pl.BlockSpec((2, PADDED, PADDED), lambda i: (0, 0, 0)),
+            pl.BlockSpec((WINDOWED + SHIFT, WINDOWED), lambda i: (0, 0)),
         ]
         + [ANYWHERE] * len(earlier),
         out_specs=pl.BlockSpec((step, width), lambda i: (i, 0)),
         out_shape=jax.ShapeDtypeStruct((rows, width), jnp.bfloat16),
         compiler_params=pltpu.CompilerParams(vmem_limit_bytes=56 << 20),
         cost_estimate=cost(16),
+        name="mix",
     )(hidden, mix_tables(), *earlier)
 
 
@@ -268,9 +274,8 @@
     out_ref[...] = ((codes_ref[...] - 8).astype(jnp.float32) * wide[rows, :]).astype(jnp.bfloat16)
 
 
-def dequant(half_id, codes, scales, chunk, earlier=()):
+def dequant(half_id, codes, scales, first, size, earlier=()):
     width = codes.shape[1] // 2
-    first, size = CHUNKS[chunk]
     step = 48
     groups = scales.shape[0]
     spread = np.repeat(np.eye(groups, dtype=np.float32) * CODE_STEP, GROUP, axis=1)
@@ -290,20 +295,21 @@
         ),
         out_shape=jax.ShapeDtypeStruct((size, width), jnp.bfloat16),
         cost_estimate=cost(3),
+        name="decode",
     )(half_id, codes, scales, jnp.asarray(spread, dtype=jnp.bfloat16), *earlier)
 
 
 def level_kernel(sign_ref, own_ref, partner_ref, *refs):
-    out_ref = refs[-1]
     sign = sign_ref[0].astype(jnp.float32).astype(jnp.bfloat16)
-    out_ref[...] = own_ref[...] * sign + partner_ref[...]
+    out_refs = refs[-1:]
+    out_refs[0][...] = own_ref[...] * sign + partner_ref[...]
 
 
 def level_step(value, bit, earlier=()):
     partner = flipped(value, "tp", bit)
     sign = jnp.where(lax.axis_index("tp") & bit == 0, 1, -1).reshape(1)
     size, width = value.shape
-    step = 96 if size % 96 == 0 else 48
+    step = next(rows for rows in (112, 96, 80, 64, 48) if size % rows == 0)
     spec = pl.BlockSpec((step, width), lambda i, sign: (i, 0))
     return pl.pallas_call(
         level_kernel,
@@ -315,6 +321,7 @@
         ),
         out_shape=jax.ShapeDtypeStruct(value.shape, jnp.bfloat16),
         cost_estimate=cost(3),
+        name="level",
     )(sign, value, partner, *earlier)
 
 
@@ -330,10 +337,11 @@
         out_shape=jax.ShapeDtypeStruct(value.shape, value.dtype),
         input_output_aliases={0: 0},
         cost_estimate=cost(0),
+        name="gate",
     )(value, *earlier)
 
 
-def project_kernel(chunks, count, place_ref, *refs):
+def project_kernel(chunks, count, half_ref, *refs):
     row_refs, attn_refs, out_side = refs[:count], refs[count : 2 * count], refs[2 * count]
     weights = refs[2 * count + 1 : 2 * count + 1 + 2 * len(chunks)]
     out_ref, total = refs[-2:]
@@ -372,7 +380,7 @@
                 ].astype(jnp.bfloat16)
 
 
-def project(place, shards, row_parts, attn, flips, out_side, weights, chunks, earlier=()):
+def project(half_id, shards, row_parts, attn_parts, out_side, weights, chunks, earlier=()):
     count = len(row_parts)
     rows, width = row_parts[0].shape
     steps = 6
@@ -387,8 +395,8 @@
         ]
     row_spec = pl.BlockSpec((rows, depth), lambda i, h: (0, lax.rem(i + h[0] * (last + 1), steps)))
 
-    def attn_spec(flip):
-        return pl.BlockSpec((rows, attn.shape[1]), lambda i, h: (h[1] ^ flip, 0))
+    def attn_spec(block):
+        return pl.BlockSpec((rows, out_side.shape[1]), lambda i, h: (block, 0))
 
     shape = (shards, columns, count * rows // shards)
     return pl.pallas_call(
@@ -397,7 +405,7 @@
             num_scalar_prefetch=1,
             grid=(steps,),
             in_specs=[row_spec] * count
-            + [attn_spec(flip) for flip in flips]
+            + [attn_spec(block) for _, block in attn_parts]
             + [pl.BlockSpec(out_side.shape, lambda i, h: (0, 0))]
             + weight_specs
             + [ANYWHERE] * len(earlier),
@@ -407,7 +415,8 @@
         out_shape=jax.ShapeDtypeStruct(shape, jnp.bfloat16),
         compiler_params=pltpu.CompilerParams(vmem_limit_bytes=56 << 20),
         cost_estimate=cost(10),
-    )(place, *row_parts, *[attn] * count, out_side, *weights, *earlier)
+        name="project",
+    )(half_id, *row_parts, *[part for part, _ in attn_parts], out_side, *weights, *earlier)
 
 
 def turned(head, cosine, signed_sine):
@@ -415,40 +424,21 @@
     return (head * cosine + pltpu.roll(head, HD // 2, 1) * signed_sine).astype(jnp.bfloat16)
 
 
-def attend_kernel(
-    place_ref,
-    query_ref,
-    cosine_ref,
-    sine_ref,
-    key0,
-    value0,
-    key1,
-    value1,
-    cached_key1,
-    cached_value1,
-    key2,
-    value2,
-    cached_key2,
-    cached_value2,
-    out_ref,
-):
+def attend_kernel(place_ref, query_ref, cosine_ref, sine_ref, *refs):
+    blocks, out_ref = refs[:16], refs[-1]
     rows = query_ref.shape[0]
-
-    def chosen(block, halo, cached):
-        return jnp.where(place_ref[0] >= block, halo[...], cached[...])
-
-    key1, value1 = chosen(1, key1, cached_key1), chosen(1, value1, cached_value1)
-    key2, value2 = chosen(2, key2, cached_key2), chosen(2, value2, cached_value2)
-    keys = [
-        turned(
-            key,
-            cosine_ref[block * rows : (block + 1) * rows, :],
-            sine_ref[block * rows : (block + 1) * rows, :],
-        )
-        for block, key in enumerate((key0[...], key1, key2))
-    ]
     half = rows // 2
     heads = query_ref.shape[1] // HD
+    key0, value0 = blocks[:2]
+    keys = [turned(key0[...], cosine_ref[...], sine_ref[...])]
+    values = [value0[...]]
+    for block in (1, 2):
+        key, value, cosine, sine, cached_key, cached_value = blocks[6 * block - 4 : 6 * block + 2]
+        inside = place_ref[pl.program_id(0)] >= block
+        keys.append(
+            jnp.where(inside, turned(key[...], cosine[...], sine[...]), cached_key[...])
+        )
+        values.append(jnp.where(inside, value[...], cached_value[...]))
     for part in range(2):
         low = part * half
         here = slice(low, low + half)
@@ -490,69 +480,60 @@
         )
         mass = jnp.zeros_like(top)
         total = jnp.zeros((heads * half, HD), jnp.float32)
-        for scores, values in (
-            (score0, value0[own, :]),
-            (score1, value1),
-            (score2, value2[old, :]),
+        for scores, block in (
+            (score0, values[0][own, :]),
+            (score1, values[1]),
+            (score2, values[2][old, :]),
         ):
             weight = jnp.exp(scores - top)
             mass += jnp.sum(weight, axis=1, keepdims=True)
             total += jnp.dot(
-                weight.astype(jnp.bfloat16), values, preferred_element_type=jnp.float32
+                weight.astype(jnp.bfloat16), block, preferred_element_type=jnp.float32
             )
         total = (total / mass).astype(jnp.bfloat16)
         for head in range(heads):
             out_ref[here, head * HD : (head + 1) * HD] = total[head * half : (head + 1) * half]
 
 
-def attend(place, queries, cosine, signed_sine, pairs, all_pairs, cached1, cached2):
-    rows, width = queries.shape
-    kv_heads = pairs.shape[1] // (2 * HD)
+def attend(places, kv_heads, cosine, signed_sine, all_shared, ordered, earlier, weight):
+    rows = ordered.shape[0] // 2
+    first = 2 * kv_heads * HD
+    width = all_shared.shape[1] - first
     wide = width // kv_heads
-
-    def specs(back):
-        def row(p):
-            return 0 if back is None else jnp.maximum(p[0] - back, 0)
-
+    parts = places.shape[0]
+
+    def pair_specs(row):
         return [
-            pl.BlockSpec((rows, HD), lambda i, p: (row(p), i)),
-            pl.BlockSpec((rows, HD), lambda i, p: (row(p), kv_heads + i)),
+            pl.BlockSpec((rows, HD), lambda t, i, p: (row(p[t]), i)),
+            pl.BlockSpec((rows, HD), lambda t, i, p: (row(p[t]), kv_heads + i)),
         ]
 
-    table_spec = pl.BlockSpec(cosine.shape, lambda i, p: (0, 0))
-    query_spec = pl.BlockSpec((rows, wide), lambda i, p: (0, i))
+    def table_specs(row):
+        return [pl.BlockSpec((rows, HD), lambda t, i, p: (row(p[t]), 0))] * 2
+
+    def back(block):
+        return lambda place: jnp.maximum(place - block, 0)
+
+    specs = [pl.BlockSpec((rows, wide), lambda t, i, p: (p[t], first // wide + i))]
+    specs += table_specs(back(0)) + pair_specs(back(0))
+    operands = [all_shared, cosine, signed_sine, all_shared, all_shared]
+    for block in (1, 2):
+        specs += pair_specs(back(block)) + table_specs(back(block))
+        specs += pair_specs(lambda place, block=block: jnp.minimum(place + 2 - block, 1))
+        operands += [all_shared, all_shared, cosine, signed_sine, ordered, ordered]
     return pl.pallas_call(
         attend_kernel,
         grid_spec=pltpu.PrefetchScalarGridSpec(
             num_scalar_prefetch=1,
-            grid=(kv_heads,),
-            in_specs=[query_spec, table_spec, table_spec]
-            + specs(None)
-            + specs(1)
-            + specs(None)
-            + specs(2)
-            + specs(None),
-            out_specs=query_spec,
+            grid=(parts, kv_heads),
+            in_specs=specs + [ANYWHERE] * len(earlier),
+            out_specs=pl.BlockSpec((rows, wide), lambda t, i, p: (t, i)),
         ),
-        out_shape=jax.ShapeDtypeStruct(queries.shape, jnp.bfloat16),
+        out_shape=jax.ShapeDtypeStruct((parts * rows, width), jnp.bfloat16),
         compiler_params=pltpu.CompilerParams(vmem_limit_bytes=56 << 20),
-        cost_estimate=cost(13),
-    )(
-        place,
-        queries,
-        cosine,
-        signed_sine,
-        pairs,
-        pairs,
-        all_pairs,
-        all_pairs,
-        cached1,
-        cached1,
-        all_pairs,
-        all_pairs,
-        cached2,
-        cached2,
-    )
+        cost_estimate=cost(weight),
+        name="attend",
+    )(places, *operands, *earlier)
 
 
 def flipped(value, axis, bit):
@@ -568,72 +549,83 @@
     side = seq_index >> 1
     tok_rows = queries.shape[0]
 
-    pairs = key_value.reshape(tok_rows, -1)
-    all_pairs = lax.all_gather(pairs, "seq", axis=0, tiled=True)
+    shared = jnp.concatenate([key_value.reshape(tok_rows, -1), queries], axis=1)
+    all_shared = lax.all_gather(shared, "seq", axis=0, tiled=True)
+
+    def both_cores(value):
+        return [value, flipped(value, "seq", 1)]
 
     codes = down_codes.T
     out_own = out_weight.T
-    piece_a = dequant(half_id, codes, down_scales, 0)
-    piece_c = dequant(half_id, codes, down_scales, 1, (piece_a, pairs))
-    rotated = mix_hidden(hidden, piece_c)
-    piece_b = dequant(half_id, codes, down_scales, 2, (rotated,))
-    piece_d = dequant(half_id, codes, down_scales, 3, (piece_b,))
-
-    def both_cores(value):
-        return [value, flipped(value, "seq", 1)]
-
-    own_rows = both_cores(rotated)
-    piece_a = level_step(piece_a, 2)
+    (piece_a, piece_c), (piece_b, piece_d) = EARLY, LATE
+    piece_a = dequant(half_id, codes, down_scales, *piece_a, (shared,))
+    piece_c = dequant(half_id, codes, down_scales, *piece_c, (piece_a,))
+    piece_b = dequant(half_id, codes, down_scales, *piece_b, (piece_c,))
+    near_hidden = flipped(hidden, "seq", 1)
+    rotated = mix_hidden(hidden, piece_b)
+
+    first_pos = gate(span_start, piece_b)[0]
+    span = tok_rows * lax.axis_size("seq")
+    positions = first_pos + jnp.arange(span, dtype=jnp.int32)
+    inv_freq = ROPE_BASE ** (-(2.0 * jnp.arange(HD // 2, dtype=jnp.float32)) / HD)
+    angles = positions.astype(jnp.float32)[:, None] * inv_freq[None, :]
+    cosine, sine = jnp.cos(angles), jnp.sin(angles)
+    cosine = jnp.concatenate([cosine, cosine], axis=1)
+    signed_sine = jnp.concatenate([-sine, sine], axis=1)
+    cache = window_cache.reshape(WINDOW, -1)
+    doubled = jnp.concatenate([cache, cache], axis=0)
+    ordered = lax.dynamic_slice_in_dim(doubled, first_pos % WINDOW, WINDOW, 0)
+
+    kv_heads = key_value.shape[2] // HD
+
+    piece_a = level_step(piece_a, 2, (rotated, ordered, cosine, signed_sine))
     piece_c = level_step(piece_c, 1, (piece_a,))
-    first_pos = gate(span_start, piece_c)[0]
-
-    block_first = first_pos + (seq_index - jnp.arange(3, dtype=jnp.int32)) * tok_rows
-    positions = block_first[:, None] + jnp.arange(tok_rows, dtype=jnp.int32)[None, :]
-    inv_freq = ROPE_BASE ** (-(2.0 * jnp.arange(HD // 2, dtype=jnp.float32)) / HD)
-    angles = positions.astype(jnp.float32)[:, :, None] * inv_freq
-    turn = (seq_index >= jnp.arange(3))[:, None, None]
-    cosine, sine = jnp.where(turn, jnp.cos(angles), 1.0), jnp.where(turn, jnp.sin(angles), 0.0)
-    cosine = jnp.concatenate([cosine, cosine], axis=2).reshape(-1, HD)
-    signed_sine = jnp.concatenate([-sine, sine], axis=2).reshape(-1, HD)
-    cache = gate(window_cache, piece_c).reshape(WINDOW, -1)
-    doubled = jnp.concatenate([cache, cache], axis=0)
-    first1 = (first_pos + tok_rows) % WINDOW
-    first2 = (first_pos + jnp.minimum(seq_index, 1) * tok_rows) % WINDOW
-    cached1 = lax.dynamic_slice_in_dim(doubled, first1, tok_rows, 0)
-    cached2 = lax.dynamic_slice_in_dim(doubled, first2, tok_rows, 0)
-    attended = attend(
-        seq_index.reshape(1), queries, cosine, signed_sine, pairs, all_pairs, cached1, cached2
-    )
-
-    piece_b = level_step(piece_b, 2, (piece_c, attended))
-    piece_d = level_step(piece_d, 1, (piece_b, own_rows[1]))
-    piece_a = level_step(piece_a, 1, (piece_d,))
+    own_rows = [rotated, mix_hidden(near_hidden, piece_c)]
+    def attended_by(flip, earlier, weight):
+        places = (seq_index ^ flip).reshape(1)
+        return attend(
+            places, kv_heads, cosine, signed_sine, all_shared, ordered, earlier, weight
+        ), 0
+
+    late_d = dequant(half_id, codes, down_scales, *LATE[1], (own_rows[1],))
+    attended = [None] * 4
+    attended[0] = attended_by(0, (late_d,), 13)
+    piece_b = level_step(piece_b, 2, (piece_c, attended[0][0]))
+    attended[2] = attended_by(2, (piece_b,), 13)
+    piece_a = level_step(piece_a, 1, (attended[2][0],))
     across_a = flipped(piece_a, "group", 1)
     piece_c = level_step(piece_c, 2, (piece_a,))
     across_c = flipped(piece_c, "group", 1)
-    piece_b = level_step(piece_b, 1, (piece_c, across_a))
+    piece_d = level_step(late_d, 1, (piece_c,))
+    attended[1] = attended_by(1, (piece_d,), 0)
+    attended[3] = attended_by(3, (attended[1][0],), 0)
+    piece_b = level_step(piece_b, 1, (attended[3][0], across_a))
     across_b = flipped(piece_b, "group", 1)
-    piece_d = level_step(piece_d, 2, (piece_b, across_c))
+    own_attn, far_attn = attended[:2], attended[2:]
+    shards = lax.axis_size("tp")
+
+    def reduced(rows, attn, weights, chunks, earlier=(), after=()):
+        partial = project(half_id, shards, rows, attn, out_own, weights, chunks, earlier)
+        if after:
+            partial = gate(partial, *after)
+        return lax.psum_scatter(partial, "tp", scatter_dimension=0, tiled=True)[0], partial
+
+    early = [piece_a, across_a, piece_c, across_c]
+    own_early, own_done = reduced(own_rows, own_attn, early, EARLY, (piece_b,))
+    piece_d = level_step(piece_d, 2, (piece_b, own_done))
     across_d = flipped(piece_d, "group", 1)
-
-    shards = lax.axis_size("tp")
-    place = jnp.stack([half_id[0], seq_index])
-    all_attended = lax.all_gather(attended, "seq", axis=0, tiled=True)
-
-    def reduced(rows, flips, weights, chunks, earlier=()):
-        partial = project(
-            place, shards, rows, all_attended, flips, out_own, weights, chunks, earlier
-        )
-        return lax.psum_scatter(partial, "tp", scatter_dimension=0, tiled=True)[0], partial
-
-    early, late = [piece_a, across_a, piece_c, across_c], [piece_b, across_b, piece_d, across_d]
-    own_early, own_done = reduced(own_rows, (0, 1), early, CHUNKS[:2], (piece_d,))
-    far_rows = both_cores(gate(flipped(rotated, "seq", 2), own_done, across_b))
-    far_early, far_done = reduced(far_rows, (2, 3), early, CHUNKS[:2], (across_d,))
-    all_late, _ = reduced(own_rows + far_rows, (0, 1, 2, 3), late, CHUNKS[2:], (far_done,))
+    late = [piece_b, across_b, piece_d, across_d]
+    far_rows = both_cores(gate(flipped(rotated, "seq", 2), piece_d,across_b))
+    far_early, far_done = reduced(far_rows, far_attn, early, EARLY, (across_d,))
+    all_late, _ = reduced(
+        own_rows + far_rows, own_attn + far_attn, late, LATE, (far_done, own_early), (far_early,)
+    )
     kept = tok_rows // shards
-    sums = jnp.concatenate([own_early, far_early], axis=1)
-    sums = jnp.concatenate([sums, all_late], axis=0)
+    all_early = jnp.concatenate([own_early, far_early], axis=1)
+    sums = jnp.concatenate(
+        [all_early[:WIDE], all_late[: HALF - WIDE], all_early[WIDE:], all_late[HALF - WIDE :]],
+        axis=0,
+    )
     strips = [sums[:, i * kept : (i + 1) * kept] for i in range(4)]
     strips = strips[:1] + [flipped(strips[i], "seq", i) for i in (1, 2, 3)]
     strips = [jnp.where(core == 0, strips[i], strips[i ^ 1]) for i in range(4)]

time: 366 us -> 319 us (0.87)
  waiting for transfers between devices: 190 us -> 83.7 us
  Pallas kernels: 116 us -> 165 us
  starting transfers between devices: 18.9 us -> 22.8 us
  other arithmetic: 7.1 us -> 11 us
    ppermute x18, waiting for transfers between devices: 155 us -> 42.5 us  [flipped(): lax.ppermute(value, axis, [(i, i ^ bit) for i in range(lax.axis_size(axis...]
    pallas_call x1 -> x4, Pallas kernels: 14.2 us -> 58.6 us  [attend(): pl.pallas_call(attend_kernel, grid_spec=pltpu.PrefetchScalarGridSpec(num_...]
    all_gather x2 -> x1, waiting for transfers between devices: 0.01 us -> 6.95 us  [planned(): all_shared = lax.all_gather(shared, 'seq', axis=0, tiled=True)]
    pallas_call x1 -> x2, Pallas kernels: 16.5 us -> 23.1 us  [mix_hidden(): pl.pallas_call(mix_kernel, grid=(rows // step,), in_specs=[pl.BlockSpec((...]
    ppermute x18, starting transfers between devices: 18.8 us -> 22.7 us  [flipped(): lax.ppermute(value, axis, [(i, i ^ bit) for i in range(lax.axis_size(axis...]
    concatenate x2 -> x4, other arithmetic: 2.79 us -> 6.48 us  [the longest x1 4.49 us: planned(): doubled = jnp.concatenate([cache, cache], axis=0)]
    unnamed x28 -> x27, local copies, waits for them, and re-layouts: 14.2 us -> 13 us
  transfers between devices with their start and end apart: 23 -> 22, of which waited for: 13 -> 10; matrix products, arithmetic and copies ran while one was open for 3% -> 4% of each run, Pallas kernels for 32% -> 52%
where the time goes in v1:
time: 319 us; the launch traced here: 314 us
  Pallas kernels  165 us (52%)
  waiting for transfers between devices  83.7 us (26%)
  starting transfers between devices  22.8 us (7%)
  between operations  16.6 us (5%)
  local copies, waits for them, and re-layouts  15.3 us (5%)
  other arithmetic  11 us (3%)
    pallas_call x4, Pallas kernels, attend(): pl.pallas_call(attend_kernel, grid_spec=pltpu.PrefetchScalarGridSpec(num_...  58.6 us
    pallas_call x3, Pallas kernels, project(): pl.pallas_call(lambda *refs: project_kernel(chunks, count, *refs), grid_s...  44.1 us
    ppermute x18, waiting for transfers between devices, flipped(): lax.ppermute(value, axis, [(i, i ^ bit) for i in range(lax.axis_size(axis...  42.5 us
    reduce_scatter x3, waiting for transfers between devices, reduced(): lax.psum_scatter(partial, 'tp', scatter_dimension=0, tiled=True)[0]  34.2 us
    pallas_call x2, Pallas kernels, mix_hidden(): pl.pallas_call(mix_kernel, grid=(rows // step,), in_specs=[pl.BlockSpec((...  23.1 us
    ppermute x18, starting transfers between devices, flipped(): lax.ppermute(value, axis, [(i, i ^ bit) for i in range(lax.axis_size(axis...  22.7 us
    pallas_call x8, Pallas kernels, level_step(): pl.pallas_call(level_kernel, grid_spec=pltpu.PrefetchScalarGridSpec(num_s...  22 us
    pallas_call x4, Pallas kernels, dequant(): pl.pallas_call(lambda *refs: dequant_kernel(first, *refs), grid_spec=pltp...  16.3 us
  transfers between devices with their start and end apart: 22, of which 10 were waited for; matrix products, arithmetic and copies ran while one was open for 4% of the time, Pallas kernels for 52%

profile of v1, /device:TPU:0, one launch (start us, length us, event | category | flops | bytes accessed | tf_op | source)
XLA Modules:
  0.0 314.0 jit_solution(4548295399123499701)
XLA Ops:
  6.5 1.6 copy.19
  8.3 1.3 copy-done
  10.2 4.2 %decode.4.refs_4_.own_ref = bf16[192,2688]{1,0:T(8,128)(2,1)} custom-call(s32[1]{0:T(128)} %bitcast.refs_0_, s32[672,5376]{1,0:T(8,128)} %bitcast.22, s32[42,672]{1,0:T(8,128)} %refs_2_.7, bf16[42,5376]{1,0:T(8,128)(2,1)} %constant.48.clone.refs_3_, bf16[512,2048]{1,0:T(8,128)(2,1)} %copy-done), custom_call_target="tpu_custom_call" | custom-call | flops 3450000128 | bytes 1 | tf_op jit(solution)/shard_map/decode/pallas_call | solution.py:282
  14.4 3.6 %collective-permute-start.2 = (bf16[192,2688]{1,0:T(8,128)(2,1)}, bf16[192,2688]{1,0:T(8,128)(2,1)S(1)}, u32[]{:S(2)}, u32[]{:S(2)}) collective-permute-start(bf16[192,2688]{1,0:T(8,128)(2,1)} %decode.4.refs_4_.own_ref), channel_id=1, source_target_pairs={{0,2},{1,3},{2,0},{3,1},{4,6},{5,7},{6,4},{7,5},{8,10},{9,11},{10,... | collective-permute-start | bytes 3096584 | tf_op jit(solution)/shard_map/ppermute | solution.py:540
  18.1 4.6 %decode.5.refs_4_.own_ref = bf16[192,2688]{1,0:T(8,128)(2,1)} custom-call(s32[1]{0:T(128)} %bitcast.refs_0_, s32[672,5376]{1,0:T(8,128)} %bitcast.23, s32[42,672]{1,0:T(8,128)} %refs_2_.7, bf16[42,5376]{1,0:T(8,128)(2,1)} %constant.48.clone.refs_3_, bf16[192,2688]{1,0:T(8,128)(2,1)} %decode.4.refs_4_.own_ref), custom_call_target="tpu_custom_call" | custom-call | flops 3450000128 | bytes 1 | tf_op jit(solution)/shard_map/decode/pallas_call | solution.py:282
  22.6 1.6 collective-permute-start.1
  24.2 3.8 %decode.6.refs_0_.refs_1_.own_ref = bf16[144,2688]{1,0:T(8,128)(2,1)} custom-call(s32[1]{0:T(128)} %bitcast.refs_0_, s32[672,5376]{1,0:T(8,128)} %bitcast.24, s32[42,672]{1,0:T(8,128)} %refs_2_.7, bf16[42,5376]{1,0:T(8,128)(2,1)} %constant.48.clone.refs_3_, bf16[192,2688]{1,0:T(8,128)(2,1)} %decode.5.refs_4_.own_ref), custom_call_target="tpu_custom_call" | custom-call | flops 3450000128 | bytes 1 | tf_op jit(solution)/shard_map/decode/pallas_call | solution.py:282
  28.9 11.6 %mix.2.refs_0_.refs_1_ = bf16[512,5376]{1,0:T(8,128)(2,1)} custom-call(bf16[512,5376]{1,0:T(8,128)(2,1)} %hidden_ref.1, bf16[864,768]{1,0:T(8,128)(2,1)} %constant.49.clone.table_ref, bf16[144,2688]{1,0:T(8,128)(2,1)} %decode.6.refs_0_.refs_1_.own_ref), custom_call_target="tpu_custom_call" | custom-call | flops 18400000000 | bytes 1 | tf_op jit(solution)/shard_map/mix/pallas_call | solution.py:246
  40.5 1.7 collective-permute-start.10
  44.8 2.1 copy.20
  47.7 4.5 %fusion.refs_1_.refs_6_.refs_7_.refs_12_.refs_13_ = bf16[1024,1024]{1,0:T(8,128)(2,1)} fusion(s32[]{:T(128)S(6)} %select_n.66, bf16[1024,1024]{1,0:T(8,128)(2,1)S(1)} %bitcast.26), kind=kLoop, calls=%fused_computation.2 | loop fusion | flops 4194304 | bytes 4194308 | tf_op jit(solution)/shard_map/concatenate | solution.py:576
  52.2 3.7 %fusion.7 = (f32[2048,64]{1,0:T(8,128)S(1)}, f32[2048,64]{1,0:T(8,128)S(1)}, f32[2048,64]{1,0:T(8,128)S(1)}) fusion(f32[64]{0:T(128)S(1)} %multiply_power_fusion, f32[2048]{0:T(1024)S(1)} %add_convert_fusion), kind=kLoop, calls=%fused_computation.18 | loop fusion | flops 262144 | bytes 1581312 | tf_op jit(solution)/shard_map/neg | solution.py:574
  55.9 1.9 pad_maximum_fusion
  57.8 6.3 %collective-permute-done.2.partner_ref = bf16[192,2688]{1,0:T(8,128)(2,1)S(1)} collective-permute-done((bf16[192,2688]{1,0:T(8,128)(2,1)}, bf16[192,2688]{1,0:T(8,128)(2,1)S(1)}, u32[]{:S(2)}, u32[]{:S(2)}) %collective-permute-start.2) | collective-permute-done | bytes 1032224 | tf_op jit(solution)/shard_map/ppermute | solution.py:540
  65.2 2.4 level.8.refs_0_.own_ref
  68.4 1.6 collective-permute-done.1.partner_ref
  70.0 2.4 level.9.refs_0_.own_ref
  72.4 1.9 collective-permute-start.4
  74.2 11.5 %mix.3.refs_4_.refs_2_ = bf16[512,5376]{1,0:T(8,128)(2,1)} custom-call(bf16[512,5376]{1,0:T(8,128)(2,1)} %collective-permute-done.hidden_ref, bf16[864,768]{1,0:T(8,128)(2,1)} %constant.49.clone.table_ref, bf16[192,2688]{1,0:T(8,128)(2,1)} %level.9.refs_0_.own_ref), custom_call_target="tpu_custom_call" | custom-call | flops 18400000000 | bytes 1 | tf_op jit(solution)/shard_map/mix/pallas_call | solution.py:246
  85.8 3.7 %decode.7.refs_14_.own_ref = bf16[144,2688]{1,0:T(8,128)(2,1)} custom-call(s32[1]{0:T(128)} %bitcast.refs_0_, s32[672,5376]{1,0:T(8,128)} %bitcast.25, s32[42,672]{1,0:T(8,128)} %refs_2_.7, bf16[42,5376]{1,0:T(8,128)(2,1)} %constant.48.clone.refs_3_, bf16[512,5376]{1,0:T(8,128)(2,1)} %mix.3.refs_4_.refs_2_), custom_call_target="tpu_custom_call" | custom-call | flops 3450000128 | bytes 1 | tf_op jit(solution)/shard_map/decode/pallas_call | solution.py:282
  89.6 6.9 %all-gather.2.cloned.1.call-done.query_ref.refs_0_.refs_1_.refs_2_.refs_3_.refs_8_.refs_9_ = bf16[2048,2048]{1,0:T(8,128)(2,1)} async-done(((bf16[512,2048]{1,0:T(8,128)(2,1)}), bf16[2048,2048]{1,0:T(8,128)(2,1)}) %all-gather.2.cloned.1.call-update) | async-done | bytes 8388624 | tf_op jit(solution)/shard_map/all_gather | solution.py:553
  96.5 14.8 %attend.4.refs_1_.refs_3_.refs_5_ = bf16[512,1024]{1,0:T(8,128)(2,1)} custom-call(s32[1]{0:T(128)} %bitcast.5.place_ref, bf16[2048,2048]{1,0:T(8,128)(2,1)} %all-gather.2.cloned.1.call-done.query_ref.refs_0_.refs_1_.refs_2_.refs_3_.refs_8_.refs_9_, f32[2048,128]{1,0:T(8,128)} %get-tuple-element.17.refs_2_.cosine_ref.refs_4_.refs_10_, ...), custom_call_target="tpu_custom_call" | custom-call | flops 14949999616 | bytes 1 | tf_op jit(solution)/shard_map/attend/pallas_call | solution.py:524
  111.3 3.2 %level.10.refs_14_.own_ref = bf16[144,2688]{1,0:T(8,128)(2,1)} custom-call(s32[1]{0:T(128)} %bitcast.3.sign_ref, bf16[144,2688]{1,0:T(8,128)(2,1)} %decode.6.refs_0_.refs_1_.own_ref, bf16[144,2688]{1,0:T(8,128)(2,1)} %collective-permute-done.6.partner_ref, bf16[192,2688]{1,0:T(8,128)(2,1)} %level.9.refs_0_.own_ref, ...), custom_call_target="tpu_custom_call" | custom-call | flops 3450000128 | bytes 1 | tf_op jit(solution)/shard_map/level/pallas_call | solution.py:314
  114.5 2.4 collective-permute-start.9
  116.8 14.4 %attend.5.refs_0_.refs_3_.refs_7_ = bf16[512,1024]{1,0:T(8,128)(2,1)} custom-call(s32[1]{0:T(128)} %bitcast.7.place_ref, bf16[2048,2048]{1,0:T(8,128)(2,1)} %all-gather.2.cloned.1.call-done.query_ref.refs_0_.refs_1_.refs_2_.refs_3_.refs_8_.refs_9_, f32[2048,128]{1,0:T(8,128)} %get-tuple-element.17.refs_2_.cosine_ref.refs_4_.refs_10_, ...), custom_call_target="tpu_custom_call" | custom-call | flops 14949999616 | bytes 1 | tf_op jit(solution)/shard_map/attend/pallas_call | solution.py:524
  132.2 2.4 level.11.refs_0_.refs_6_
  134.6 1.4 collective-permute-start.7
  136.1 5.5 %collective-permute-done.4.partner_ref = bf16[192,2688]{1,0:T(8,128)(2,1)} collective-permute-done((bf16[192,2688]{1,0:T(8,128)(2,1)}, bf16[192,2688]{1,0:T(8,128)(2,1)}, u32[]{:S(2)}, u32[]{:S(2)}) %collective-permute-start.4) | collective-permute-done | bytes 1032224 | tf_op jit(solution)/shard_map/ppermute | solution.py:540
  141.6 2.4 level.12.refs_0_.refs_8_
  143.9 1.5 collective-permute-start.8
  145.5 2.2 collective-permute-done.3.partner_ref
  147.7 3.1 level.13.refs_14_.own_ref
  150.8 2.9 collective-permute-start.11
  153.7 15.0 %attend.6.refs_14_.refs_4_.refs_6_ = bf16[512,1024]{1,0:T(8,128)(2,1)} custom-call(s32[1]{0:T(128)} %bitcast.6.place_ref, bf16[2048,2048]{1,0:T(8,128)(2,1)} %all-gather.2.cloned.1.call-done.query_ref.refs_0_.refs_1_.refs_2_.refs_3_.refs_8_.refs_9_, f32[2048,128]{1,0:T(8,128)} %get-tuple-element.17.refs_2_.cosine_ref.refs_4_.refs_10_, ...), custom_call_target="tpu_custom_call" | custom-call | flops 1 | bytes 1 | tf_op jit(solution)/shard_map/attend/pallas_call | solution.py:524
  168.6 14.4 %attend.7.refs_0_.refs_4_.refs_8_ = bf16[512,1024]{1,0:T(8,128)(2,1)} custom-call(s32[1]{0:T(128)} %bitcast.9.place_ref, bf16[2048,2048]{1,0:T(8,128)(2,1)} %all-gather.2.cloned.1.call-done.query_ref.refs_0_.refs_1_.refs_2_.refs_3_.refs_8_.refs_9_, f32[2048,128]{1,0:T(8,128)} %get-tuple-element.17.refs_2_.cosine_ref.refs_4_.refs_10_, ...), custom_call_target="tpu_custom_call" | custom-call | flops 1 | bytes 1 | tf_op jit(solution)/shard_map/attend/pallas_call | solution.py:524
  184.9 3.1 level.14.refs_10_.refs_0_
  188.1 1.5 collective-permute-start.12
  189.5 13.0 %project.3.refs_1_ = bf16[4,384,256]{2,1,0:T(8,128)(2,1)} custom-call(s32[1]{0:T(128)} %bitcast.refs_0_, bf16[512,5376]{1,0:T(8,128)(2,1)} %mix.2.refs_0_.refs_1_, bf16[512,5376]{1,0:T(8,128)(2,1)} %mix.3.refs_4_.refs_2_, bf16[512,1024]{1,0:T(8,128)(2,1)} %attend.4.refs_1_.refs_3_.refs_5_, bf16[512,1024]{1,0:T(8,128)(2,1)} %attend.6.refs_14_.refs_4_.refs_6_, ...), custom_call_target="tpu_custom_call" | custom-call | flops 11500000256 | bytes 1 | tf_op jit(solution)/shard_map/project/pallas_call | solution.py:402
  203.5 3.1 level.15.refs_1_.refs_12_
  208.6 18.6 %collective-permute-done.14.refs_10_.refs_13_ = bf16[144,2688]{1,0:T(8,128)(2,1)S(1)} collective-permute-done((bf16[144,2688]{1,0:T(8,128)(2,1)S(1)}, bf16[144,2688]{1,0:T(8,128)(2,1)S(1)}, u32[]{:S(2)}, u32[]{:S(2)}) %collective-permute-start.14) | collective-permute-done | bytes 774176 | tf_op jit(solution)/shard_map/ppermute | solution.py:540
  228.1 13.0 %project.4.refs_14_ = bf16[4,384,256]{2,1,0:T(8,128)(2,1)} custom-call(s32[1]{0:T(128)} %bitcast.refs_0_, bf16[512,5376]{1,0:T(8,128)(2,1)} %gate.4.refs_1_.refs_3_, bf16[512,5376]{1,0:T(8,128)(2,1)} %collective-permute-done.13.refs_2_.refs_4_, bf16[512,1024]{1,0:T(8,128)(2,1)} %attend.5.refs_0_.refs_3_.refs_7_, ...), custom_call_target="tpu_custom_call" | custom-call | flops 11500000256 | bytes 1 | tf_op jit(solution)/shard_map/project/pallas_call | solution.py:402
  241.2 18.2 %project.5.refs_0_ = bf16[4,288,512]{2,1,0:T(8,128)(2,1)} custom-call(s32[1]{0:T(128)} %bitcast.refs_0_, bf16[512,5376]{1,0:T(8,128)(2,1)} %mix.2.refs_0_.refs_1_, bf16[512,5376]{1,0:T(8,128)(2,1)} %mix.3.refs_4_.refs_2_, bf16[512,5376]{1,0:T(8,128)(2,1)} %gate.4.refs_1_.refs_3_, bf16[512,5376]{1,0:T(8,128)(2,1)} %collective-permute-done.13.refs_2_.refs_4_, ...), custom_call_target="tpu_custom_call" | custom-call | flops 11500000256 | bytes 1 | tf_op jit(solution)/shard_map/project/pallas_call | solution.py:402
  259.3 4.4 %reduce-scatter.6.cloned.1.call-done = bf16[1,384,256]{2,1,0:T(8,128)(2,1)} async-done(((bf16[4,384,256]{2,1,0:T(8,128)(2,1)}), bf16[1,384,256]{2,1,0:T(8,128)(2,1)}) %reduce-scatter.6.cloned.1.call-update) | async-done | bytes 196624 | tf_op jit(solution)/shard_map/reduce_scatter | solution.py:611
  264.7 29.7 %reduce-scatter.8.cloned.1.call-done = bf16[1,288,512]{2,1,0:T(8,128)(2,1)} async-done(((bf16[4,288,512]{2,1,0:T(8,128)(2,1)}), bf16[1,288,512]{2,1,0:T(8,128)(2,1)}) %reduce-scatter.8.cloned.1.call-update) | async-done | bytes 294928 | tf_op jit(solution)/shard_map/reduce_scatter | solution.py:611
  295.7 1.5 collective-permute-start.16
  297.6 5.4 %collective-permute-done.16 = bf16[672,128]{1,0:T(8,128)(2,1)S(1)} collective-permute-done((bf16[672,128]{1,0:T(8,128)(2,1)S(1)}, bf16[672,128]{1,0:T(8,128)(2,1)S(1)}, u32[]{:S(2)}, u32[]{:S(2)}) %collective-permute-start.16) | collective-permute-done | bytes 172064 | tf_op jit(solution)/shard_map/ppermute | solution.py:540
  302.9 2.8 collective-permute-done.17
  305.8 1.1 copy.18
  (64 shorter events, 13.5 us)
Async XLA Ops:
  6.5 90.0 %all-gather.2.cloned.1.call-start = ((), (), s32[]{:S(2)}) async-start(), calls=%async_computation.3 | async-start | bytes 10485760 | tf_op jit(solution)/shard_map/all_gather | solution.py:553
  6.5 1.7 copy-start.2
  8.3 1.3 copy-start
  9.6 231.5 %reduce-scatter.4.cloned.1.call-start = ((), (), s32[]{:S(2)}) async-start(), calls=%async_computation.4 | async-start | bytes 983040 | tf_op jit(solution)/shard_map/reduce_scatter | solution.py:611
  9.7 64.5 %collective-permute-start = (bf16[512,5376]{1,0:T(8,128)(2,1)}, bf16[512,5376]{1,0:T(8,128)(2,1)}, u32[]{:S(2)}, u32[]{:S(2)}) collective-permute-start(bf16[512,5376]{1,0:T(8,128)(2,1)} %hidden_ref.1), channel_id=1, source_target_pairs={{0,4},{4,0},{8,12},{12,8},{1,5},{5,1},{9,13},{13,9},{2,6},{6,2},{1... | collective-permute-start | bytes 16515080 | tf_op jit(solution)/shard_map/ppermute | solution.py:540
  14.4 49.7 %collective-permute-start.2 = (bf16[192,2688]{1,0:T(8,128)(2,1)}, bf16[192,2688]{1,0:T(8,128)(2,1)S(1)}, u32[]{:S(2)}, u32[]{:S(2)}) collective-permute-start(bf16[192,2688]{1,0:T(8,128)(2,1)} %decode.4.refs_4_.own_ref), channel_id=1, source_target_pairs={{0,2},{1,3},{2,0},{3,1},{4,6},{5,7},{6,4},{7,5},{8,10},{9,11},{10,... | collective-permute-start | bytes 3096584 | tf_op jit(solution)/shard_map/ppermute | solution.py:540
  22.6 47.3 %collective-permute-start.1 = (bf16[192,2688]{1,0:T(8,128)(2,1)}, bf16[192,2688]{1,0:T(8,128)(2,1)}, u32[]{:S(2)}, u32[]{:S(2)}) collective-permute-start(bf16[192,2688]{1,0:T(8,128)(2,1)} %decode.5.refs_4_.own_ref), channel_id=1, source_target_pairs={{0,1},{1,0},{2,3},{3,2},{4,5},{5,4},{6,7},{7,6},{8,9},{9,8},{10,11... | collective-permute-start | bytes 3096584 | tf_op jit(solution)/shard_map/ppermute | solution.py:540
  28.0 83.3 %collective-permute-start.6 = (bf16[144,2688]{1,0:T(8,128)(2,1)}, bf16[144,2688]{1,0:T(8,128)(2,1)}, u32[]{:S(2)}, u32[]{:S(2)}) collective-permute-start(bf16[144,2688]{1,0:T(8,128)(2,1)} %decode.6.refs_0_.refs_1_.own_ref), channel_id=1, source_target_pairs={{0,2},{1,3},{2,0},{3,1},{4,6},{5,7},{6,4},{7,5},{8,10},{9,11},{10,... | collective-permute-start | bytes 2322440 | tf_op jit(solution)/shard_map/ppermute | solution.py:540
  40.5 166.1 %collective-permute-start.10 = (bf16[512,5376]{1,0:T(8,128)(2,1)}, bf16[512,5376]{1,0:T(8,128)(2,1)}, u32[]{:S(2)}, u32[]{:S(2)}) collective-permute-start(bf16[512,5376]{1,0:T(8,128)(2,1)} %mix.2.refs_0_.refs_1_), channel_id=1, source_target_pairs={{0,8},{4,12},{8,0},{12,4},{1,9},{5,13},{9,1},{13,5},{2,10},{6,14},... | collective-permute-start | bytes 16515080 | tf_op jit(solution)/shard_map/ppermute | solution.py:540
  64.2 1.0 copy-start.3
  67.5 63.7 %collective-permute-start.5 = (bf16[192,2688]{1,0:T(8,128)(2,1)}, bf16[192,2688]{1,0:T(8,128)(2,1)S(1)}, u32[]{:S(2)}, u32[]{:S(2)}) collective-permute-start(bf16[192,2688]{1,0:T(8,128)(2,1)} %level.8.refs_0_.own_ref), channel_id=1, source_target_pairs={{0,1},{1,0},{2,3},{3,2},{4,5},{5,4},{6,7},{7,6},{8,9},{9,8},{10,11... | collective-permute-start | bytes 3096584 | tf_op jit(solution)/shard_map/ppermute | solution.py:540
  72.4 69.2 %collective-permute-start.4 = (bf16[192,2688]{1,0:T(8,128)(2,1)}, bf16[192,2688]{1,0:T(8,128)(2,1)}, u32[]{:S(2)}, u32[]{:S(2)}) collective-permute-start(bf16[192,2688]{1,0:T(8,128)(2,1)} %level.9.refs_0_.own_ref), channel_id=1, source_target_pairs={{0,2},{1,3},{2,0},{3,1},{4,6},{5,7},{6,4},{7,5},{8,10},{9,11},{10,... | collective-permute-start | bytes 3096584 | tf_op jit(solution)/shard_map/ppermute | solution.py:540
  89.5 58.2 %collective-permute-start.3 = (bf16[144,2688]{1,0:T(8,128)(2,1)}, bf16[144,2688]{1,0:T(8,128)(2,1)}, u32[]{:S(2)}, u32[]{:S(2)}) collective-permute-start(bf16[144,2688]{1,0:T(8,128)(2,1)} %decode.7.refs_14_.own_ref), channel_id=1, source_target_pairs={{0,1},{1,0},{2,3},{3,2},{4,5},{5,4},{6,7},{7,6},{8,9},{9,8},{10,11... | collective-permute-start | bytes 2322440 | tf_op jit(solution)/shard_map/ppermute | solution.py:540
  114.5 68.6 %collective-permute-start.9 = (bf16[144,2688]{1,0:T(8,128)(2,1)}, bf16[144,2688]{1,0:T(8,128)(2,1)S(1)}, u32[]{:S(2)}, u32[]{:S(2)}) collective-permute-start(bf16[144,2688]{1,0:T(8,128)(2,1)} %level.10.refs_14_.own_ref), channel_id=1, source_target_pairs={{0,1},{1,0},{2,3},{3,2},{4,5},{5,4},{6,7},{7,6},{8,9},{9,8},{10,11... | collective-permute-start | bytes 2322440 | tf_op jit(solution)/shard_map/ppermute | solution.py:540
  131.2 1.0 copy-start.8
  134.6 48.5 %collective-permute-start.7 = (bf16[192,2688]{1,0:T(8,128)(2,1)}, bf16[192,2688]{1,0:T(8,128)(2,1)S(1)}, u32[]{:S(2)}, u32[]{:S(2)}) collective-permute-start(bf16[192,2688]{1,0:T(8,128)(2,1)} %level.11.refs_0_.refs_6_), channel_id=1, source_target_pairs={{0,16},{16,0},{1,17},{17,1},{2,18},{18,2},{3,19},{19,3},{4,20},{20... | collective-permute-start | bytes 3096584 | tf_op jit(solution)/shard_map/ppermute | solution.py:540
  143.9 45.6 %collective-permute-start.8 = (bf16[192,2688]{1,0:T(8,128)(2,1)}, bf16[192,2688]{1,0:T(8,128)(2,1)}, u32[]{:S(2)}, u32[]{:S(2)}) collective-permute-start(bf16[192,2688]{1,0:T(8,128)(2,1)} %level.12.refs_0_.refs_8_), channel_id=1, source_target_pairs={{0,16},{16,0},{1,17},{17,1},{2,18},{18,2},{3,19},{19,3},{4,20},{20... | collective-permute-start | bytes 3096584 | tf_op jit(solution)/shard_map/ppermute | solution.py:540
  150.8 51.7 %collective-permute-start.11 = (bf16[144,2688]{1,0:T(8,128)(2,1)}, bf16[144,2688]{1,0:T(8,128)(2,1)S(1)}, u32[]{:S(2)}, u32[]{:S(2)}) collective-permute-start(bf16[144,2688]{1,0:T(8,128)(2,1)} %level.13.refs_14_.own_ref), channel_id=1, source_target_pairs={{0,2},{1,3},{2,0},{3,1},{4,6},{5,7},{6,4},{7,5},{8,10},{9,11},{10,... | collective-permute-start | bytes 2322440 | tf_op jit(solution)/shard_map/ppermute | solution.py:540
  183.1 0.9 copy-start.9
  184.0 1.0 copy-start.7
  188.1 18.5 %collective-permute-start.12 = (bf16[144,2688]{1,0:T(8,128)(2,1)}, bf16[144,2688]{1,0:T(8,128)(2,1)S(1)}, u32[]{:S(2)}, u32[]{:S(2)}) collective-permute-start(bf16[144,2688]{1,0:T(8,128)(2,1)} %level.14.refs_10_.refs_0_), channel_id=1, source_target_pairs={{0,16},{16,0},{1,17},{17,1},{2,18},{18,2},{3,19},{19,3},{4,20},{20... | collective-permute-start | bytes 2322440 | tf_op jit(solution)/shard_map/ppermute | solution.py:540
  202.5 0.9 copy-start.11
  206.6 1.4 copy-start.6
  206.6 0.9 copy-start.5
  207.5 19.7 %collective-permute-start.13 = (bf16[512,5376]{1,0:T(8,128)(2,1)}, bf16[512,5376]{1,0:T(8,128)(2,1)}, u32[]{:S(2)}, u32[]{:S(2)}) collective-permute-start(bf16[512,5376]{1,0:T(8,128)(2,1)} %gate.4.refs_1_.refs_3_), channel_id=1, source_target_pairs={{0,4},{4,0},{8,12},{12,8},{1,5},{5,1},{9,13},{13,9},{2,6},{6,2},{1... | collective-permute-start | bytes 16515080 | tf_op jit(solution)/shard_map/ppermute | solution.py:540
  208.0 19.2 %collective-permute-start.14 = (bf16[144,2688]{1,0:T(8,128)(2,1)S(1)}, bf16[144,2688]{1,0:T(8,128)(2,1)S(1)}, u32[]{:S(2)}, u32[]{:S(2)}) collective-permute-start(bf16[144,2688]{1,0:T(8,128)(2,1)S(1)} %copy-done.6), channel_id=1, source_target_pairs={{0,16},{16,0},{1,17},{17,1},{2,18},{18,2},{3,19},{19,3},{4,20},{20... | collective-permute-start | bytes 2322440 | tf_op jit(solution)/shard_map/ppermute | solution.py:540
  208.6 55.2 %reduce-scatter.6.cloned.1.call-start = ((), (), s32[]{:S(2)}) async-start(), calls=%async_computation.5 | async-start | bytes 983040 | tf_op jit(solution)/shard_map/reduce_scatter | solution.py:611
  227.2 0.9 copy-start.10
  241.1 53.4 %reduce-scatter.8.cloned.1.call-start = ((), (), s32[]{:S(2)}) async-start(), calls=%async_computation.6 | async-start | bytes 1474560 | tf_op jit(solution)/shard_map/reduce_scatter | solution.py:611
  259.3 4.5 %copy-start.4 = (bf16[1,384,256]{2,1,0:T(8,128)(2,1)S(1)}, bf16[1,384,256]{2,1,0:T(8,128)(2,1)}, u32[]{:S(2)}) copy-start(bf16[1,384,256]{2,1,0:T(8,128)(2,1)} %reduce-scatter.4.cloned.1.call-done) | copy-start | bytes 589828
  263.8 0.9 copy-start.1
  295.6 1.9 collective-permute-start.15
  295.7 7.2 %collective-permute-start.16 = (bf16[672,128]{1,0:T(8,128)(2,1)S(1)}, bf16[672,128]{1,0:T(8,128)(2,1)S(1)}, u32[]{:S(2)}, u32[]{:S(2)}) collective-permute-start(bf16[672,128]{1,0:T(8,128)(2,1)S(1)} %get-tuple-element.11), channel_id=1, source_target_pairs={{0,8},{4,12},{8,0},{12,4},{1,9},{5,13},{9,1},{13,5},{2,10},{6,14},... | collective-permute-start | bytes 516104 | tf_op jit(solution)/shard_map/ppermute | solution.py:540
  297.2 8.5 %collective-permute-start.17 = (bf16[672,128]{1,0:T(8,128)(2,1)S(1)}, bf16[672,128]{1,0:T(8,128)(2,1)S(1)}, u32[]{:S(2)}, u32[]{:S(2)}) collective-permute-start(bf16[672,128]{1,0:T(8,128)(2,1)S(1)} %get-tuple-element.10), channel_id=1, source_target_pairs={{0,12},{4,8},{8,4},{12,0},{1,13},{5,9},{9,5},{13,1},{2,14},{6,10},... | collective-permute-start | bytes 516104 | tf_op jit(solution)/shard_map/ppermute | solution.py:540
Sparse Core Ops, SparseCore 0:
  9.8 86.7 all-gather.1
  208.7 23.4 reduce-scatter.3
  241.2 22.4 reduce-scatter.5
  265.9 28.4 reduce-scatter.7

commit v2 on v1

--- a/solution.py
+++ b/solution.py
@@ -184,6 +184,7 @@
 EARLY = ((0, WIDE), (HALF, WIDE))
 LATE = ((WIDE, HALF - WIDE), (HALF + WIDE, HALF - WIDE))
 NT = (((1,), (1,)), ((), ()))
+EXPONENT = SCORE_SCALE / float(np.log(2.0))
 ANYWHERE = pl.BlockSpec(memory_space=pl.ANY)
 
 
@@ -276,7 +277,7 @@
 
 def dequant(half_id, codes, scales, first, size, earlier=()):
     width = codes.shape[1] // 2
-    step = 48
+    step = next(rows for rows in (112, 96, 48) if first % rows == size % rows == 0)
     groups = scales.shape[0]
     spread = np.repeat(np.eye(groups, dtype=np.float32) * CODE_STEP, GROUP, axis=1)
     return pl.pallas_call(
@@ -341,7 +342,7 @@
     )(value, *earlier)
 
 
-def project_kernel(chunks, count, half_ref, *refs):
+def project_kernel(chunks, count, place_ref, *refs):
     row_refs, attn_refs, out_side = refs[:count], refs[count : 2 * count], refs[2 * count]
     weights = refs[2 * count + 1 : 2 * count + 1 + 2 * len(chunks)]
     out_ref, total = refs[-2:]
@@ -380,7 +381,7 @@
                 ].astype(jnp.bfloat16)
 
 
-def project(half_id, shards, row_parts, attn_parts, out_side, weights, chunks, earlier=()):
+def project(place, shards, row_parts, attn_parts, out_side, weights, chunks, earlier=()):
     count = len(row_parts)
     rows, width = row_parts[0].shape
     steps = 6
@@ -395,8 +396,10 @@
         ]
     row_spec = pl.BlockSpec((rows, depth), lambda i, h: (0, lax.rem(i + h[0] * (last + 1), steps)))
 
-    def attn_spec(block):
-        return pl.BlockSpec((rows, out_side.shape[1]), lambda i, h: (block, 0))
+    def attn_spec(part, flip):
+        return pl.BlockSpec(
+            (rows, part.shape[1]), lambda i, h: (0 if flip is None else h[1] ^ flip, 0)
+        )
 
     shape = (shards, columns, count * rows // shards)
     return pl.pallas_call(
@@ -405,7 +408,7 @@
             num_scalar_prefetch=1,
             grid=(steps,),
             in_specs=[row_spec] * count
-            + [attn_spec(block) for _, block in attn_parts]
+            + [attn_spec(*part) for part in attn_parts]
             + [pl.BlockSpec(out_side.shape, lambda i, h: (0, 0))]
             + weight_specs
             + [ANYWHERE] * len(earlier),
@@ -416,7 +419,7 @@
         compiler_params=pltpu.CompilerParams(vmem_limit_bytes=56 << 20),
         cost_estimate=cost(10),
         name="project",
-    )(half_id, *row_parts, *[part for part, _ in attn_parts], out_side, *weights, *earlier)
+    )(place, *row_parts, *[part for part, _ in attn_parts], out_side, *weights, *earlier)
 
 
 def turned(head, cosine, signed_sine):
@@ -434,7 +437,7 @@
     values = [value0[...]]
     for block in (1, 2):
         key, value, cosine, sine, cached_key, cached_value = blocks[6 * block - 4 : 6 * block + 2]
-        inside = place_ref[pl.program_id(0)] >= block
+        inside = place_ref[0] >= block
         keys.append(
             jnp.where(inside, turned(key[...], cosine[...], sine[...]), cached_key[...])
         )
@@ -457,9 +460,7 @@
         )
 
         def score(block):
-            return (
-                lax.dot_general(query, block, NT, preferred_element_type=jnp.float32) * SCORE_SCALE
-            )
+            return lax.dot_general(query, block, NT, preferred_element_type=jnp.float32)
 
         def places(count, first):
             query_at = lax.broadcasted_iota(jnp.int32, (heads, half, count), 1) + low
@@ -478,58 +479,56 @@
                 jnp.max(score1, axis=1, keepdims=True), jnp.max(score2, axis=1, keepdims=True)
             ),
         )
-        mass = jnp.zeros_like(top)
-        total = jnp.zeros((heads * half, HD), jnp.float32)
+        top = top * EXPONENT
+        total = jnp.zeros((heads * half, 2 * HD), jnp.float32)
         for scores, block in (
             (score0, values[0][own, :]),
             (score1, values[1]),
             (score2, values[2][old, :]),
         ):
-            weight = jnp.exp(scores - top)
-            mass += jnp.sum(weight, axis=1, keepdims=True)
-            total += jnp.dot(
-                weight.astype(jnp.bfloat16), block, preferred_element_type=jnp.float32
-            )
-        total = (total / mass).astype(jnp.bfloat16)
+            weight = jnp.exp2(scores * EXPONENT - top).astype(jnp.bfloat16)
+            block = jnp.concatenate([block, jnp.ones_like(block)], axis=1)
+            total += jnp.dot(weight, block, preferred_element_type=jnp.float32)
+        total = (total[:, :HD] / total[:, HD:]).astype(jnp.bfloat16)
         for head in range(heads):
             out_ref[here, head * HD : (head + 1) * HD] = total[head * half : (head + 1) * half]
 
 
-def attend(places, kv_heads, cosine, signed_sine, all_shared, ordered, earlier, weight):
+def attend(places, queries, cosine, signed_sine, all_pairs, ordered, earlier, weight):
     rows = ordered.shape[0] // 2
-    first = 2 * kv_heads * HD
-    width = all_shared.shape[1] - first
+    width = queries.shape[1]
+    kv_heads = all_pairs.shape[1] // (2 * HD)
     wide = width // kv_heads
-    parts = places.shape[0]
+    gathered = queries.shape[0] > rows
 
     def pair_specs(row):
         return [
-            pl.BlockSpec((rows, HD), lambda t, i, p: (row(p[t]), i)),
-            pl.BlockSpec((rows, HD), lambda t, i, p: (row(p[t]), kv_heads + i)),
+            pl.BlockSpec((rows, HD), lambda i, p: (row(p[0]), i)),
+            pl.BlockSpec((rows, HD), lambda i, p: (row(p[0]), kv_heads + i)),
         ]
 
     def table_specs(row):
-        return [pl.BlockSpec((rows, HD), lambda t, i, p: (row(p[t]), 0))] * 2
+        return [pl.BlockSpec((rows, HD), lambda i, p: (row(p[0]), 0))] * 2
 
     def back(block):
         return lambda place: jnp.maximum(place - block, 0)
 
-    specs = [pl.BlockSpec((rows, wide), lambda t, i, p: (p[t], first // wide + i))]
+    specs = [pl.BlockSpec((rows, wide), lambda i, p: (p[0] if gathered else 0, i))]
     specs += table_specs(back(0)) + pair_specs(back(0))
-    operands = [all_shared, cosine, signed_sine, all_shared, all_shared]
+    operands = [queries, cosine, signed_sine, all_pairs, all_pairs]
     for block in (1, 2):
         specs += pair_specs(back(block)) + table_specs(back(block))
         specs += pair_specs(lambda place, block=block: jnp.minimum(place + 2 - block, 1))
-        operands += [all_shared, all_shared, cosine, signed_sine, ordered, ordered]
+        operands += [all_pairs, all_pairs, cosine, signed_sine, ordered, ordered]
     return pl.pallas_call(
         attend_kernel,
         grid_spec=pltpu.PrefetchScalarGridSpec(
             num_scalar_prefetch=1,
-            grid=(parts, kv_heads),
+            grid=(kv_heads,),
             in_specs=specs + [ANYWHERE] * len(earlier),
-            out_specs=pl.BlockSpec((rows, wide), lambda t, i, p: (t, i)),
+            out_specs=pl.BlockSpec((rows, wide), lambda i, p: (0, i)),
         ),
-        out_shape=jax.ShapeDtypeStruct((parts * rows, width), jnp.bfloat16),
+        out_shape=jax.ShapeDtypeStruct((rows, width), jnp.bfloat16),
         compiler_params=pltpu.CompilerParams(vmem_limit_bytes=56 << 20),
         cost_estimate=cost(weight),
         name="attend",
@@ -549,8 +548,8 @@
     side = seq_index >> 1
     tok_rows = queries.shape[0]
 
-    shared = jnp.concatenate([key_value.reshape(tok_rows, -1), queries], axis=1)
-    all_shared = lax.all_gather(shared, "seq", axis=0, tiled=True)
+    pairs = key_value.reshape(tok_rows, -1)
+    all_pairs = lax.all_gather(pairs, "seq", axis=0, tiled=True)
 
     def both_cores(value):
         return [value, flipped(value, "seq", 1)]
@@ -558,9 +557,10 @@
     codes = down_codes.T
     out_own = out_weight.T
     (piece_a, piece_c), (piece_b, piece_d) = EARLY, LATE
-    piece_a = dequant(half_id, codes, down_scales, *piece_a, (shared,))
-    piece_c = dequant(half_id, codes, down_scales, *piece_c, (piece_a,))
-    piece_b = dequant(half_id, codes, down_scales, *piece_b, (piece_c,))
+    piece_a = dequant(half_id, codes, down_scales, *piece_a)
+    piece_c = dequant(half_id, codes, down_scales, *piece_c, (piece_a, pairs))
+    near_queries = flipped(queries, "seq", 1)
+    piece_b = dequant(half_id, codes, down_scales, *piece_b, (piece_c, near_queries))
     near_hidden = flipped(hidden, "seq", 1)
     rotated = mix_hidden(hidden, piece_b)
 
@@ -576,58 +576,62 @@
     doubled = jnp.concatenate([cache, cache], axis=0)
     ordered = lax.dynamic_slice_in_dim(doubled, first_pos % WINDOW, WINDOW, 0)
 
-    kv_heads = key_value.shape[2] // HD
 
     piece_a = level_step(piece_a, 2, (rotated, ordered, cosine, signed_sine))
     piece_c = level_step(piece_c, 1, (piece_a,))
-    own_rows = [rotated, mix_hidden(near_hidden, piece_c)]
-    def attended_by(flip, earlier, weight):
+
+
+    def attended_by(flip, rows, earlier, weight):
         places = (seq_index ^ flip).reshape(1)
-        return attend(
-            places, kv_heads, cosine, signed_sine, all_shared, ordered, earlier, weight
-        ), 0
-
-    late_d = dequant(half_id, codes, down_scales, *LATE[1], (own_rows[1],))
-    attended = [None] * 4
-    attended[0] = attended_by(0, (late_d,), 13)
-    piece_b = level_step(piece_b, 2, (piece_c, attended[0][0]))
-    attended[2] = attended_by(2, (piece_b,), 13)
-    piece_a = level_step(piece_a, 1, (attended[2][0],))
+        return attend(places, rows, cosine, signed_sine, all_pairs, ordered, earlier, weight)
+
+    attended = attended_by(0, queries, (piece_c,), 13)
+    all_attended = lax.all_gather(attended, "seq", axis=0, tiled=True)
+    late_d = dequant(half_id, codes, down_scales, *LATE[1], (attended,))
+    own_rows = [rotated, mix_hidden(near_hidden, late_d)]
+    piece_b = level_step(piece_b, 2, (piece_c, own_rows[1]))
+    piece_a = level_step(piece_a, 1, (piece_b,))
     across_a = flipped(piece_a, "group", 1)
     piece_c = level_step(piece_c, 2, (piece_a,))
     across_c = flipped(piece_c, "group", 1)
     piece_d = level_step(late_d, 1, (piece_c,))
-    attended[1] = attended_by(1, (piece_d,), 0)
-    attended[3] = attended_by(3, (attended[1][0],), 0)
-    piece_b = level_step(piece_b, 1, (attended[3][0], across_a))
+    near_attended = attended_by(1, near_queries, (piece_d,), 0)
+    piece_b = level_step(piece_b, 1, (near_attended, across_a))
     across_b = flipped(piece_b, "group", 1)
-    own_attn, far_attn = attended[:2], attended[2:]
+    place = jnp.stack([half_id[0], seq_index])
+    own_attn = [(attended, None), (near_attended, None)]
+    far_attn = [(all_attended, 2), (all_attended, 3)]
     shards = lax.axis_size("tp")
 
     def reduced(rows, attn, weights, chunks, earlier=(), after=()):
-        partial = project(half_id, shards, rows, attn, out_own, weights, chunks, earlier)
+        partial = project(place, shards, rows, attn, out_own, weights, chunks, earlier)
         if after:
             partial = gate(partial, *after)
         return lax.psum_scatter(partial, "tp", scatter_dimension=0, tiled=True)[0], partial
 
     early = [piece_a, across_a, piece_c, across_c]
     own_early, own_done = reduced(own_rows, own_attn, early, EARLY, (piece_b,))
-    piece_d = level_step(piece_d, 2, (piece_b, own_done))
+    piece_d = level_step(piece_d, 2, (piece_b, own_done,across_b))
     across_d = flipped(piece_d, "group", 1)
+    far_rows = both_cores(gate(flipped(rotated, "seq", 2), piece_d))
     late = [piece_b, across_b, piece_d, across_d]
-    far_rows = both_cores(gate(flipped(rotated, "seq", 2), piece_d,across_b))
-    far_early, far_done = reduced(far_rows, far_attn, early, EARLY, (across_d,))
+    far_early, far_done = reduced(far_rows, far_attn, early, EARLY, (piece_d,))
     all_late, _ = reduced(
         own_rows + far_rows, own_attn + far_attn, late, LATE, (far_done, own_early), (far_early,)
     )
     kept = tok_rows // shards
-    all_early = jnp.concatenate([own_early, far_early], axis=1)
-    sums = jnp.concatenate(
-        [all_early[:WIDE], all_late[: HALF - WIDE], all_early[WIDE:], all_late[HALF - WIDE :]],
-        axis=0,
-    )
-    strips = [sums[:, i * kept : (i + 1) * kept] for i in range(4)]
-    strips = strips[:1] + [flipped(strips[i], "seq", i) for i in (1, 2, 3)]
+
+    def handed_out(sums):
+        strips = [sums[:, i * kept : (i + 1) * kept] for i in range(4)]
+        return strips[:1] + [flipped(strips[i], "seq", i) for i in (1, 2, 3)]
+
+    early_strips = handed_out(jnp.concatenate([own_early, far_early], axis=1))
+    late_strips = handed_out(all_late)
+    wide, rest = WIDE, HALF - WIDE
+    strips = [
+        jnp.concatenate([x[:wide], y[:rest], x[wide:], y[rest:]], axis=0)
+        for x, y in zip(early_strips, late_strips)
+    ]
     strips = [jnp.where(core == 0, strips[i], strips[i ^ 1]) for i in range(4)]
     strips = [jnp.where(side == 0, strips[i], strips[i ^ 2]) for i in range(4)]
     return jnp.concatenate(strips, axis=0).T

time: 319 us -> 291 us (0.912); the launches traced: 314 us -> 290 us
  Pallas kernels: 165 us -> 134 us
  waiting for transfers between devices: 83.7 us -> 87.2 us
    pallas_call x4 -> x2, Pallas kernels: 58.6 us -> 28.1 us  [attend(): pl.pallas_call(attend_kernel, grid_spec=pltpu.PrefetchScalarGridSpec(num_...]
    ppermute x18 -> x22, waiting for transfers between devices: 42.5 us -> 56.8 us  [flipped(): lax.ppermute(value, axis, [(i, i ^ bit) for i in range(lax.axis_size(axis...]
    all_gather x1 -> x2, waiting for transfers between devices: 6.95 us -> 0.01 us  [the longest x1 0.01 us: planned(): all_pairs = lax.all_gather(pairs, 'seq', axis=0, tiled=True)]
    reduce_scatter x3, waiting for transfers between devices: 34.2 us -> 30.4 us  [reduced(): lax.psum_scatter(partial, 'tp', scatter_dimension=0, tiled=True)[0]]
    ppermute x18 -> x22, starting transfers between devices: 22.7 us -> 25.1 us  [flipped(): lax.ppermute(value, axis, [(i, i ^ bit) for i in range(lax.axis_size(axis...]
    unnamed x27 -> x24, local copies, waits for them, and re-layouts: 13 us -> 12.1 us
  transfers between devices with their start and end apart: 22 -> 27, of which waited for: 10 -> 14; matrix products, arithmetic and copies ran while one was open for 4% -> 5% of each run, Pallas kernels for 52% -> 46%
where the time goes in v2:
time: 291 us; the launch traced here: 290 us
  Pallas kernels  134 us (46%)
  waiting for transfers between devices  87.2 us (30%)
  starting transfers between devices  25.3 us (9%)
  between operations  16 us (5%)
  local copies, waits for them, and re-layouts  15 us (5%)
  other arithmetic  11.9 us (4%)
    ppermute x22, waiting for transfers between devices, flipped(): lax.ppermute(value, axis, [(i, i ^ bit) for i in range(lax.axis_size(axis...  56.8 us
    pallas_call x3, Pallas kernels, project(): pl.pallas_call(lambda *refs: project_kernel(chunks, count, *refs), grid_s...  46.2 us
    reduce_scatter x3, waiting for transfers between devices, reduced(): lax.psum_scatter(partial, 'tp', scatter_dimension=0, tiled=True)[0]  30.4 us
    pallas_call x2, Pallas kernels, attend(): pl.pallas_call(attend_kernel, grid_spec=pltpu.PrefetchScalarGridSpec(num_...  28.1 us
    ppermute x22, starting transfers between devices, flipped(): lax.ppermute(value, axis, [(i, i ^ bit) for i in range(lax.axis_size(axis...  25.1 us
    pallas_call x2, Pallas kernels, mix_hidden(): pl.pallas_call(mix_kernel, grid=(rows // step,), in_specs=[pl.BlockSpec((...  22.6 us
    pallas_call x8, Pallas kernels, level_step(): pl.pallas_call(level_kernel, grid_spec=pltpu.PrefetchScalarGridSpec(num_s...  22.1 us
    pallas_call x4, Pallas kernels, dequant(): pl.pallas_call(lambda *refs: dequant_kernel(first, *refs), grid_spec=pltp...  14.7 us
  transfers between devices with their start and end apart: 27, of which 14 were waited for; matrix products, arithmetic and copies ran while one was open for 5% of the time, Pallas kernels for 46%

profile of v2, /device:TPU:0, one launch (start us, length us, event | category | flops | bytes accessed | tf_op | source)
XLA Modules:
  0.0 289.6 jit_solution(7827217887635477986)
XLA Ops:
  6.5 2.5 copy.19
  9.6 2.9 decode.4.refs_4_.own_ref
  12.5 3.6 %collective-permute-start.3 = (bf16[192,2688]{1,0:T(8,128)(2,1)}, bf16[192,2688]{1,0:T(8,128)(2,1)}, u32[]{:S(2)}, u32[]{:S(2)}) collective-permute-start(bf16[192,2688]{1,0:T(8,128)(2,1)} %decode.4.refs_4_.own_ref), channel_id=1, source_target_pairs={{0,2},{1,3},{2,0},{3,1},{4,6},{5,7},{6,4},{7,5},{8,10},{9,11},{10,... | collective-permute-start | bytes 3096584 | tf_op jit(solution)/shard_map/ppermute | solution.py:539
  16.1 4.4 %decode.5.refs_4_.own_ref = bf16[192,2688]{1,0:T(8,128)(2,1)} custom-call(s32[1]{0:T(128)} %bitcast.refs_0_, s32[672,5376]{1,0:T(8,128)} %bitcast.18, s32[42,672]{1,0:T(8,128)} %refs_2_.7, bf16[42,5376]{1,0:T(8,128)(2,1)} %constant.46.clone.refs_3_, bf16[192,2688]{1,0:T(8,128)(2,1)} %decode.4.refs_4_.own_ref, bf16[512,1024]{1,0:T(8,128)(2,1)} %bitcast.22), custom_call_target="tpu_custom_call" | custom-call | flops 3450000128 | bytes 1 | tf_op jit(solution)/shard_map/decode/pallas_call | solution.py:283
  20.5 1.6 collective-permute-start.2
  22.7 2.1 copy.20
  25.8 3.7 %decode.6.refs_0_.refs_1_.own_ref = bf16[144,2688]{1,0:T(8,128)(2,1)} custom-call(s32[1]{0:T(128)} %bitcast.refs_0_, s32[672,5376]{1,0:T(8,128)} %bitcast.19, s32[42,672]{1,0:T(8,128)} %refs_2_.7, bf16[42,5376]{1,0:T(8,128)(2,1)} %constant.46.clone.refs_3_, bf16[192,2688]{1,0:T(8,128)(2,1)} %decode.5.refs_4_.own_ref, bf16[512,1024]{1,0:T(8,128)(2,1)} %copy-done), custom_call_target="tpu_custom_call" | custom-call | flops 3450000128 | bytes 1 | tf_op jit(solution)/shard_map/decode/pallas_call | solution.py:283
  32.8 11.3 %mix.2.refs_0_.refs_1_ = bf16[512,5376]{1,0:T(8,128)(2,1)} custom-call(bf16[512,5376]{1,0:T(8,128)(2,1)} %hidden_ref.1, bf16[864,768]{1,0:T(8,128)(2,1)} %constant.47.clone.table_ref, bf16[144,2688]{1,0:T(8,128)(2,1)} %decode.6.refs_0_.refs_1_.own_ref), custom_call_target="tpu_custom_call" | custom-call | flops 18400000000 | bytes 1 | tf_op jit(solution)/shard_map/mix/pallas_call | solution.py:247
  44.1 1.5 collective-permute-start.11
  46.3 4.4 %fusion.refs_1_.refs_6_.refs_7_.refs_12_.refs_13_ = bf16[1024,1024]{1,0:T(8,128)(2,1)} fusion(s32[]{:T(128)S(6)} %select_n.64, bf16[1024,1024]{1,0:T(8,128)(2,1)S(1)} %bitcast.23), kind=kLoop, calls=%fused_computation.2 | loop fusion | flops 4194304 | bytes 4194308 | tf_op jit(solution)/shard_map/concatenate | solution.py:576
  50.7 3.7 %fusion.1 = (f32[2048,64]{1,0:T(8,128)S(1)}, f32[2048,64]{1,0:T(8,128)S(1)}, f32[2048,64]{1,0:T(8,128)S(1)}) fusion(f32[64]{0:T(128)S(1)} %multiply_power_fusion, f32[2048]{0:T(1024)S(1)} %add_convert_fusion), kind=kLoop, calls=%fused_computation.8 | loop fusion | flops 262144 | bytes 1581312 | tf_op jit(solution)/shard_map/neg | solution.py:574
  54.5 2.0 pad_maximum_fusion
  56.4 5.8 %collective-permute-done.3.partner_ref = bf16[192,2688]{1,0:T(8,128)(2,1)} collective-permute-done((bf16[192,2688]{1,0:T(8,128)(2,1)}, bf16[192,2688]{1,0:T(8,128)(2,1)}, u32[]{:S(2)}, u32[]{:S(2)}) %collective-permute-start.3) | collective-permute-done | bytes 1032224 | tf_op jit(solution)/shard_map/ppermute | solution.py:539
  62.3 2.4 level.8.refs_0_.own_ref
  65.4 2.9 %collective-permute-done.2.partner_ref = bf16[192,2688]{1,0:T(8,128)(2,1)} collective-permute-done((bf16[192,2688]{1,0:T(8,128)(2,1)}, bf16[192,2688]{1,0:T(8,128)(2,1)}, u32[]{:S(2)}, u32[]{:S(2)}) %collective-permute-start.2) | collective-permute-done | bytes 1032224 | tf_op jit(solution)/shard_map/ppermute | solution.py:539
  68.3 2.4 level.9.refs_14_.refs_0_.own_ref
  71.3 14.1 %attend.2.refs_4_.refs_3_.refs_5_ = bf16[512,1024]{1,0:T(8,128)(2,1)} custom-call(s32[1]{0:T(128)} %bitcast.1.place_ref, bf16[512,1024]{1,0:T(8,128)(2,1)} %query_ref.1, f32[2048,128]{1,0:T(8,128)} %get-tuple-element.29.refs_2_.cosine_ref.refs_4_.refs_10_, f32[2048,128]{1,0:T(8,128)} %get-tuple-element.30.refs_3_.sine_ref.refs_5_.refs_11_, ...), custom_call_target="tpu_custom_call" | custom-call | flops 14949999616 | bytes 1 | tf_op jit(solution)/shard_map/attend/pallas_call | solution.py:523
  85.4 3.8 %decode.7.refs_0_.own_ref = bf16[144,2688]{1,0:T(8,128)(2,1)} custom-call(s32[1]{0:T(128)} %bitcast.refs_0_, s32[672,5376]{1,0:T(8,128)} %bitcast.20, s32[42,672]{1,0:T(8,128)} %refs_2_.7, bf16[42,5376]{1,0:T(8,128)(2,1)} %constant.46.clone.refs_3_, bf16[512,1024]{1,0:T(8,128)(2,1)} %attend.2.refs_4_.refs_3_.refs_5_), custom_call_target="tpu_custom_call" | custom-call | flops 3450000128 | bytes 1 | tf_op jit(solution)/shard_map/decode/pallas_call | solution.py:283
  89.9 11.3 %mix.3.refs_1_.refs_2_ = bf16[512,5376]{1,0:T(8,128)(2,1)} custom-call(bf16[512,5376]{1,0:T(8,128)(2,1)} %collective-permute-done.1.hidden_ref, bf16[864,768]{1,0:T(8,128)(2,1)} %constant.47.clone.table_ref, bf16[144,2688]{1,0:T(8,128)(2,1)} %decode.7.refs_0_.own_ref), custom_call_target="tpu_custom_call" | custom-call | flops 18400000000 | bytes 1 | tf_op jit(solution)/shard_map/mix/pallas_call | solution.py:247
  101.2 3.1 %level.10.refs_0_.own_ref = bf16[144,2688]{1,0:T(8,128)(2,1)} custom-call(s32[1]{0:T(128)} %bitcast.5.sign_ref, bf16[144,2688]{1,0:T(8,128)(2,1)} %decode.6.refs_0_.refs_1_.own_ref, bf16[144,2688]{1,0:T(8,128)(2,1)} %collective-permute-done.7.partner_ref, bf16[192,2688]{1,0:T(8,128)(2,1)} %level.9.refs_14_.refs_0_.own_ref, bf16[512,5376]{1,0:T(8,128)(2,1)} %mix.3.refs_1_.refs_2_), custom_call_target="tpu_custom_call" | custom-call | flops 3450000128 | bytes 1 | tf_op jit(solution)/shard_map/level/pallas_call | solution.py:315
  104.3 1.4 collective-permute-start.10
  105.7 7.0 %collective-permute-done.6.partner_ref = bf16[192,2688]{1,0:T(8,128)(2,1)S(1)} collective-permute-done((bf16[192,2688]{1,0:T(8,128)(2,1)}, bf16[192,2688]{1,0:T(8,128)(2,1)S(1)}, u32[]{:S(2)}, u32[]{:S(2)}) %collective-permute-start.6) | collective-permute-done | bytes 1032224 | tf_op jit(solution)/shard_map/ppermute | solution.py:539
  113.7 2.3 level.11.refs_0_.refs_6_
  116.0 1.8 collective-permute-start.8
  117.8 21.7 %collective-permute-done.5.partner_ref = bf16[192,2688]{1,0:T(8,128)(2,1)S(1)} collective-permute-done((bf16[192,2688]{1,0:T(8,128)(2,1)}, bf16[192,2688]{1,0:T(8,128)(2,1)S(1)}, u32[]{:S(2)}, u32[]{:S(2)}) %collective-permute-start.5) | collective-permute-done | bytes 1032224 | tf_op jit(solution)/shard_map/ppermute | solution.py:539
  140.4 2.4 level.12.refs_0_.refs_8_
  142.8 1.5 collective-permute-start.9
  145.1 3.1 %level.13.refs_14_.own_ref = bf16[144,2688]{1,0:T(8,128)(2,1)} custom-call(s32[1]{0:T(128)} %bitcast.4.sign_ref, bf16[144,2688]{1,0:T(8,128)(2,1)} %decode.7.refs_0_.own_ref, bf16[144,2688]{1,0:T(8,128)(2,1)} %collective-permute-done.4.partner_ref, bf16[192,2688]{1,0:T(8,128)(2,1)} %level.12.refs_0_.refs_8_), custom_call_target="tpu_custom_call" | custom-call | flops 3450000128 | bytes 1 | tf_op jit(solution)/shard_map/level/pallas_call | solution.py:315
  148.2 2.6 collective-permute-start.12
  150.8 14.0 %attend.3.refs_0_.refs_4_.refs_6_ = bf16[512,1024]{1,0:T(8,128)(2,1)} custom-call(s32[1]{0:T(128)} %bitcast.6.place_ref, bf16[512,1024]{1,0:T(8,128)(2,1)} %copy-done, f32[2048,128]{1,0:T(8,128)} %get-tuple-element.29.refs_2_.cosine_ref.refs_4_.refs_10_, f32[2048,128]{1,0:T(8,128)} %get-tuple-element.30.refs_3_.sine_ref.refs_5_.refs_11_, ...), custom_call_target="tpu_custom_call" | custom-call | flops 1 | bytes 1 | tf_op jit(solution)/shard_map/attend/pallas_call | solution.py:523
  164.8 1.6 collective-permute-done.10.partner_ref
  167.4 3.1 %level.14.refs_10_.refs_0_ = bf16[144,2688]{1,0:T(8,128)(2,1)} custom-call(s32[1]{0:T(128)} %bitcast.4.sign_ref, bf16[144,2688]{1,0:T(8,128)(2,1)} %level.10.refs_0_.own_ref, bf16[144,2688]{1,0:T(8,128)(2,1)} %collective-permute-done.10.partner_ref, bf16[512,1024]{1,0:T(8,128)(2,1)} %attend.3.refs_0_.refs_4_.refs_6_, bf16[192,2688]{1,0:T(8,128)(2,1)} %copy-done.4), custom_call_target="tpu_custom_call" | custom-call | flops 3450000128 | bytes 1 | tf_op jit(solution)/shard_map/level/pallas_call | solution.py:315
  170.6 2.3 collective-permute-start.13
  173.8 13.7 %project.3.refs_1_ = bf16[4,384,256]{2,1,0:T(8,128)(2,1)} custom-call(s32[2]{0:T(128)} %pad_add_fusion.refs_0_, bf16[512,5376]{1,0:T(8,128)(2,1)} %mix.2.refs_0_.refs_1_, bf16[512,5376]{1,0:T(8,128)(2,1)} %mix.3.refs_1_.refs_2_, bf16[512,1024]{1,0:T(8,128)(2,1)} %attend.2.refs_4_.refs_3_.refs_5_, bf16[512,1024]{1,0:T(8,128)(2,1)} %attend.3.refs_0_.refs_4_.refs_6_, ...), custom_call_target="tpu_custom_call" | custom-call | flops 11500000256 | bytes 1 | tf_op jit(solution)/shard_map/project/pallas_call | solution.py:405
  187.5 2.0 collective-permute-done.13.refs_2_.refs_11_
  190.4 3.1 %level.15.refs_1_.refs_10_.refs_12_ = bf16[144,2688]{1,0:T(8,128)(2,1)} custom-call(s32[1]{0:T(128)} %bitcast.5.sign_ref, bf16[144,2688]{1,0:T(8,128)(2,1)} %level.13.refs_14_.own_ref, bf16[144,2688]{1,0:T(8,128)(2,1)} %copy-done.10, bf16[144,2688]{1,0:T(8,128)(2,1)} %level.14.refs_10_.refs_0_, bf16[4,384,256]{2,1,0:T(8,128)(2,1)} %project.3.refs_1_, ...), custom_call_target="tpu_custom_call" | custom-call | flops 3450000128 | bytes 1 | tf_op jit(solution)/shard_map/level/pallas_call | solution.py:315
  194.7 1.7 collective-permute-start.15
  196.4 6.6 %collective-permute-done.14.refs_2_.refs_4_ = bf16[512,5376]{1,0:T(8,128)(2,1)} collective-permute-done((bf16[512,5376]{1,0:T(8,128)(2,1)}, bf16[512,5376]{1,0:T(8,128)(2,1)}, u32[]{:S(2)}, u32[]{:S(2)}) %collective-permute-start.14) | collective-permute-done | bytes 5505056 | tf_op jit(solution)/shard_map/ppermute | solution.py:539
  203.0 13.9 %project.4.refs_14_ = bf16[4,384,256]{2,1,0:T(8,128)(2,1)} custom-call(s32[2]{0:T(128)} %pad_add_fusion.refs_0_, bf16[512,5376]{1,0:T(8,128)(2,1)} %gate.4.refs_1_.refs_3_, bf16[512,5376]{1,0:T(8,128)(2,1)} %collective-permute-done.14.refs_2_.refs_4_, bf16[2048,1024]{1,0:T(8,128)(2,1)} %all-gather.5.cloned.1.call-done.refs_3_.refs_4_.refs_7_.refs_8_, ...), custom_call_target="tpu_custom_call" | custom-call | flops 11500000256 | bytes 1 | tf_op jit(solution)/shard_map/project/pallas_call | solution.py:405
  217.0 1.2 reduce-scatter.4.cloned.1.call-done
  218.2 18.6 %project.5.refs_0_ = bf16[4,288,512]{2,1,0:T(8,128)(2,1)} custom-call(s32[2]{0:T(128)} %pad_add_fusion.refs_0_, bf16[512,5376]{1,0:T(8,128)(2,1)} %mix.2.refs_0_.refs_1_, bf16[512,5376]{1,0:T(8,128)(2,1)} %mix.3.refs_1_.refs_2_, bf16[512,5376]{1,0:T(8,128)(2,1)} %gate.4.refs_1_.refs_3_, bf16[512,5376]{1,0:T(8,128)(2,1)} %collective-permute-done.14.refs_2_.refs_4_, ...), custom_call_target="tpu_custom_call" | custom-call | flops 11500000256 | bytes 1 | tf_op jit(solution)/shard_map/project/pallas_call | solution.py:405
  236.8 6.2 %reduce-scatter.6.cloned.1.call-done = bf16[1,384,256]{2,1,0:T(8,128)(2,1)} async-done(((bf16[4,384,256]{2,1,0:T(8,128)(2,1)}), bf16[1,384,256]{2,1,0:T(8,128)(2,1)}) %reduce-scatter.6.cloned.1.call-update) | async-done | bytes 196624 | tf_op jit(solution)/shard_map/reduce_scatter | solution.py:610
  243.9 1.5 collective-permute-start.18
  245.7 3.0 %collective-permute-done.18 = bf16[384,128]{1,0:T(8,128)(2,1)S(1)} collective-permute-done((bf16[384,128]{1,0:T(8,128)(2,1)S(1)}, bf16[384,128]{1,0:T(8,128)(2,1)S(1)}, u32[]{:S(2)}, u32[]{:S(2)}) %collective-permute-start.18) | collective-permute-done | bytes 98336 | tf_op jit(solution)/shard_map/ppermute | solution.py:539
  248.7 1.9 collective-permute-done.20
  250.6 23.0 %reduce-scatter.8.cloned.1.call-done = bf16[1,288,512]{2,1,0:T(8,128)(2,1)} async-done(((bf16[4,288,512]{2,1,0:T(8,128)(2,1)}), bf16[1,288,512]{2,1,0:T(8,128)(2,1)}) %reduce-scatter.8.cloned.1.call-update) | async-done | bytes 294928 | tf_op jit(solution)/shard_map/reduce_scatter | solution.py:610
  275.5 1.5 collective-permute-start.19
  277.3 3.0 %collective-permute-done.19 = bf16[288,128]{1,0:T(8,128)(2,1)S(1)} collective-permute-done((bf16[288,128]{1,0:T(8,128)(2,1)S(1)}, bf16[288,128]{1,0:T(8,128)(2,1)S(1)}, u32[]{:S(2)}, u32[]{:S(2)}) %collective-permute-start.19) | collective-permute-done | bytes 73760 | tf_op jit(solution)/shard_map/ppermute | solution.py:539
  (80 shorter events, 18.2 us)
Async XLA Ops:
  6.5 64.8 %all-gather.3.cloned.1.call-start = ((), (), s32[]{:S(2)}) async-start(), calls=%async_computation.3 | async-start | bytes 5242880 | tf_op jit(solution)/shard_map/all_gather | solution.py:552
  9.0 187.4 %all-gather.5.cloned.1.call-start = ((), (), s32[]{:S(2)}) async-start(), calls=%async_computation.5 | async-start | bytes 5242880 | tf_op jit(solution)/shard_map/all_gather | solution.py:589
  9.1 15.8 %collective-permute-start = (bf16[512,1024]{1,0:T(8,128)(2,1)}, bf16[512,1024]{1,0:T(8,128)(2,1)S(1)}, u32[]{:S(2)}, u32[]{:S(2)}) collective-permute-start(bf16[512,1024]{1,0:T(8,128)(2,1)} %query_ref.1), channel_id=1, source_target_pairs={{0,4},{4,0},{8,12},{12,8},{1,5},{5,1},{9,13},{13,9},{2,6},{6,2},{1... | collective-permute-start | bytes 3145736 | tf_op jit(solution)/shard_map/ppermute | solution.py:539
  12.5 49.8 %collective-permute-start.3 = (bf16[192,2688]{1,0:T(8,128)(2,1)}, bf16[192,2688]{1,0:T(8,128)(2,1)}, u32[]{:S(2)}, u32[]{:S(2)}) collective-permute-start(bf16[192,2688]{1,0:T(8,128)(2,1)} %decode.4.refs_4_.own_ref), channel_id=1, source_target_pairs={{0,2},{1,3},{2,0},{3,1},{4,6},{5,7},{6,4},{7,5},{8,10},{9,11},{10,... | collective-permute-start | bytes 3096584 | tf_op jit(solution)/shard_map/ppermute | solution.py:539
  20.5 47.9 %collective-permute-start.2 = (bf16[192,2688]{1,0:T(8,128)(2,1)}, bf16[192,2688]{1,0:T(8,128)(2,1)}, u32[]{:S(2)}, u32[]{:S(2)}) collective-permute-start(bf16[192,2688]{1,0:T(8,128)(2,1)} %decode.5.refs_4_.own_ref), channel_id=1, source_target_pairs={{0,1},{1,0},{2,3},{3,2},{4,5},{5,4},{6,7},{7,6},{8,9},{9,8},{10,11... | collective-permute-start | bytes 3096584 | tf_op jit(solution)/shard_map/ppermute | solution.py:539
  22.0 67.2 %collective-permute-start.1 = (bf16[512,5376]{1,0:T(8,128)(2,1)}, bf16[512,5376]{1,0:T(8,128)(2,1)}, u32[]{:S(2)}, u32[]{:S(2)}) collective-permute-start(bf16[512,5376]{1,0:T(8,128)(2,1)} %hidden_ref.1), channel_id=1, source_target_pairs={{0,4},{4,0},{8,12},{12,8},{1,5},{5,1},{9,13},{13,9},{2,6},{6,2},{1... | collective-permute-start | bytes 16515080 | tf_op jit(solution)/shard_map/ppermute | solution.py:539
  24.9 1.0 copy-start
  32.0 69.2 %collective-permute-start.7 = (bf16[144,2688]{1,0:T(8,128)(2,1)}, bf16[144,2688]{1,0:T(8,128)(2,1)}, u32[]{:S(2)}, u32[]{:S(2)}) collective-permute-start(bf16[144,2688]{1,0:T(8,128)(2,1)} %decode.6.refs_0_.refs_1_.own_ref), channel_id=1, source_target_pairs={{0,2},{1,3},{2,0},{3,1},{4,6},{5,7},{6,4},{7,5},{8,10},{9,11},{10,... | collective-permute-start | bytes 2322440 | tf_op jit(solution)/shard_map/ppermute | solution.py:539
  44.1 149.4 %collective-permute-start.11 = (bf16[512,5376]{1,0:T(8,128)(2,1)}, bf16[512,5376]{1,0:T(8,128)(2,1)}, u32[]{:S(2)}, u32[]{:S(2)}) collective-permute-start(bf16[512,5376]{1,0:T(8,128)(2,1)} %mix.2.refs_0_.refs_1_), channel_id=1, source_target_pairs={{0,8},{4,12},{8,0},{12,4},{1,9},{5,13},{9,1},{13,5},{2,10},{6,14},... | collective-permute-start | bytes 16515080 | tf_op jit(solution)/shard_map/ppermute | solution.py:539
  64.6 48.1 %collective-permute-start.6 = (bf16[192,2688]{1,0:T(8,128)(2,1)}, bf16[192,2688]{1,0:T(8,128)(2,1)S(1)}, u32[]{:S(2)}, u32[]{:S(2)}) collective-permute-start(bf16[192,2688]{1,0:T(8,128)(2,1)} %level.8.refs_0_.own_ref), channel_id=1, source_target_pairs={{0,1},{1,0},{2,3},{3,2},{4,5},{5,4},{6,7},{7,6},{8,9},{9,8},{10,11... | collective-permute-start | bytes 3096584 | tf_op jit(solution)/shard_map/ppermute | solution.py:539
  70.7 68.8 %collective-permute-start.5 = (bf16[192,2688]{1,0:T(8,128)(2,1)}, bf16[192,2688]{1,0:T(8,128)(2,1)S(1)}, u32[]{:S(2)}, u32[]{:S(2)}) collective-permute-start(bf16[192,2688]{1,0:T(8,128)(2,1)} %level.9.refs_14_.refs_0_.own_ref), channel_id=1, source_target_pairs={{0,2},{1,3},{2,0},{3,1},{4,6},{5,7},{6,4},{7,5},{8,10},{9,11},{10,... | collective-permute-start | bytes 3096584 | tf_op jit(solution)/shard_map/ppermute | solution.py:539
  89.2 55.9 %collective-permute-start.4 = (bf16[144,2688]{1,0:T(8,128)(2,1)}, bf16[144,2688]{1,0:T(8,128)(2,1)}, u32[]{:S(2)}, u32[]{:S(2)}) collective-permute-start(bf16[144,2688]{1,0:T(8,128)(2,1)} %decode.7.refs_0_.own_ref), channel_id=1, source_target_pairs={{0,1},{1,0},{2,3},{3,2},{4,5},{5,4},{6,7},{7,6},{8,9},{9,8},{10,11... | collective-permute-start | bytes 2322440 | tf_op jit(solution)/shard_map/ppermute | solution.py:539
  104.3 62.1 %collective-permute-start.10 = (bf16[144,2688]{1,0:T(8,128)(2,1)}, bf16[144,2688]{1,0:T(8,128)(2,1)}, u32[]{:S(2)}, u32[]{:S(2)}) collective-permute-start(bf16[144,2688]{1,0:T(8,128)(2,1)} %level.10.refs_0_.own_ref), channel_id=1, source_target_pairs={{0,1},{1,0},{2,3},{3,2},{4,5},{5,4},{6,7},{7,6},{8,9},{9,8},{10,11... | collective-permute-start | bytes 2322440 | tf_op jit(solution)/shard_map/ppermute | solution.py:539
  112.7 1.0 copy-start.6
  116.0 50.4 %collective-permute-start.8 = (bf16[192,2688]{1,0:T(8,128)(2,1)}, bf16[192,2688]{1,0:T(8,128)(2,1)S(1)}, u32[]{:S(2)}, u32[]{:S(2)}) collective-permute-start(bf16[192,2688]{1,0:T(8,128)(2,1)} %level.11.refs_0_.refs_6_), channel_id=1, source_target_pairs={{0,16},{16,0},{1,17},{17,1},{2,18},{18,2},{3,19},{19,3},{4,20},{20... | collective-permute-start | bytes 3096584 | tf_op jit(solution)/shard_map/ppermute | solution.py:539
  139.5 1.0 copy-start.7
  142.8 30.1 %collective-permute-start.9 = (bf16[192,2688]{1,0:T(8,128)(2,1)}, bf16[192,2688]{1,0:T(8,128)(2,1)S(1)}, u32[]{:S(2)}, u32[]{:S(2)}) collective-permute-start(bf16[192,2688]{1,0:T(8,128)(2,1)} %level.12.refs_0_.refs_8_), channel_id=1, source_target_pairs={{0,16},{16,0},{1,17},{17,1},{2,18},{18,2},{3,19},{19,3},{4,20},{20... | collective-permute-start | bytes 3096584 | tf_op jit(solution)/shard_map/ppermute | solution.py:539
  145.0 73.2 %reduce-scatter.4.cloned.1.call-start = ((), (), s32[]{:S(2)}) async-start(), calls=%async_computation.4 | async-start | bytes 983040 | tf_op jit(solution)/shard_map/reduce_scatter | solution.py:610
  148.2 39.3 %collective-permute-start.12 = (bf16[144,2688]{1,0:T(8,128)(2,1)}, bf16[144,2688]{1,0:T(8,128)(2,1)S(1)}, u32[]{:S(2)}, u32[]{:S(2)}) collective-permute-start(bf16[144,2688]{1,0:T(8,128)(2,1)} %level.13.refs_14_.own_ref), channel_id=1, source_target_pairs={{0,2},{1,3},{2,0},{3,1},{4,6},{5,7},{6,4},{7,5},{8,10},{9,11},{10,... | collective-permute-start | bytes 2322440 | tf_op jit(solution)/shard_map/ppermute | solution.py:539
  166.4 1.0 copy-start.4
  170.6 18.9 %collective-permute-start.13 = (bf16[144,2688]{1,0:T(8,128)(2,1)}, bf16[144,2688]{1,0:T(8,128)(2,1)S(1)}, u32[]{:S(2)}, u32[]{:S(2)}) collective-permute-start(bf16[144,2688]{1,0:T(8,128)(2,1)} %level.14.refs_10_.refs_0_), channel_id=1, source_target_pairs={{0,16},{16,0},{1,17},{17,1},{2,18},{18,2},{3,19},{19,3},{4,20},{20... | collective-permute-start | bytes 2322440 | tf_op jit(solution)/shard_map/ppermute | solution.py:539
  172.9 1.0 copy-start.5
  187.5 2.0 copy-start.10
  189.5 0.9 copy-start.8
  193.5 1.1 copy-start.2
  193.6 9.4 %collective-permute-start.14 = (bf16[512,5376]{1,0:T(8,128)(2,1)}, bf16[512,5376]{1,0:T(8,128)(2,1)}, u32[]{:S(2)}, u32[]{:S(2)}) collective-permute-start(bf16[512,5376]{1,0:T(8,128)(2,1)} %gate.4.refs_1_.refs_3_), channel_id=1, source_target_pairs={{0,4},{4,0},{8,12},{12,8},{1,5},{5,1},{9,13},{13,9},{2,6},{6,2},{1... | collective-permute-start | bytes 16515080 | tf_op jit(solution)/shard_map/ppermute | solution.py:539
  193.7 49.3 %reduce-scatter.6.cloned.1.call-start = ((), (), s32[]{:S(2)}) async-start(), calls=%async_computation.6 | async-start | bytes 983040 | tf_op jit(solution)/shard_map/reduce_scatter | solution.py:610
  194.7 22.3 %collective-permute-start.15 = (bf16[144,2688]{1,0:T(8,128)(2,1)S(1)}, bf16[144,2688]{1,0:T(8,128)(2,1)S(1)}, u32[]{:S(2)}, u32[]{:S(2)}) collective-permute-start(bf16[144,2688]{1,0:T(8,128)(2,1)S(1)} %copy-done.2), channel_id=1, source_target_pairs={{0,16},{16,0},{1,17},{17,1},{2,18},{18,2},{3,19},{19,3},{4,20},{20... | collective-permute-start | bytes 2322440 | tf_op jit(solution)/shard_map/ppermute | solution.py:539
  217.0 56.7 %reduce-scatter.8.cloned.1.call-start = ((), (), s32[]{:S(2)}) async-start(), calls=%async_computation.7 | async-start | bytes 1474560 | tf_op jit(solution)/shard_map/reduce_scatter | solution.py:610
  217.0 1.2 copy-start.9
  236.8 6.2 %copy-start.3 = (bf16[1,384,256]{2,1,0:T(8,128)(2,1)S(1)}, bf16[1,384,256]{2,1,0:T(8,128)(2,1)}, u32[]{:S(2)}) copy-start(bf16[1,384,256]{2,1,0:T(8,128)(2,1)} %reduce-scatter.4.cloned.1.call-done) | copy-start | bytes 589828
  243.0 0.9 copy-start.1
  243.0 2.4 collective-permute-start.16
  243.9 4.8 %collective-permute-start.18 = (bf16[384,128]{1,0:T(8,128)(2,1)S(1)}, bf16[384,128]{1,0:T(8,128)(2,1)S(1)}, u32[]{:S(2)}, u32[]{:S(2)}) collective-permute-start(bf16[384,128]{1,0:T(8,128)(2,1)S(1)} %get-tuple-element.12), channel_id=1, source_target_pairs={{0,8},{4,12},{8,0},{12,4},{1,9},{5,13},{9,1},{13,5},{2,10},{6,14},... | collective-permute-start | bytes 294920 | tf_op jit(solution)/shard_map/ppermute | solution.py:539
  245.5 5.2 %collective-permute-start.20 = (bf16[384,128]{1,0:T(8,128)(2,1)S(1)}, bf16[384,128]{1,0:T(8,128)(2,1)S(1)}, u32[]{:S(2)}, u32[]{:S(2)}) collective-permute-start(bf16[384,128]{1,0:T(8,128)(2,1)S(1)} %get-tuple-element.13), channel_id=1, source_target_pairs={{0,12},{4,8},{8,4},{12,0},{1,13},{5,9},{9,5},{13,1},{2,14},{6,10},... | collective-permute-start | bytes 294920 | tf_op jit(solution)/shard_map/ppermute | solution.py:539
  274.6 2.7 collective-permute-start.17
  275.5 4.9 %collective-permute-start.19 = (bf16[288,128]{1,0:T(8,128)(2,1)S(1)}, bf16[288,128]{1,0:T(8,128)(2,1)S(1)}, u32[]{:S(2)}, u32[]{:S(2)}) collective-permute-start(bf16[288,128]{1,0:T(8,128)(2,1)S(1)} %get-tuple-element.9), channel_id=1, source_target_pairs={{0,8},{4,12},{8,0},{12,4},{1,9},{5,13},{9,1},{13,5},{2,10},{6,14},... | collective-permute-start | bytes 221192 | tf_op jit(solution)/shard_map/ppermute | solution.py:539
  277.0 4.6 %collective-permute-start.21 = (bf16[288,128]{1,0:T(8,128)(2,1)S(1)}, bf16[288,128]{1,0:T(8,128)(2,1)S(1)}, u32[]{:S(2)}, u32[]{:S(2)}) collective-permute-start(bf16[288,128]{1,0:T(8,128)(2,1)S(1)} %get-tuple-element.8), channel_id=1, source_target_pairs={{0,12},{4,8},{8,4},{12,0},{1,13},{5,9},{9,5},{13,1},{2,14},{6,10},... | collective-permute-start | bytes 221192 | tf_op jit(solution)/shard_map/ppermute | solution.py:539
Sparse Core Ops, SparseCore 0:
  9.2 37.1 all-gather.2
  145.2 43.8 all-gather.4
  193.8 24.4 reduce-scatter.3
  220.4 22.5 reduce-scatter.5
  245.1 28.4 reduce-scatter.7

commit v3 on v2

--- a/solution.py
+++ b/solution.py
@@ -342,10 +342,11 @@
     )(value, *earlier)
 
 
-def project_kernel(chunks, count, place_ref, *refs):
-    row_refs, attn_refs, out_side = refs[:count], refs[count : 2 * count], refs[2 * count]
+def project_kernel(chunks, flips, place_ref, *refs):
+    count = len(flips)
+    row_refs, attn_refs, side_ref = refs[:count], refs[count : 2 * count], refs[2 * count]
     weights = refs[2 * count + 1 : 2 * count + 1 + 2 * len(chunks)]
-    out_ref, total = refs[-2:]
+    out_ref, total, attn, out_side, arrived = refs[-5:]
     step = pl.program_id(0)
     steps = pl.num_programs(0)
     rows = row_refs[0].shape[0]
@@ -359,11 +360,20 @@
             value = lax.dot_general(part, ref[...], NT, preferred_element_type=jnp.float32)
             total[:, lanes] = value if first else total[:, lanes] + value
 
+    def fetches():
+        yield pltpu.make_async_copy(side_ref, out_side, arrived.at[count])
+        for place, flip in enumerate(flips):
+            block = 0 if flip is None else place_ref[1] ^ flip
+            source = attn_refs[place].at[pl.ds(pl.multiple_of(block * rows, rows), rows), :]
+            yield pltpu.make_async_copy(source, attn.at[place], arrived.at[place])
+
     @pl.when(step == 0)
     def _():
-        add([out_side[first : first + size, :] for first, size in chunks], attn_refs, True)
-
-    @pl.when(step < steps // 2)
+        for fetch in fetches():
+            fetch.start()
+        add([ref[...] for ref in weights[0::2]], row_refs, True)
+
+    @pl.when((step > 0) & (step < steps // 2))
     def _():
         add([ref[...] for ref in weights[0::2]], row_refs, False)
 
@@ -373,6 +383,10 @@
 
     @pl.when(step == steps - 1)
     def _():
+        for fetch in fetches():
+            fetch.wait()
+        side = [out_side[first : first + size, :] for first, size in chunks]
+        add(side, [attn.at[place] for place in range(count)], False)
         for shard in range(shards):
             for place in range(count):
                 first = place * rows + shard * kept
@@ -396,24 +410,23 @@
         ]
     row_spec = pl.BlockSpec((rows, depth), lambda i, h: (0, lax.rem(i + h[0] * (last + 1), steps)))
 
-    def attn_spec(part, flip):
-        return pl.BlockSpec(
-            (rows, part.shape[1]), lambda i, h: (0 if flip is None else h[1] ^ flip, 0)
-        )
-
     shape = (shards, columns, count * rows // shards)
     return pl.pallas_call(
-        lambda *refs: project_kernel(chunks, count, *refs),
+        lambda *refs: project_kernel(chunks, [flip for _, flip in attn_parts], *refs),
         grid_spec=pltpu.PrefetchScalarGridSpec(
             num_scalar_prefetch=1,
             grid=(steps,),
             in_specs=[row_spec] * count
-            + [attn_spec(*part) for part in attn_parts]
-            + [pl.BlockSpec(out_side.shape, lambda i, h: (0, 0))]
+            + [ANYWHERE] * (count + 1)
             + weight_specs
             + [ANYWHERE] * len(earlier),
             out_specs=pl.BlockSpec(shape, lambda i, h: (0, 0, 0)),
-            scratch_shapes=[pltpu.VMEM((columns, count * rows), jnp.float32)],
+            scratch_shapes=[
+                pltpu.VMEM((columns, count * rows), jnp.float32),
+                pltpu.VMEM((count, rows, out_side.shape[1]), jnp.bfloat16),
+                pltpu.VMEM(out_side.shape, jnp.bfloat16),
+                pltpu.SemaphoreType.DMA((count + 1,)),
+            ],
         ),
         out_shape=jax.ShapeDtypeStruct(shape, jnp.bfloat16),
         compiler_params=pltpu.CompilerParams(vmem_limit_bytes=56 << 20),
@@ -592,11 +605,11 @@
     piece_b = level_step(piece_b, 2, (piece_c, own_rows[1]))
     piece_a = level_step(piece_a, 1, (piece_b,))
     across_a = flipped(piece_a, "group", 1)
-    piece_c = level_step(piece_c, 2, (piece_a,))
+    near_attended = attended_by(1, near_queries, (piece_a,), 0)
+    piece_c = level_step(piece_c, 2, (near_attended,))
     across_c = flipped(piece_c, "group", 1)
     piece_d = level_step(late_d, 1, (piece_c,))
-    near_attended = attended_by(1, near_queries, (piece_d,), 0)
-    piece_b = level_step(piece_b, 1, (near_attended, across_a))
+    piece_b = level_step(piece_b, 1, (piece_d, across_a))
     across_b = flipped(piece_b, "group", 1)
     place = jnp.stack([half_id[0], seq_index])
     own_attn = [(attended, None), (near_attended, None)]

time: 291 us -> 296 us (1.017); the launches traced: 290 us -> 290 us
  waiting for transfers between devices: 87.2 us -> 91.9 us
  Pallas kernels: 134 us -> 130 us
    pallas_call x3, Pallas kernels: 46.2 us -> 41.4 us  [project(): pl.pallas_call(lambda *refs: project_kernel(chunks, [flip for _, flip in...]
    reduce_scatter x3, waiting for transfers between devices: 30.4 us -> 33.8 us  [reduced(): lax.psum_scatter(partial, 'tp', scatter_dimension=0, tiled=True)[0]]
  transfers between devices with their start and end apart: 27 -> 27, of which waited for: 14 -> 14; matrix products, arithmetic and copies ran while one was open for 5% -> 5% of each run, Pallas kernels for 46% -> 45%
where the time goes in v3:
time: 296 us; the launch traced here: 290 us
  Pallas kernels  130 us (44%)
  waiting for transfers between devices  91.9 us (31%)
  starting transfers between devices  25.3 us (9%)
  between operations  16.2 us (5%)
  local copies, waits for them, and re-layouts  15.2 us (5%)
  other arithmetic  11.7 us (4%)
    ppermute x22, waiting for transfers between devices, flipped(): lax.ppermute(value, axis, [(i, i ^ bit) for i in range(lax.axis_size(axis...  58 us
    pallas_call x3, Pallas kernels, project(): pl.pallas_call(lambda *refs: project_kernel(chunks, [flip for _, flip in...  41.4 us
    reduce_scatter x3, waiting for transfers between devices, reduced(): lax.psum_scatter(partial, 'tp', scatter_dimension=0, tiled=True)[0]  33.8 us
    pallas_call x2, Pallas kernels, attend(): pl.pallas_call(attend_kernel, grid_spec=pltpu.PrefetchScalarGridSpec(num_...  28.1 us
    ppermute x22, starting transfers between devices, flipped(): lax.ppermute(value, axis, [(i, i ^ bit) for i in range(lax.axis_size(axis...  25.1 us
    pallas_call x2, Pallas kernels, mix_hidden(): pl.pallas_call(mix_kernel, grid=(rows // step,), in_specs=[pl.BlockSpec((...  23 us
    pallas_call x8, Pallas kernels, level_step(): pl.pallas_call(level_kernel, grid_spec=pltpu.PrefetchScalarGridSpec(num_s...  22 us
    pallas_call x4, Pallas kernels, dequant(): pl.pallas_call(lambda *refs: dequant_kernel(first, *refs), grid_spec=pltp...  14.8 us
  transfers between devices with their start and end apart: 27, of which 14 were waited for; matrix products, arithmetic and copies ran while one was open for 5% of the time, Pallas kernels for 45%

profile of v3, /device:TPU:0, one launch (start us, length us, event | category | flops | bytes accessed | tf_op | source)
XLA Modules:
  0.0 290.1 jit_solution(7310799162213096480)
XLA Ops:
  6.5 2.5 copy.19
  9.6 2.9 %decode.4.refs_4_.own_ref = bf16[192,2688]{1,0:T(8,128)(2,1)} custom-call(s32[1]{0:T(128)} %bitcast.refs_0_, s32[672,5376]{1,0:T(8,128)} %bitcast.17, s32[42,672]{1,0:T(8,128)} %refs_2_.7, bf16[42,5376]{1,0:T(8,128)(2,1)} %constant.46.clone.refs_3_), custom_call_target="tpu_custom_call" | custom-call | flops 3450000128 | bytes 1 | tf_op jit(solution)/shard_map/decode/pallas_call | solution.py:283
  12.5 3.6 %collective-permute-start.3 = (bf16[192,2688]{1,0:T(8,128)(2,1)}, bf16[192,2688]{1,0:T(8,128)(2,1)}, u32[]{:S(2)}, u32[]{:S(2)}) collective-permute-start(bf16[192,2688]{1,0:T(8,128)(2,1)} %decode.4.refs_4_.own_ref), channel_id=1, source_target_pairs={{0,2},{1,3},{2,0},{3,1},{4,6},{5,7},{6,4},{7,5},{8,10},{9,11},{10,... | collective-permute-start | bytes 3096584 | tf_op jit(solution)/shard_map/ppermute | solution.py:552
  16.1 4.4 %decode.5.refs_4_.own_ref = bf16[192,2688]{1,0:T(8,128)(2,1)} custom-call(s32[1]{0:T(128)} %bitcast.refs_0_, s32[672,5376]{1,0:T(8,128)} %bitcast.18, s32[42,672]{1,0:T(8,128)} %refs_2_.7, bf16[42,5376]{1,0:T(8,128)(2,1)} %constant.46.clone.refs_3_, bf16[192,2688]{1,0:T(8,128)(2,1)} %decode.4.refs_4_.own_ref, bf16[512,1024]{1,0:T(8,128)(2,1)} %bitcast.22), custom_call_target="tpu_custom_call" | custom-call | flops 3450000128 | bytes 1 | tf_op jit(solution)/shard_map/decode/pallas_call | solution.py:283
  20.5 1.6 collective-permute-start.2
  22.7 2.1 copy.20
  26.0 3.7 %decode.6.refs_0_.refs_1_.own_ref = bf16[144,2688]{1,0:T(8,128)(2,1)} custom-call(s32[1]{0:T(128)} %bitcast.refs_0_, s32[672,5376]{1,0:T(8,128)} %bitcast.19, s32[42,672]{1,0:T(8,128)} %refs_2_.7, bf16[42,5376]{1,0:T(8,128)(2,1)} %constant.46.clone.refs_3_, bf16[192,2688]{1,0:T(8,128)(2,1)} %decode.5.refs_4_.own_ref, bf16[512,1024]{1,0:T(8,128)(2,1)} %copy-done), custom_call_target="tpu_custom_call" | custom-call | flops 3450000128 | bytes 1 | tf_op jit(solution)/shard_map/decode/pallas_call | solution.py:283
  32.7 11.5 %mix.2.refs_0_.refs_1_ = bf16[512,5376]{1,0:T(8,128)(2,1)} custom-call(bf16[512,5376]{1,0:T(8,128)(2,1)} %hidden_ref.1, bf16[864,768]{1,0:T(8,128)(2,1)} %constant.47.clone.table_ref, bf16[144,2688]{1,0:T(8,128)(2,1)} %decode.6.refs_0_.refs_1_.own_ref), custom_call_target="tpu_custom_call" | custom-call | flops 18400000000 | bytes 1 | tf_op jit(solution)/shard_map/mix/pallas_call | solution.py:247
  44.2 1.6 collective-permute-start.11
  46.3 4.4 %fusion.refs_1_.refs_6_.refs_7_.refs_12_.refs_13_ = bf16[1024,1024]{1,0:T(8,128)(2,1)} fusion(s32[]{:T(128)S(6)} %select_n.64, bf16[1024,1024]{1,0:T(8,128)(2,1)S(1)} %bitcast.23), kind=kLoop, calls=%fused_computation.2 | loop fusion | flops 4194304 | bytes 4194308 | tf_op jit(solution)/shard_map/concatenate | solution.py:589
  50.8 3.7 %fusion.1 = (f32[2048,64]{1,0:T(8,128)S(1)}, f32[2048,64]{1,0:T(8,128)S(1)}, f32[2048,64]{1,0:T(8,128)S(1)}) fusion(f32[64]{0:T(128)S(1)} %multiply_power_fusion, f32[2048]{0:T(1024)S(1)} %add_convert_fusion), kind=kLoop, calls=%fused_computation.8 | loop fusion | flops 262144 | bytes 1581312 | tf_op jit(solution)/shard_map/neg | solution.py:587
  54.5 1.9 pad_maximum_fusion
  56.4 5.9 %collective-permute-done.3.partner_ref = bf16[192,2688]{1,0:T(8,128)(2,1)} collective-permute-done((bf16[192,2688]{1,0:T(8,128)(2,1)}, bf16[192,2688]{1,0:T(8,128)(2,1)}, u32[]{:S(2)}, u32[]{:S(2)}) %collective-permute-start.3) | collective-permute-done | bytes 1032224 | tf_op jit(solution)/shard_map/ppermute | solution.py:552
  62.3 2.4 level.8.refs_0_.own_ref
  65.4 3.0 %collective-permute-done.2.partner_ref = bf16[192,2688]{1,0:T(8,128)(2,1)} collective-permute-done((bf16[192,2688]{1,0:T(8,128)(2,1)}, bf16[192,2688]{1,0:T(8,128)(2,1)}, u32[]{:S(2)}, u32[]{:S(2)}) %collective-permute-start.2) | collective-permute-done | bytes 1032224 | tf_op jit(solution)/shard_map/ppermute | solution.py:552
  68.4 2.4 level.9.refs_14_.refs_0_.own_ref
  71.4 14.1 %attend.2.refs_4_.refs_3_.refs_5_ = bf16[512,1024]{1,0:T(8,128)(2,1)} custom-call(s32[1]{0:T(128)} %bitcast.1.place_ref, bf16[512,1024]{1,0:T(8,128)(2,1)} %query_ref.1, f32[2048,128]{1,0:T(8,128)} %get-tuple-element.29.refs_2_.cosine_ref.refs_4_.refs_10_, f32[2048,128]{1,0:T(8,128)} %get-tuple-element.30.refs_3_.sine_ref.refs_5_.refs_11_, ...), custom_call_target="tpu_custom_call" | custom-call | flops 14949999616 | bytes 1 | tf_op jit(solution)/shard_map/attend/pallas_call | solution.py:536
  85.4 3.8 %decode.7.refs_0_.own_ref = bf16[144,2688]{1,0:T(8,128)(2,1)} custom-call(s32[1]{0:T(128)} %bitcast.refs_0_, s32[672,5376]{1,0:T(8,128)} %bitcast.20, s32[42,672]{1,0:T(8,128)} %refs_2_.7, bf16[42,5376]{1,0:T(8,128)(2,1)} %constant.46.clone.refs_3_, bf16[512,1024]{1,0:T(8,128)(2,1)} %attend.2.refs_4_.refs_3_.refs_5_), custom_call_target="tpu_custom_call" | custom-call | flops 3450000128 | bytes 1 | tf_op jit(solution)/shard_map/decode/pallas_call | solution.py:283
  89.9 11.5 %mix.3.refs_1_.refs_2_ = bf16[512,5376]{1,0:T(8,128)(2,1)} custom-call(bf16[512,5376]{1,0:T(8,128)(2,1)} %collective-permute-done.1.hidden_ref, bf16[864,768]{1,0:T(8,128)(2,1)} %constant.47.clone.table_ref, bf16[144,2688]{1,0:T(8,128)(2,1)} %decode.7.refs_0_.own_ref), custom_call_target="tpu_custom_call" | custom-call | flops 18400000000 | bytes 1 | tf_op jit(solution)/shard_map/mix/pallas_call | solution.py:247
  101.4 3.1 %level.10.refs_0_.own_ref = bf16[144,2688]{1,0:T(8,128)(2,1)} custom-call(s32[1]{0:T(128)} %bitcast.5.sign_ref, bf16[144,2688]{1,0:T(8,128)(2,1)} %decode.6.refs_0_.refs_1_.own_ref, bf16[144,2688]{1,0:T(8,128)(2,1)} %collective-permute-done.5.partner_ref, bf16[192,2688]{1,0:T(8,128)(2,1)} %level.9.refs_14_.refs_0_.own_ref, bf16[512,5376]{1,0:T(8,128)(2,1)} %mix.3.refs_1_.refs_2_), custom_call_target="tpu_custom_call" | custom-call | flops 3450000128 | bytes 1 | tf_op jit(solution)/shard_map/level/pallas_call | solution.py:315
  104.5 1.3 collective-permute-start.9
  105.9 6.8 %collective-permute-done.4.partner_ref = bf16[192,2688]{1,0:T(8,128)(2,1)S(1)} collective-permute-done((bf16[192,2688]{1,0:T(8,128)(2,1)}, bf16[192,2688]{1,0:T(8,128)(2,1)S(1)}, u32[]{:S(2)}, u32[]{:S(2)}) %collective-permute-start.4) | collective-permute-done | bytes 1032224 | tf_op jit(solution)/shard_map/ppermute | solution.py:552
  113.7 2.3 level.11.refs_14_.refs_6_
  116.0 1.8 collective-permute-start.6
  117.8 14.0 %attend.3.refs_0_.refs_4_.refs_6_ = bf16[512,1024]{1,0:T(8,128)(2,1)} custom-call(s32[1]{0:T(128)} %bitcast.6.place_ref, bf16[512,1024]{1,0:T(8,128)(2,1)} %copy-done, f32[2048,128]{1,0:T(8,128)} %get-tuple-element.29.refs_2_.cosine_ref.refs_4_.refs_10_, f32[2048,128]{1,0:T(8,128)} %get-tuple-element.30.refs_3_.sine_ref.refs_5_.refs_11_, ...), custom_call_target="tpu_custom_call" | custom-call | flops 1 | bytes 1 | tf_op jit(solution)/shard_map/attend/pallas_call | solution.py:536
  131.8 7.7 %collective-permute-done.7.partner_ref = bf16[192,2688]{1,0:T(8,128)(2,1)S(1)} collective-permute-done((bf16[192,2688]{1,0:T(8,128)(2,1)}, bf16[192,2688]{1,0:T(8,128)(2,1)S(1)}, u32[]{:S(2)}, u32[]{:S(2)}) %collective-permute-start.7) | collective-permute-done | bytes 1032224 | tf_op jit(solution)/shard_map/ppermute | solution.py:552
  140.5 2.4 level.12.refs_0_.refs_8_
  142.8 1.5 collective-permute-start.8
  145.1 3.1 %level.13.refs_0_.own_ref = bf16[144,2688]{1,0:T(8,128)(2,1)} custom-call(s32[1]{0:T(128)} %bitcast.4.sign_ref, bf16[144,2688]{1,0:T(8,128)(2,1)} %decode.7.refs_0_.own_ref, bf16[144,2688]{1,0:T(8,128)(2,1)} %collective-permute-done.10.partner_ref, bf16[192,2688]{1,0:T(8,128)(2,1)} %level.12.refs_0_.refs_8_), custom_call_target="tpu_custom_call" | custom-call | flops 3450000128 | bytes 1 | tf_op jit(solution)/shard_map/level/pallas_call | solution.py:315
  148.2 2.6 collective-permute-start.12
  150.8 15.7 %collective-permute-done.9.partner_ref = bf16[144,2688]{1,0:T(8,128)(2,1)} collective-permute-done((bf16[144,2688]{1,0:T(8,128)(2,1)}, bf16[144,2688]{1,0:T(8,128)(2,1)}, u32[]{:S(2)}, u32[]{:S(2)}) %collective-permute-start.9) | collective-permute-done | bytes 774176 | tf_op jit(solution)/shard_map/ppermute | solution.py:552
  167.5 3.2 %level.14.refs_10_.refs_0_ = bf16[144,2688]{1,0:T(8,128)(2,1)} custom-call(s32[1]{0:T(128)} %bitcast.4.sign_ref, bf16[144,2688]{1,0:T(8,128)(2,1)} %level.10.refs_0_.own_ref, bf16[144,2688]{1,0:T(8,128)(2,1)} %collective-permute-done.9.partner_ref, bf16[144,2688]{1,0:T(8,128)(2,1)} %level.13.refs_0_.own_ref, bf16[192,2688]{1,0:T(8,128)(2,1)} %copy-done.4), custom_call_target="tpu_custom_call" | custom-call | flops 3450000128 | bytes 1 | tf_op jit(solution)/shard_map/level/pallas_call | solution.py:315
  170.7 2.3 collective-permute-start.13
  174.0 12.3 %project.3.refs_1_ = bf16[4,384,256]{2,1,0:T(8,128)(2,1)} custom-call(s32[2]{0:T(128)} %pad_add_fusion.refs_0_, bf16[512,5376]{1,0:T(8,128)(2,1)} %mix.2.refs_0_.refs_1_, bf16[512,5376]{1,0:T(8,128)(2,1)} %mix.3.refs_1_.refs_2_, bf16[512,1024]{1,0:T(8,128)(2,1)} %attend.2.refs_4_.refs_3_.refs_5_, bf16[512,1024]{1,0:T(8,128)(2,1)} %attend.3.refs_0_.refs_4_.refs_6_, ...), custom_call_target="tpu_custom_call" | custom-call | flops 11500000256 | bytes 1 | tf_op jit(solution)/shard_map/project/pallas_call | solution.py:414
  186.3 3.2 %collective-permute-done.13.refs_2_.refs_11_ = bf16[144,2688]{1,0:T(8,128)(2,1)S(1)} collective-permute-done((bf16[144,2688]{1,0:T(8,128)(2,1)}, bf16[144,2688]{1,0:T(8,128)(2,1)S(1)}, u32[]{:S(2)}, u32[]{:S(2)}) %collective-permute-start.13) | collective-permute-done | bytes 774176 | tf_op jit(solution)/shard_map/ppermute | solution.py:552
  190.5 3.1 %level.15.refs_1_.refs_10_.refs_12_ = bf16[144,2688]{1,0:T(8,128)(2,1)} custom-call(s32[1]{0:T(128)} %bitcast.5.sign_ref, bf16[144,2688]{1,0:T(8,128)(2,1)} %level.13.refs_0_.own_ref, bf16[144,2688]{1,0:T(8,128)(2,1)} %copy-done.10, bf16[144,2688]{1,0:T(8,128)(2,1)} %level.14.refs_10_.refs_0_, bf16[4,384,256]{2,1,0:T(8,128)(2,1)} %project.3.refs_1_, ...), custom_call_target="tpu_custom_call" | custom-call | flops 3450000128 | bytes 1 | tf_op jit(solution)/shard_map/level/pallas_call | solution.py:315
  194.7 1.7 collective-permute-start.15
  196.5 6.6 %collective-permute-done.14.refs_2_.refs_4_ = bf16[512,5376]{1,0:T(8,128)(2,1)} collective-permute-done((bf16[512,5376]{1,0:T(8,128)(2,1)}, bf16[512,5376]{1,0:T(8,128)(2,1)}, u32[]{:S(2)}, u32[]{:S(2)}) %collective-permute-start.14) | collective-permute-done | bytes 5505056 | tf_op jit(solution)/shard_map/ppermute | solution.py:552
  203.1 12.6 %project.4.refs_14_ = bf16[4,384,256]{2,1,0:T(8,128)(2,1)} custom-call(s32[2]{0:T(128)} %pad_add_fusion.refs_0_, bf16[512,5376]{1,0:T(8,128)(2,1)} %gate.4.refs_1_.refs_3_, bf16[512,5376]{1,0:T(8,128)(2,1)} %collective-permute-done.14.refs_2_.refs_4_, bf16[2048,1024]{1,0:T(8,128)(2,1)} %all-gather.5.cloned.1.call-done.refs_3_.refs_4_.refs_7_.refs_8_, ...), custom_call_target="tpu_custom_call" | custom-call | flops 11500000256 | bytes 1 | tf_op jit(solution)/shard_map/project/pallas_call | solution.py:414
  215.8 2.5 reduce-scatter.4.cloned.1.call-done
  218.3 16.5 %project.5.refs_0_ = bf16[4,288,512]{2,1,0:T(8,128)(2,1)} custom-call(s32[2]{0:T(128)} %pad_add_fusion.refs_0_, bf16[512,5376]{1,0:T(8,128)(2,1)} %mix.2.refs_0_.refs_1_, bf16[512,5376]{1,0:T(8,128)(2,1)} %mix.3.refs_1_.refs_2_, bf16[512,5376]{1,0:T(8,128)(2,1)} %gate.4.refs_1_.refs_3_, bf16[512,5376]{1,0:T(8,128)(2,1)} %collective-permute-done.14.refs_2_.refs_4_, ...), custom_call_target="tpu_custom_call" | custom-call | flops 11500000256 | bytes 1 | tf_op jit(solution)/shard_map/project/pallas_call | solution.py:414
  234.8 8.1 %reduce-scatter.6.cloned.1.call-done = bf16[1,384,256]{2,1,0:T(8,128)(2,1)} async-done(((bf16[4,384,256]{2,1,0:T(8,128)(2,1)}), bf16[1,384,256]{2,1,0:T(8,128)(2,1)}) %reduce-scatter.6.cloned.1.call-update) | async-done | bytes 196624 | tf_op jit(solution)/shard_map/reduce_scatter | solution.py:623
  243.9 1.5 collective-permute-start.18
  245.6 3.0 %collective-permute-done.18 = bf16[384,128]{1,0:T(8,128)(2,1)S(1)} collective-permute-done((bf16[384,128]{1,0:T(8,128)(2,1)S(1)}, bf16[384,128]{1,0:T(8,128)(2,1)S(1)}, u32[]{:S(2)}, u32[]{:S(2)}) %collective-permute-start.18) | collective-permute-done | bytes 98336 | tf_op jit(solution)/shard_map/ppermute | solution.py:552
  248.6 1.9 collective-permute-done.20
  250.6 23.1 %reduce-scatter.8.cloned.1.call-done = bf16[1,288,512]{2,1,0:T(8,128)(2,1)} async-done(((bf16[4,288,512]{2,1,0:T(8,128)(2,1)}), bf16[1,288,512]{2,1,0:T(8,128)(2,1)}) %reduce-scatter.8.cloned.1.call-update) | async-done | bytes 294928 | tf_op jit(solution)/shard_map/reduce_scatter | solution.py:623
  275.6 1.5 collective-permute-start.19
  277.4 3.0 %collective-permute-done.19 = bf16[288,128]{1,0:T(8,128)(2,1)S(1)} collective-permute-done((bf16[288,128]{1,0:T(8,128)(2,1)S(1)}, bf16[288,128]{1,0:T(8,128)(2,1)S(1)}, u32[]{:S(2)}, u32[]{:S(2)}) %collective-permute-start.19) | collective-permute-done | bytes 73760 | tf_op jit(solution)/shard_map/ppermute | solution.py:552
  (80 shorter events, 18.3 us)
Async XLA Ops:
  6.5 64.8 %all-gather.3.cloned.1.call-start = ((), (), s32[]{:S(2)}) async-start(), calls=%async_computation.3 | async-start | bytes 5242880 | tf_op jit(solution)/shard_map/all_gather | solution.py:565
  9.0 187.5 %all-gather.5.cloned.1.call-start = ((), (), s32[]{:S(2)}) async-start(), calls=%async_computation.5 | async-start | bytes 5242880 | tf_op jit(solution)/shard_map/all_gather | solution.py:602
  9.1 15.8 %collective-permute-start = (bf16[512,1024]{1,0:T(8,128)(2,1)}, bf16[512,1024]{1,0:T(8,128)(2,1)S(1)}, u32[]{:S(2)}, u32[]{:S(2)}) collective-permute-start(bf16[512,1024]{1,0:T(8,128)(2,1)} %query_ref.1), channel_id=1, source_target_pairs={{0,4},{4,0},{8,12},{12,8},{1,5},{5,1},{9,13},{13,9},{2,6},{6,2},{1... | collective-permute-start | bytes 3145736 | tf_op jit(solution)/shard_map/ppermute | solution.py:552
  12.5 49.8 %collective-permute-start.3 = (bf16[192,2688]{1,0:T(8,128)(2,1)}, bf16[192,2688]{1,0:T(8,128)(2,1)}, u32[]{:S(2)}, u32[]{:S(2)}) collective-permute-start(bf16[192,2688]{1,0:T(8,128)(2,1)} %decode.4.refs_4_.own_ref), channel_id=1, source_target_pairs={{0,2},{1,3},{2,0},{3,1},{4,6},{5,7},{6,4},{7,5},{8,10},{9,11},{10,... | collective-permute-start | bytes 3096584 | tf_op jit(solution)/shard_map/ppermute | solution.py:552
  20.5 47.9 %collective-permute-start.2 = (bf16[192,2688]{1,0:T(8,128)(2,1)}, bf16[192,2688]{1,0:T(8,128)(2,1)}, u32[]{:S(2)}, u32[]{:S(2)}) collective-permute-start(bf16[192,2688]{1,0:T(8,128)(2,1)} %decode.5.refs_4_.own_ref), channel_id=1, source_target_pairs={{0,1},{1,0},{2,3},{3,2},{4,5},{5,4},{6,7},{7,6},{8,9},{9,8},{10,11... | collective-permute-start | bytes 3096584 | tf_op jit(solution)/shard_map/ppermute | solution.py:552
  22.0 67.1 %collective-permute-start.1 = (bf16[512,5376]{1,0:T(8,128)(2,1)}, bf16[512,5376]{1,0:T(8,128)(2,1)}, u32[]{:S(2)}, u32[]{:S(2)}) collective-permute-start(bf16[512,5376]{1,0:T(8,128)(2,1)} %hidden_ref.1), channel_id=1, source_target_pairs={{0,4},{4,0},{8,12},{12,8},{1,5},{5,1},{9,13},{13,9},{2,6},{6,2},{1... | collective-permute-start | bytes 16515080 | tf_op jit(solution)/shard_map/ppermute | solution.py:552
  24.9 1.1 copy-start
  31.9 69.5 %collective-permute-start.5 = (bf16[144,2688]{1,0:T(8,128)(2,1)}, bf16[144,2688]{1,0:T(8,128)(2,1)}, u32[]{:S(2)}, u32[]{:S(2)}) collective-permute-start(bf16[144,2688]{1,0:T(8,128)(2,1)} %decode.6.refs_0_.refs_1_.own_ref), channel_id=1, source_target_pairs={{0,2},{1,3},{2,0},{3,1},{4,6},{5,7},{6,4},{7,5},{8,10},{9,11},{10,... | collective-permute-start | bytes 2322440 | tf_op jit(solution)/shard_map/ppermute | solution.py:552
  44.2 149.4 %collective-permute-start.11 = (bf16[512,5376]{1,0:T(8,128)(2,1)}, bf16[512,5376]{1,0:T(8,128)(2,1)}, u32[]{:S(2)}, u32[]{:S(2)}) collective-permute-start(bf16[512,5376]{1,0:T(8,128)(2,1)} %mix.2.refs_0_.refs_1_), channel_id=1, source_target_pairs={{0,8},{4,12},{8,0},{12,4},{1,9},{5,13},{9,1},{13,5},{2,10},{6,14},... | collective-permute-start | bytes 16515080 | tf_op jit(solution)/shard_map/ppermute | solution.py:552
  64.7 48.1 %collective-permute-start.4 = (bf16[192,2688]{1,0:T(8,128)(2,1)}, bf16[192,2688]{1,0:T(8,128)(2,1)S(1)}, u32[]{:S(2)}, u32[]{:S(2)}) collective-permute-start(bf16[192,2688]{1,0:T(8,128)(2,1)} %level.8.refs_0_.own_ref), channel_id=1, source_target_pairs={{0,1},{1,0},{2,3},{3,2},{4,5},{5,4},{6,7},{7,6},{8,9},{9,8},{10,11... | collective-permute-start | bytes 3096584 | tf_op jit(solution)/shard_map/ppermute | solution.py:552
  70.7 68.8 %collective-permute-start.7 = (bf16[192,2688]{1,0:T(8,128)(2,1)}, bf16[192,2688]{1,0:T(8,128)(2,1)S(1)}, u32[]{:S(2)}, u32[]{:S(2)}) collective-permute-start(bf16[192,2688]{1,0:T(8,128)(2,1)} %level.9.refs_14_.refs_0_.own_ref), channel_id=1, source_target_pairs={{0,2},{1,3},{2,0},{3,1},{4,6},{5,7},{6,4},{7,5},{8,10},{9,11},{10,... | collective-permute-start | bytes 3096584 | tf_op jit(solution)/shard_map/ppermute | solution.py:552
  89.2 55.9 %collective-permute-start.10 = (bf16[144,2688]{1,0:T(8,128)(2,1)}, bf16[144,2688]{1,0:T(8,128)(2,1)}, u32[]{:S(2)}, u32[]{:S(2)}) collective-permute-start(bf16[144,2688]{1,0:T(8,128)(2,1)} %decode.7.refs_0_.own_ref), channel_id=1, source_target_pairs={{0,1},{1,0},{2,3},{3,2},{4,5},{5,4},{6,7},{7,6},{8,9},{9,8},{10,11... | collective-permute-start | bytes 2322440 | tf_op jit(solution)/shard_map/ppermute | solution.py:552
  104.5 62.0 %collective-permute-start.9 = (bf16[144,2688]{1,0:T(8,128)(2,1)}, bf16[144,2688]{1,0:T(8,128)(2,1)}, u32[]{:S(2)}, u32[]{:S(2)}) collective-permute-start(bf16[144,2688]{1,0:T(8,128)(2,1)} %level.10.refs_0_.own_ref), channel_id=1, source_target_pairs={{0,1},{1,0},{2,3},{3,2},{4,5},{5,4},{6,7},{7,6},{8,9},{9,8},{10,11... | collective-permute-start | bytes 2322440 | tf_op jit(solution)/shard_map/ppermute | solution.py:552
  112.7 1.0 copy-start.7
  116.0 50.5 %collective-permute-start.6 = (bf16[192,2688]{1,0:T(8,128)(2,1)}, bf16[192,2688]{1,0:T(8,128)(2,1)S(1)}, u32[]{:S(2)}, u32[]{:S(2)}) collective-permute-start(bf16[192,2688]{1,0:T(8,128)(2,1)} %level.11.refs_14_.refs_6_), channel_id=1, source_target_pairs={{0,16},{16,0},{1,17},{17,1},{2,18},{18,2},{3,19},{19,3},{4,20},{20... | collective-permute-start | bytes 3096584 | tf_op jit(solution)/shard_map/ppermute | solution.py:552
  139.5 1.0 copy-start.6
  142.8 30.1 %collective-permute-start.8 = (bf16[192,2688]{1,0:T(8,128)(2,1)}, bf16[192,2688]{1,0:T(8,128)(2,1)S(1)}, u32[]{:S(2)}, u32[]{:S(2)}) collective-permute-start(bf16[192,2688]{1,0:T(8,128)(2,1)} %level.12.refs_0_.refs_8_), channel_id=1, source_target_pairs={{0,16},{16,0},{1,17},{17,1},{2,18},{18,2},{3,19},{19,3},{4,20},{20... | collective-permute-start | bytes 3096584 | tf_op jit(solution)/shard_map/ppermute | solution.py:552
  145.0 73.2 %reduce-scatter.4.cloned.1.call-start = ((), (), s32[]{:S(2)}) async-start(), calls=%async_computation.4 | async-start | bytes 983040 | tf_op jit(solution)/shard_map/reduce_scatter | solution.py:623
  148.2 38.1 %collective-permute-start.12 = (bf16[144,2688]{1,0:T(8,128)(2,1)}, bf16[144,2688]{1,0:T(8,128)(2,1)S(1)}, u32[]{:S(2)}, u32[]{:S(2)}) collective-permute-start(bf16[144,2688]{1,0:T(8,128)(2,1)} %level.13.refs_0_.own_ref), channel_id=1, source_target_pairs={{0,2},{1,3},{2,0},{3,1},{4,6},{5,7},{6,4},{7,5},{8,10},{9,11},{10,... | collective-permute-start | bytes 2322440 | tf_op jit(solution)/shard_map/ppermute | solution.py:552
  166.5 1.0 copy-start.4
  170.7 18.9 %collective-permute-start.13 = (bf16[144,2688]{1,0:T(8,128)(2,1)}, bf16[144,2688]{1,0:T(8,128)(2,1)S(1)}, u32[]{:S(2)}, u32[]{:S(2)}) collective-permute-start(bf16[144,2688]{1,0:T(8,128)(2,1)} %level.14.refs_10_.refs_0_), channel_id=1, source_target_pairs={{0,16},{16,0},{1,17},{17,1},{2,18},{18,2},{3,19},{19,3},{4,20},{20... | collective-permute-start | bytes 2322440 | tf_op jit(solution)/shard_map/ppermute | solution.py:552
  173.0 1.0 copy-start.5
  186.3 3.3 %copy-start.10 = (bf16[144,2688]{1,0:T(8,128)(2,1)}, bf16[144,2688]{1,0:T(8,128)(2,1)S(1)}, u32[]{:S(2)}) copy-start(bf16[144,2688]{1,0:T(8,128)(2,1)S(1)} %collective-permute-done.12.partner_ref) | copy-start | bytes 2322436
  189.6 0.9 copy-start.8
  193.6 1.1 copy-start.2
  193.6 9.4 %collective-permute-start.14 = (bf16[512,5376]{1,0:T(8,128)(2,1)}, bf16[512,5376]{1,0:T(8,128)(2,1)}, u32[]{:S(2)}, u32[]{:S(2)}) collective-permute-start(bf16[512,5376]{1,0:T(8,128)(2,1)} %gate.4.refs_1_.refs_3_), channel_id=1, source_target_pairs={{0,4},{4,0},{8,12},{12,8},{1,5},{5,1},{9,13},{13,9},{2,6},{6,2},{1... | collective-permute-start | bytes 16515080 | tf_op jit(solution)/shard_map/ppermute | solution.py:552
  193.7 49.2 %reduce-scatter.6.cloned.1.call-start = ((), (), s32[]{:S(2)}) async-start(), calls=%async_computation.6 | async-start | bytes 983040 | tf_op jit(solution)/shard_map/reduce_scatter | solution.py:623
  194.7 21.0 %collective-permute-start.15 = (bf16[144,2688]{1,0:T(8,128)(2,1)S(1)}, bf16[144,2688]{1,0:T(8,128)(2,1)S(1)}, u32[]{:S(2)}, u32[]{:S(2)}) collective-permute-start(bf16[144,2688]{1,0:T(8,128)(2,1)S(1)} %copy-done.2), channel_id=1, source_target_pairs={{0,16},{16,0},{1,17},{17,1},{2,18},{18,2},{3,19},{19,3},{4,20},{20... | collective-permute-start | bytes 2322440 | tf_op jit(solution)/shard_map/ppermute | solution.py:552
  215.7 58.0 %reduce-scatter.8.cloned.1.call-start = ((), (), s32[]{:S(2)}) async-start(), calls=%async_computation.7 | async-start | bytes 1474560 | tf_op jit(solution)/shard_map/reduce_scatter | solution.py:623
  215.8 2.5 copy-start.9
  234.8 8.2 %copy-start.3 = (bf16[1,384,256]{2,1,0:T(8,128)(2,1)S(1)}, bf16[1,384,256]{2,1,0:T(8,128)(2,1)}, u32[]{:S(2)}) copy-start(bf16[1,384,256]{2,1,0:T(8,128)(2,1)} %reduce-scatter.4.cloned.1.call-done) | copy-start | bytes 589828
  242.9 0.9 copy-start.1
  243.0 2.4 collective-permute-start.16
  243.9 4.8 %collective-permute-start.18 = (bf16[384,128]{1,0:T(8,128)(2,1)S(1)}, bf16[384,128]{1,0:T(8,128)(2,1)S(1)}, u32[]{:S(2)}, u32[]{:S(2)}) collective-permute-start(bf16[384,128]{1,0:T(8,128)(2,1)S(1)} %get-tuple-element.12), channel_id=1, source_target_pairs={{0,8},{4,12},{8,0},{12,4},{1,9},{5,13},{9,1},{13,5},{2,10},{6,14},... | collective-permute-start | bytes 294920 | tf_op jit(solution)/shard_map/ppermute | solution.py:552
  245.4 5.2 %collective-permute-start.20 = (bf16[384,128]{1,0:T(8,128)(2,1)S(1)}, bf16[384,128]{1,0:T(8,128)(2,1)S(1)}, u32[]{:S(2)}, u32[]{:S(2)}) collective-permute-start(bf16[384,128]{1,0:T(8,128)(2,1)S(1)} %get-tuple-element.13), channel_id=1, source_target_pairs={{0,12},{4,8},{8,4},{12,0},{1,13},{5,9},{9,5},{13,1},{2,14},{6,10},... | collective-permute-start | bytes 294920 | tf_op jit(solution)/shard_map/ppermute | solution.py:552
  274.7 2.7 collective-permute-start.17
  275.6 4.9 %collective-permute-start.19 = (bf16[288,128]{1,0:T(8,128)(2,1)S(1)}, bf16[288,128]{1,0:T(8,128)(2,1)S(1)}, u32[]{:S(2)}, u32[]{:S(2)}) collective-permute-start(bf16[288,128]{1,0:T(8,128)(2,1)S(1)} %get-tuple-element.9), channel_id=1, source_target_pairs={{0,8},{4,12},{8,0},{12,4},{1,9},{5,13},{9,1},{13,5},{2,10},{6,14},... | collective-permute-start | bytes 221192 | tf_op jit(solution)/shard_map/ppermute | solution.py:552
  277.0 4.6 %collective-permute-start.21 = (bf16[288,128]{1,0:T(8,128)(2,1)S(1)}, bf16[288,128]{1,0:T(8,128)(2,1)S(1)}, u32[]{:S(2)}, u32[]{:S(2)}) collective-permute-start(bf16[288,128]{1,0:T(8,128)(2,1)S(1)} %get-tuple-element.8), channel_id=1, source_target_pairs={{0,12},{4,8},{8,4},{12,0},{1,13},{5,9},{9,5},{13,1},{2,14},{6,10},... | collective-permute-start | bytes 221192 | tf_op jit(solution)/shard_map/ppermute | solution.py:552
Sparse Core Ops, SparseCore 0:
  9.1 37.1 all-gather.2
  145.2 43.9 all-gather.4
  193.8 24.3 reduce-scatter.3
  220.4 22.4 reduce-scatter.5
  245.1 28.5 reduce-scatter.7

commit v4 on v3

--- a/solution.py
+++ b/solution.py
@@ -624,9 +624,9 @@
 
     early = [piece_a, across_a, piece_c, across_c]
     own_early, own_done = reduced(own_rows, own_attn, early, EARLY, (piece_b,))
-    piece_d = level_step(piece_d, 2, (piece_b, own_done,across_b))
+    piece_d = level_step(piece_d, 2, (piece_b, own_done))
     across_d = flipped(piece_d, "group", 1)
-    far_rows = both_cores(gate(flipped(rotated, "seq", 2), piece_d))
+    far_rows = both_cores(gate(flipped(rotated, "seq", 2), piece_d,across_b))
     late = [piece_b, across_b, piece_d, across_d]
     far_early, far_done = reduced(far_rows, far_attn, early, EARLY, (piece_d,))
     all_late, _ = reduced(

time: 296 us -> 294 us (level)
  waiting for transfers between devices: 91.9 us -> 88.3 us
    ppermute x22, waiting for transfers between devices: 58 us -> 54.5 us  [flipped(): lax.ppermute(value, axis, [(i, i ^ bit) for i in range(lax.axis_size(axis...]
    unnamed x24 -> x26, local copies, waits for them, and re-layouts: 12.2 us -> 12.9 us
where the time goes in v4:
time: 294 us; the launch traced here: 288 us
  Pallas kernels  130 us (44%)
  waiting for transfers between devices  88.3 us (30%)
  starting transfers between devices  25.5 us (9%)
  between operations  16.6 us (6%)
  local copies, waits for them, and re-layouts  15.9 us (5%)
  other arithmetic  11.8 us (4%)
    ppermute x22, waiting for transfers between devices, flipped(): lax.ppermute(value, axis, [(i, i ^ bit) for i in range(lax.axis_size(axis...  54.5 us
    pallas_call x3, Pallas kernels, project(): pl.pallas_call(lambda *refs: project_kernel(chunks, [flip for _, flip in...  41.4 us
    reduce_scatter x3, waiting for transfers between devices, reduced(): lax.psum_scatter(partial, 'tp', scatter_dimension=0, tiled=True)[0]  33.7 us
    pallas_call x2, Pallas kernels, attend(): pl.pallas_call(attend_kernel, grid_spec=pltpu.PrefetchScalarGridSpec(num_...  28.1 us
    ppermute x22, starting transfers between devices, flipped(): lax.ppermute(value, axis, [(i, i ^ bit) for i in range(lax.axis_size(axis...  25.4 us
    pallas_call x2, Pallas kernels, mix_hidden(): pl.pallas_call(mix_kernel, grid=(rows // step,), in_specs=[pl.BlockSpec((...  23 us
    pallas_call x8, Pallas kernels, level_step(): pl.pallas_call(level_kernel, grid_spec=pltpu.PrefetchScalarGridSpec(num_s...  22 us
    pallas_call x4, Pallas kernels, dequant(): pl.pallas_call(lambda *refs: dequant_kernel(first, *refs), grid_spec=pltp...  14.7 us
  transfers between devices with their start and end apart: 27, of which 14 were waited for; matrix products, arithmetic and copies ran while one was open for 5% of the time, Pallas kernels for 45%

profile of v4, /device:TPU:0, one launch (start us, length us, event | category | flops | bytes accessed | tf_op | source)
XLA Modules:
  0.0 287.9 jit_solution(7280522667345282014)
XLA Ops:
  6.5 2.5 copy.19
  9.6 2.9 %decode.4.refs_4_.own_ref = bf16[192,2688]{1,0:T(8,128)(2,1)} custom-call(s32[1]{0:T(128)} %bitcast.refs_0_, s32[672,5376]{1,0:T(8,128)} %bitcast.17, s32[42,672]{1,0:T(8,128)} %refs_2_.7, bf16[42,5376]{1,0:T(8,128)(2,1)} %constant.46.clone.refs_3_), custom_call_target="tpu_custom_call" | custom-call | flops 3450000128 | bytes 1 | tf_op jit(solution)/shard_map/decode/pallas_call | solution.py:283
  12.5 3.6 %collective-permute-start.3 = (bf16[192,2688]{1,0:T(8,128)(2,1)}, bf16[192,2688]{1,0:T(8,128)(2,1)}, u32[]{:S(2)}, u32[]{:S(2)}) collective-permute-start(bf16[192,2688]{1,0:T(8,128)(2,1)} %decode.4.refs_4_.own_ref), channel_id=1, source_target_pairs={{0,2},{1,3},{2,0},{3,1},{4,6},{5,7},{6,4},{7,5},{8,10},{9,11},{10,... | collective-permute-start | bytes 3096584 | tf_op jit(solution)/shard_map/ppermute | solution.py:552
  16.2 4.4 %decode.5.refs_4_.own_ref = bf16[192,2688]{1,0:T(8,128)(2,1)} custom-call(s32[1]{0:T(128)} %bitcast.refs_0_, s32[672,5376]{1,0:T(8,128)} %bitcast.18, s32[42,672]{1,0:T(8,128)} %refs_2_.7, bf16[42,5376]{1,0:T(8,128)(2,1)} %constant.46.clone.refs_3_, bf16[192,2688]{1,0:T(8,128)(2,1)} %decode.4.refs_4_.own_ref, bf16[512,1024]{1,0:T(8,128)(2,1)} %bitcast.22), custom_call_target="tpu_custom_call" | custom-call | flops 3450000128 | bytes 1 | tf_op jit(solution)/shard_map/decode/pallas_call | solution.py:283
  20.5 1.6 collective-permute-start.2
  22.8 2.1 copy.20
  25.9 3.7 %decode.6.refs_0_.refs_1_.own_ref = bf16[144,2688]{1,0:T(8,128)(2,1)} custom-call(s32[1]{0:T(128)} %bitcast.refs_0_, s32[672,5376]{1,0:T(8,128)} %bitcast.19, s32[42,672]{1,0:T(8,128)} %refs_2_.7, bf16[42,5376]{1,0:T(8,128)(2,1)} %constant.46.clone.refs_3_, bf16[192,2688]{1,0:T(8,128)(2,1)} %decode.5.refs_4_.own_ref, bf16[512,1024]{1,0:T(8,128)(2,1)} %copy-done), custom_call_target="tpu_custom_call" | custom-call | flops 3450000128 | bytes 1 | tf_op jit(solution)/shard_map/decode/pallas_call | solution.py:283
  33.0 11.5 %mix.2.refs_0_.refs_1_ = bf16[512,5376]{1,0:T(8,128)(2,1)} custom-call(bf16[512,5376]{1,0:T(8,128)(2,1)} %hidden_ref.1, bf16[864,768]{1,0:T(8,128)(2,1)} %constant.47.clone.table_ref, bf16[144,2688]{1,0:T(8,128)(2,1)} %decode.6.refs_0_.refs_1_.own_ref), custom_call_target="tpu_custom_call" | custom-call | flops 18400000000 | bytes 1 | tf_op jit(solution)/shard_map/mix/pallas_call | solution.py:247
  44.5 1.5 collective-permute-start.11
  46.7 4.4 %fusion.refs_1_.refs_6_.refs_7_.refs_12_.refs_13_ = bf16[1024,1024]{1,0:T(8,128)(2,1)} fusion(s32[]{:T(128)S(6)} %select_n.64, bf16[1024,1024]{1,0:T(8,128)(2,1)S(1)} %bitcast.23), kind=kLoop, calls=%fused_computation.2 | loop fusion | flops 4194304 | bytes 4194308 | tf_op jit(solution)/shard_map/concatenate | solution.py:589
  51.2 3.7 %fusion.1 = (f32[2048,64]{1,0:T(8,128)S(1)}, f32[2048,64]{1,0:T(8,128)S(1)}, f32[2048,64]{1,0:T(8,128)S(1)}) fusion(f32[64]{0:T(128)S(1)} %multiply_power_fusion, f32[2048]{0:T(1024)S(1)} %add_convert_fusion), kind=kLoop, calls=%fused_computation.8 | loop fusion | flops 262144 | bytes 1581312 | tf_op jit(solution)/shard_map/neg | solution.py:587
  54.9 1.9 pad_maximum_fusion
  56.8 5.5 %collective-permute-done.3.partner_ref = bf16[192,2688]{1,0:T(8,128)(2,1)} collective-permute-done((bf16[192,2688]{1,0:T(8,128)(2,1)}, bf16[192,2688]{1,0:T(8,128)(2,1)}, u32[]{:S(2)}, u32[]{:S(2)}) %collective-permute-start.3) | collective-permute-done | bytes 1032224 | tf_op jit(solution)/shard_map/ppermute | solution.py:552
  62.4 2.4 level.8.refs_0_.own_ref
  65.5 2.9 collective-permute-done.2.partner_ref
  68.3 2.4 level.9.refs_14_.refs_0_.own_ref
  71.4 14.1 %attend.2.refs_4_.refs_3_.refs_5_ = bf16[512,1024]{1,0:T(8,128)(2,1)} custom-call(s32[1]{0:T(128)} %bitcast.1.place_ref, bf16[512,1024]{1,0:T(8,128)(2,1)} %query_ref.1, f32[2048,128]{1,0:T(8,128)} %get-tuple-element.29.refs_2_.cosine_ref.refs_4_.refs_10_, f32[2048,128]{1,0:T(8,128)} %get-tuple-element.30.refs_3_.sine_ref.refs_5_.refs_11_, ...), custom_call_target="tpu_custom_call" | custom-call | flops 14949999616 | bytes 1 | tf_op jit(solution)/shard_map/attend/pallas_call | solution.py:536
  85.5 3.8 %decode.7.refs_0_.own_ref = bf16[144,2688]{1,0:T(8,128)(2,1)} custom-call(s32[1]{0:T(128)} %bitcast.refs_0_, s32[672,5376]{1,0:T(8,128)} %bitcast.20, s32[42,672]{1,0:T(8,128)} %refs_2_.7, bf16[42,5376]{1,0:T(8,128)(2,1)} %constant.46.clone.refs_3_, bf16[512,1024]{1,0:T(8,128)(2,1)} %attend.2.refs_4_.refs_3_.refs_5_), custom_call_target="tpu_custom_call" | custom-call | flops 3450000128 | bytes 1 | tf_op jit(solution)/shard_map/decode/pallas_call | solution.py:283
  89.9 11.5 %mix.3.refs_1_.refs_2_ = bf16[512,5376]{1,0:T(8,128)(2,1)} custom-call(bf16[512,5376]{1,0:T(8,128)(2,1)} %collective-permute-done.1.hidden_ref, bf16[864,768]{1,0:T(8,128)(2,1)} %constant.47.clone.table_ref, bf16[144,2688]{1,0:T(8,128)(2,1)} %decode.7.refs_0_.own_ref), custom_call_target="tpu_custom_call" | custom-call | flops 18400000000 | bytes 1 | tf_op jit(solution)/shard_map/mix/pallas_call | solution.py:247
  102.3 3.1 %level.10.refs_0_.own_ref = bf16[144,2688]{1,0:T(8,128)(2,1)} custom-call(s32[1]{0:T(128)} %bitcast.5.sign_ref, bf16[144,2688]{1,0:T(8,128)(2,1)} %decode.6.refs_0_.refs_1_.own_ref, bf16[144,2688]{1,0:T(8,128)(2,1)} %copy-done.8, bf16[192,2688]{1,0:T(8,128)(2,1)} %level.9.refs_14_.refs_0_.own_ref, bf16[512,5376]{1,0:T(8,128)(2,1)} %mix.3.refs_1_.refs_2_), custom_call_target="tpu_custom_call" | custom-call | flops 3450000128 | bytes 1 | tf_op jit(solution)/shard_map/level/pallas_call | solution.py:315
  105.4 1.4 collective-permute-start.9
  106.8 6.0 %collective-permute-done.4.partner_ref = bf16[192,2688]{1,0:T(8,128)(2,1)S(1)} collective-permute-done((bf16[192,2688]{1,0:T(8,128)(2,1)}, bf16[192,2688]{1,0:T(8,128)(2,1)S(1)}, u32[]{:S(2)}, u32[]{:S(2)}) %collective-permute-start.4) | collective-permute-done | bytes 1032224 | tf_op jit(solution)/shard_map/ppermute | solution.py:552
  113.8 2.4 level.11.refs_14_.refs_6_
  116.1 1.8 collective-permute-start.6
  117.9 14.0 %attend.3.refs_0_.refs_4_.refs_6_ = bf16[512,1024]{1,0:T(8,128)(2,1)} custom-call(s32[1]{0:T(128)} %bitcast.6.place_ref, bf16[512,1024]{1,0:T(8,128)(2,1)} %copy-done, f32[2048,128]{1,0:T(8,128)} %get-tuple-element.29.refs_2_.cosine_ref.refs_4_.refs_10_, f32[2048,128]{1,0:T(8,128)} %get-tuple-element.30.refs_3_.sine_ref.refs_5_.refs_11_, ...), custom_call_target="tpu_custom_call" | custom-call | flops 1 | bytes 1 | tf_op jit(solution)/shard_map/attend/pallas_call | solution.py:536
  131.9 7.6 %collective-permute-done.7.partner_ref = bf16[192,2688]{1,0:T(8,128)(2,1)S(1)} collective-permute-done((bf16[192,2688]{1,0:T(8,128)(2,1)}, bf16[192,2688]{1,0:T(8,128)(2,1)S(1)}, u32[]{:S(2)}, u32[]{:S(2)}) %collective-permute-start.7) | collective-permute-done | bytes 1032224 | tf_op jit(solution)/shard_map/ppermute | solution.py:552
  140.5 2.4 level.12.refs_0_.refs_8_
  142.8 1.6 collective-permute-start.8
  145.0 3.1 %level.13.refs_0_.own_ref = bf16[144,2688]{1,0:T(8,128)(2,1)} custom-call(s32[1]{0:T(128)} %bitcast.4.sign_ref, bf16[144,2688]{1,0:T(8,128)(2,1)} %decode.7.refs_0_.own_ref, bf16[144,2688]{1,0:T(8,128)(2,1)} %collective-permute-done.10.partner_ref, bf16[192,2688]{1,0:T(8,128)(2,1)} %level.12.refs_0_.refs_8_), custom_call_target="tpu_custom_call" | custom-call | flops 3450000128 | bytes 1 | tf_op jit(solution)/shard_map/level/pallas_call | solution.py:315
  148.2 2.7 collective-permute-start.12
  150.9 15.6 %collective-permute-done.9.partner_ref = bf16[144,2688]{1,0:T(8,128)(2,1)S(1)} collective-permute-done((bf16[144,2688]{1,0:T(8,128)(2,1)}, bf16[144,2688]{1,0:T(8,128)(2,1)S(1)}, u32[]{:S(2)}, u32[]{:S(2)}) %collective-permute-start.9) | collective-permute-done | bytes 774176 | tf_op jit(solution)/shard_map/ppermute | solution.py:552
  168.4 3.1 %level.14.refs_10_.refs_0_ = bf16[144,2688]{1,0:T(8,128)(2,1)} custom-call(s32[1]{0:T(128)} %bitcast.4.sign_ref, bf16[144,2688]{1,0:T(8,128)(2,1)} %level.10.refs_0_.own_ref, bf16[144,2688]{1,0:T(8,128)(2,1)} %copy-done.9, bf16[144,2688]{1,0:T(8,128)(2,1)} %level.13.refs_0_.own_ref, bf16[192,2688]{1,0:T(8,128)(2,1)} %copy-done.5), custom_call_target="tpu_custom_call" | custom-call | flops 3450000128 | bytes 1 | tf_op jit(solution)/shard_map/level/pallas_call | solution.py:315
  171.5 2.4 collective-permute-start.13
  173.9 12.3 %project.3.refs_1_ = bf16[4,384,256]{2,1,0:T(8,128)(2,1)} custom-call(s32[2]{0:T(128)} %pad_add_fusion.refs_0_, bf16[512,5376]{1,0:T(8,128)(2,1)} %mix.2.refs_0_.refs_1_, bf16[512,5376]{1,0:T(8,128)(2,1)} %mix.3.refs_1_.refs_2_, bf16[512,1024]{1,0:T(8,128)(2,1)} %attend.2.refs_4_.refs_3_.refs_5_, bf16[512,1024]{1,0:T(8,128)(2,1)} %attend.3.refs_0_.refs_4_.refs_6_, ...), custom_call_target="tpu_custom_call" | custom-call | flops 11500000256 | bytes 1 | tf_op jit(solution)/shard_map/project/pallas_call | solution.py:414
  187.2 3.2 %level.15.refs_1_.refs_10_.refs_12_ = bf16[144,2688]{1,0:T(8,128)(2,1)} custom-call(s32[1]{0:T(128)} %bitcast.5.sign_ref, bf16[144,2688]{1,0:T(8,128)(2,1)} %level.13.refs_0_.own_ref, bf16[144,2688]{1,0:T(8,128)(2,1)} %copy-done.11, bf16[144,2688]{1,0:T(8,128)(2,1)} %level.14.refs_10_.refs_0_, bf16[4,384,256]{2,1,0:T(8,128)(2,1)} %project.3.refs_1_), custom_call_target="tpu_custom_call" | custom-call | flops 3450000128 | bytes 1 | tf_op jit(solution)/shard_map/level/pallas_call | solution.py:315
  191.7 1.8 collective-permute-start.15
  193.5 7.5 %collective-permute-done.14.refs_2_.refs_4_ = bf16[512,5376]{1,0:T(8,128)(2,1)} collective-permute-done((bf16[512,5376]{1,0:T(8,128)(2,1)}, bf16[512,5376]{1,0:T(8,128)(2,1)}, u32[]{:S(2)}, u32[]{:S(2)}) %collective-permute-start.14) | collective-permute-done | bytes 5505056 | tf_op jit(solution)/shard_map/ppermute | solution.py:552
  201.0 12.6 %project.4.refs_14_ = bf16[4,384,256]{2,1,0:T(8,128)(2,1)} custom-call(s32[2]{0:T(128)} %pad_add_fusion.refs_0_, bf16[512,5376]{1,0:T(8,128)(2,1)} %gate.4.refs_1_.refs_3_, bf16[512,5376]{1,0:T(8,128)(2,1)} %collective-permute-done.14.refs_2_.refs_4_, bf16[2048,1024]{1,0:T(8,128)(2,1)} %all-gather.5.cloned.1.call-done.refs_3_.refs_4_.refs_7_.refs_8_, ...), custom_call_target="tpu_custom_call" | custom-call | flops 11500000256 | bytes 1 | tf_op jit(solution)/shard_map/project/pallas_call | solution.py:414
  213.7 2.3 reduce-scatter.4.cloned.1.call-done
  216.0 16.5 %project.5.refs_0_ = bf16[4,288,512]{2,1,0:T(8,128)(2,1)} custom-call(s32[2]{0:T(128)} %pad_add_fusion.refs_0_, bf16[512,5376]{1,0:T(8,128)(2,1)} %mix.2.refs_0_.refs_1_, bf16[512,5376]{1,0:T(8,128)(2,1)} %mix.3.refs_1_.refs_2_, bf16[512,5376]{1,0:T(8,128)(2,1)} %gate.4.refs_1_.refs_3_, bf16[512,5376]{1,0:T(8,128)(2,1)} %collective-permute-done.14.refs_2_.refs_4_, ...), custom_call_target="tpu_custom_call" | custom-call | flops 11500000256 | bytes 1 | tf_op jit(solution)/shard_map/project/pallas_call | solution.py:414
  232.5 8.3 %reduce-scatter.6.cloned.1.call-done = bf16[1,384,256]{2,1,0:T(8,128)(2,1)} async-done(((bf16[4,384,256]{2,1,0:T(8,128)(2,1)}), bf16[1,384,256]{2,1,0:T(8,128)(2,1)}) %reduce-scatter.6.cloned.1.call-update) | async-done | bytes 196624 | tf_op jit(solution)/shard_map/reduce_scatter | solution.py:623
  241.7 1.5 collective-permute-start.18
  243.4 3.2 %collective-permute-done.18 = bf16[384,128]{1,0:T(8,128)(2,1)S(1)} collective-permute-done((bf16[384,128]{1,0:T(8,128)(2,1)S(1)}, bf16[384,128]{1,0:T(8,128)(2,1)S(1)}, u32[]{:S(2)}, u32[]{:S(2)}) %collective-permute-start.18) | collective-permute-done | bytes 98336 | tf_op jit(solution)/shard_map/ppermute | solution.py:552
  246.6 1.7 collective-permute-done.20
  248.3 23.1 %reduce-scatter.8.cloned.1.call-done = bf16[1,288,512]{2,1,0:T(8,128)(2,1)} async-done(((bf16[4,288,512]{2,1,0:T(8,128)(2,1)}), bf16[1,288,512]{2,1,0:T(8,128)(2,1)}) %reduce-scatter.8.cloned.1.call-update) | async-done | bytes 294928 | tf_op jit(solution)/shard_map/reduce_scatter | solution.py:623
  273.3 1.5 collective-permute-start.19
  275.1 3.0 %collective-permute-done.19 = bf16[288,128]{1,0:T(8,128)(2,1)S(1)} collective-permute-done((bf16[288,128]{1,0:T(8,128)(2,1)S(1)}, bf16[288,128]{1,0:T(8,128)(2,1)S(1)}, u32[]{:S(2)}, u32[]{:S(2)}) %collective-permute-start.19) | collective-permute-done | bytes 73760 | tf_op jit(solution)/shard_map/ppermute | solution.py:552
  279.8 1.1 copy.18
  (82 shorter events, 18.1 us)
Async XLA Ops:
  6.5 64.9 %all-gather.3.cloned.1.call-start = ((), (), s32[]{:S(2)}) async-start(), calls=%async_computation.3 | async-start | bytes 5242880 | tf_op jit(solution)/shard_map/all_gather | solution.py:565
  9.1 184.4 %all-gather.5.cloned.1.call-start = ((), (), s32[]{:S(2)}) async-start(), calls=%async_computation.5 | async-start | bytes 5242880 | tf_op jit(solution)/shard_map/all_gather | solution.py:602
  9.1 15.8 %collective-permute-start = (bf16[512,1024]{1,0:T(8,128)(2,1)}, bf16[512,1024]{1,0:T(8,128)(2,1)S(1)}, u32[]{:S(2)}, u32[]{:S(2)}) collective-permute-start(bf16[512,1024]{1,0:T(8,128)(2,1)} %query_ref.1), channel_id=1, source_target_pairs={{0,4},{4,0},{8,12},{12,8},{1,5},{5,1},{9,13},{13,9},{2,6},{6,2},{1... | collective-permute-start | bytes 3145736 | tf_op jit(solution)/shard_map/ppermute | solution.py:552
  12.5 49.8 %collective-permute-start.3 = (bf16[192,2688]{1,0:T(8,128)(2,1)}, bf16[192,2688]{1,0:T(8,128)(2,1)}, u32[]{:S(2)}, u32[]{:S(2)}) collective-permute-start(bf16[192,2688]{1,0:T(8,128)(2,1)} %decode.4.refs_4_.own_ref), channel_id=1, source_target_pairs={{0,2},{1,3},{2,0},{3,1},{4,6},{5,7},{6,4},{7,5},{8,10},{9,11},{10,... | collective-permute-start | bytes 3096584 | tf_op jit(solution)/shard_map/ppermute | solution.py:552
  20.5 47.8 %collective-permute-start.2 = (bf16[192,2688]{1,0:T(8,128)(2,1)}, bf16[192,2688]{1,0:T(8,128)(2,1)}, u32[]{:S(2)}, u32[]{:S(2)}) collective-permute-start(bf16[192,2688]{1,0:T(8,128)(2,1)} %decode.5.refs_4_.own_ref), channel_id=1, source_target_pairs={{0,1},{1,0},{2,3},{3,2},{4,5},{5,4},{6,7},{7,6},{8,9},{9,8},{10,11... | collective-permute-start | bytes 3096584 | tf_op jit(solution)/shard_map/ppermute | solution.py:552
  22.1 67.2 %collective-permute-start.1 = (bf16[512,5376]{1,0:T(8,128)(2,1)}, bf16[512,5376]{1,0:T(8,128)(2,1)}, u32[]{:S(2)}, u32[]{:S(2)}) collective-permute-start(bf16[512,5376]{1,0:T(8,128)(2,1)} %hidden_ref.1), channel_id=1, source_target_pairs={{0,4},{4,0},{8,12},{12,8},{1,5},{5,1},{9,13},{13,9},{2,6},{6,2},{1... | collective-permute-start | bytes 16515080 | tf_op jit(solution)/shard_map/ppermute | solution.py:552
  24.9 1.0 copy-start
  32.2 69.2 %collective-permute-start.5 = (bf16[144,2688]{1,0:T(8,128)(2,1)}, bf16[144,2688]{1,0:T(8,128)(2,1)S(1)}, u32[]{:S(2)}, u32[]{:S(2)}) collective-permute-start(bf16[144,2688]{1,0:T(8,128)(2,1)} %decode.6.refs_0_.refs_1_.own_ref), channel_id=1, source_target_pairs={{0,2},{1,3},{2,0},{3,1},{4,6},{5,7},{6,4},{7,5},{8,10},{9,11},{10,... | collective-permute-start | bytes 2322440 | tf_op jit(solution)/shard_map/ppermute | solution.py:552
  44.5 145.8 %collective-permute-start.11 = (bf16[512,5376]{1,0:T(8,128)(2,1)}, bf16[512,5376]{1,0:T(8,128)(2,1)}, u32[]{:S(2)}, u32[]{:S(2)}) collective-permute-start(bf16[512,5376]{1,0:T(8,128)(2,1)} %mix.2.refs_0_.refs_1_), channel_id=1, source_target_pairs={{0,8},{4,12},{8,0},{12,4},{1,9},{5,13},{9,1},{13,5},{2,10},{6,14},... | collective-permute-start | bytes 16515080 | tf_op jit(solution)/shard_map/ppermute | solution.py:552
  64.8 48.1 %collective-permute-start.4 = (bf16[192,2688]{1,0:T(8,128)(2,1)}, bf16[192,2688]{1,0:T(8,128)(2,1)S(1)}, u32[]{:S(2)}, u32[]{:S(2)}) collective-permute-start(bf16[192,2688]{1,0:T(8,128)(2,1)} %level.8.refs_0_.own_ref), channel_id=1, source_target_pairs={{0,1},{1,0},{2,3},{3,2},{4,5},{5,4},{6,7},{7,6},{8,9},{9,8},{10,11... | collective-permute-start | bytes 3096584 | tf_op jit(solution)/shard_map/ppermute | solution.py:552
  70.7 68.8 %collective-permute-start.7 = (bf16[192,2688]{1,0:T(8,128)(2,1)}, bf16[192,2688]{1,0:T(8,128)(2,1)S(1)}, u32[]{:S(2)}, u32[]{:S(2)}) collective-permute-start(bf16[192,2688]{1,0:T(8,128)(2,1)} %level.9.refs_14_.refs_0_.own_ref), channel_id=1, source_target_pairs={{0,2},{1,3},{2,0},{3,1},{4,6},{5,7},{6,4},{7,5},{8,10},{9,11},{10,... | collective-permute-start | bytes 3096584 | tf_op jit(solution)/shard_map/ppermute | solution.py:552
  89.3 55.7 %collective-permute-start.10 = (bf16[144,2688]{1,0:T(8,128)(2,1)}, bf16[144,2688]{1,0:T(8,128)(2,1)}, u32[]{:S(2)}, u32[]{:S(2)}) collective-permute-start(bf16[144,2688]{1,0:T(8,128)(2,1)} %decode.7.refs_0_.own_ref), channel_id=1, source_target_pairs={{0,1},{1,0},{2,3},{3,2},{4,5},{5,4},{6,7},{7,6},{8,9},{9,8},{10,11... | collective-permute-start | bytes 2322440 | tf_op jit(solution)/shard_map/ppermute | solution.py:552
  101.4 0.9 copy-start.8
  105.4 61.1 %collective-permute-start.9 = (bf16[144,2688]{1,0:T(8,128)(2,1)}, bf16[144,2688]{1,0:T(8,128)(2,1)S(1)}, u32[]{:S(2)}, u32[]{:S(2)}) collective-permute-start(bf16[144,2688]{1,0:T(8,128)(2,1)} %level.10.refs_0_.own_ref), channel_id=1, source_target_pairs={{0,1},{1,0},{2,3},{3,2},{4,5},{5,4},{6,7},{7,6},{8,9},{9,8},{10,11... | collective-permute-start | bytes 2322440 | tf_op jit(solution)/shard_map/ppermute | solution.py:552
  112.8 1.0 copy-start.7
  116.1 50.4 %collective-permute-start.6 = (bf16[192,2688]{1,0:T(8,128)(2,1)}, bf16[192,2688]{1,0:T(8,128)(2,1)S(1)}, u32[]{:S(2)}, u32[]{:S(2)}) collective-permute-start(bf16[192,2688]{1,0:T(8,128)(2,1)} %level.11.refs_14_.refs_6_), channel_id=1, source_target_pairs={{0,16},{16,0},{1,17},{17,1},{2,18},{18,2},{3,19},{19,3},{4,20},{20... | collective-permute-start | bytes 3096584 | tf_op jit(solution)/shard_map/ppermute | solution.py:552
  139.5 1.0 copy-start.6
  142.8 31.1 %collective-permute-start.8 = (bf16[192,2688]{1,0:T(8,128)(2,1)}, bf16[192,2688]{1,0:T(8,128)(2,1)}, u32[]{:S(2)}, u32[]{:S(2)}) collective-permute-start(bf16[192,2688]{1,0:T(8,128)(2,1)} %level.12.refs_0_.refs_8_), channel_id=1, source_target_pairs={{0,16},{16,0},{1,17},{17,1},{2,18},{18,2},{3,19},{19,3},{4,20},{20... | collective-permute-start | bytes 3096584 | tf_op jit(solution)/shard_map/ppermute | solution.py:552
  145.0 71.0 %reduce-scatter.4.cloned.1.call-start = ((), (), s32[]{:S(2)}) async-start(), calls=%async_computation.4 | async-start | bytes 983040 | tf_op jit(solution)/shard_map/reduce_scatter | solution.py:623
  148.2 38.1 %collective-permute-start.12 = (bf16[144,2688]{1,0:T(8,128)(2,1)}, bf16[144,2688]{1,0:T(8,128)(2,1)S(1)}, u32[]{:S(2)}, u32[]{:S(2)}) collective-permute-start(bf16[144,2688]{1,0:T(8,128)(2,1)} %level.13.refs_0_.own_ref), channel_id=1, source_target_pairs={{0,2},{1,3},{2,0},{3,1},{4,6},{5,7},{6,4},{7,5},{8,10},{9,11},{10,... | collective-permute-start | bytes 2322440 | tf_op jit(solution)/shard_map/ppermute | solution.py:552
  166.5 0.9 copy-start.9
  167.4 1.0 copy-start.5
  171.5 19.1 %collective-permute-start.13 = (bf16[144,2688]{1,0:T(8,128)(2,1)}, bf16[144,2688]{1,0:T(8,128)(2,1)S(1)}, u32[]{:S(2)}, u32[]{:S(2)}) collective-permute-start(bf16[144,2688]{1,0:T(8,128)(2,1)} %level.14.refs_10_.refs_0_), channel_id=1, source_target_pairs={{0,16},{16,0},{1,17},{17,1},{2,18},{18,2},{3,19},{19,3},{4,20},{20... | collective-permute-start | bytes 2322440 | tf_op jit(solution)/shard_map/ppermute | solution.py:552
  186.3 0.9 copy-start.11
  190.3 1.3 copy-start.3
  190.7 0.9 copy-start.2
  191.6 9.4 %collective-permute-start.14 = (bf16[512,5376]{1,0:T(8,128)(2,1)}, bf16[512,5376]{1,0:T(8,128)(2,1)}, u32[]{:S(2)}, u32[]{:S(2)}) collective-permute-start(bf16[512,5376]{1,0:T(8,128)(2,1)} %gate.4.refs_1_.refs_3_), channel_id=1, source_target_pairs={{0,4},{4,0},{8,12},{12,8},{1,5},{5,1},{9,13},{13,9},{2,6},{6,2},{1... | collective-permute-start | bytes 16515080 | tf_op jit(solution)/shard_map/ppermute | solution.py:552
  191.6 49.2 %reduce-scatter.6.cloned.1.call-start = ((), (), s32[]{:S(2)}) async-start(), calls=%async_computation.6 | async-start | bytes 983040 | tf_op jit(solution)/shard_map/reduce_scatter | solution.py:623
  191.7 22.0 %collective-permute-start.15 = (bf16[144,2688]{1,0:T(8,128)(2,1)S(1)}, bf16[144,2688]{1,0:T(8,128)(2,1)S(1)}, u32[]{:S(2)}, u32[]{:S(2)}) collective-permute-start(bf16[144,2688]{1,0:T(8,128)(2,1)S(1)} %copy-done.3), channel_id=1, source_target_pairs={{0,16},{16,0},{1,17},{17,1},{2,18},{18,2},{3,19},{19,3},{4,20},{20... | collective-permute-start | bytes 2322440 | tf_op jit(solution)/shard_map/ppermute | solution.py:552
  213.6 57.8 %reduce-scatter.8.cloned.1.call-start = ((), (), s32[]{:S(2)}) async-start(), calls=%async_computation.7 | async-start | bytes 1474560 | tf_op jit(solution)/shard_map/reduce_scatter | solution.py:623
  213.7 2.3 copy-start.10
  232.5 8.3 %copy-start.4 = (bf16[1,384,256]{2,1,0:T(8,128)(2,1)S(1)}, bf16[1,384,256]{2,1,0:T(8,128)(2,1)}, u32[]{:S(2)}) copy-start(bf16[1,384,256]{2,1,0:T(8,128)(2,1)} %reduce-scatter.4.cloned.1.call-done) | copy-start | bytes 589828
  240.8 0.9 copy-start.1
  240.8 2.3 collective-permute-start.16
  241.7 4.9 %collective-permute-start.18 = (bf16[384,128]{1,0:T(8,128)(2,1)S(1)}, bf16[384,128]{1,0:T(8,128)(2,1)S(1)}, u32[]{:S(2)}, u32[]{:S(2)}) collective-permute-start(bf16[384,128]{1,0:T(8,128)(2,1)S(1)} %get-tuple-element.12), channel_id=1, source_target_pairs={{0,8},{4,12},{8,0},{12,4},{1,9},{5,13},{9,1},{13,5},{2,10},{6,14},... | collective-permute-start | bytes 294920 | tf_op jit(solution)/shard_map/ppermute | solution.py:552
  243.2 5.1 %collective-permute-start.20 = (bf16[384,128]{1,0:T(8,128)(2,1)S(1)}, bf16[384,128]{1,0:T(8,128)(2,1)S(1)}, u32[]{:S(2)}, u32[]{:S(2)}) collective-permute-start(bf16[384,128]{1,0:T(8,128)(2,1)S(1)} %get-tuple-element.13), channel_id=1, source_target_pairs={{0,12},{4,8},{8,4},{12,0},{1,13},{5,9},{9,5},{13,1},{2,14},{6,10},... | collective-permute-start | bytes 294920 | tf_op jit(solution)/shard_map/ppermute | solution.py:552
  272.4 2.7 collective-permute-start.17
  273.3 4.9 %collective-permute-start.19 = (bf16[288,128]{1,0:T(8,128)(2,1)S(1)}, bf16[288,128]{1,0:T(8,128)(2,1)S(1)}, u32[]{:S(2)}, u32[]{:S(2)}) collective-permute-start(bf16[288,128]{1,0:T(8,128)(2,1)S(1)} %get-tuple-element.9), channel_id=1, source_target_pairs={{0,8},{4,12},{8,0},{12,4},{1,9},{5,13},{9,1},{13,5},{2,10},{6,14},... | collective-permute-start | bytes 221192 | tf_op jit(solution)/shard_map/ppermute | solution.py:552
  274.7 4.5 %collective-permute-start.21 = (bf16[288,128]{1,0:T(8,128)(2,1)S(1)}, bf16[288,128]{1,0:T(8,128)(2,1)S(1)}, u32[]{:S(2)}, u32[]{:S(2)}) collective-permute-start(bf16[288,128]{1,0:T(8,128)(2,1)S(1)} %get-tuple-element.8), channel_id=1, source_target_pairs={{0,12},{4,8},{8,4},{12,0},{1,13},{5,9},{9,5},{13,1},{2,14},{6,10},... | collective-permute-start | bytes 221192 | tf_op jit(solution)/shard_map/ppermute | solution.py:552
Sparse Core Ops, SparseCore 0:
  9.2 37.1 all-gather.2
  145.1 44.3 all-gather.4
  191.8 24.2 reduce-scatter.3
  218.2 22.5 reduce-scatter.5
  242.9 28.4 reduce-scatter.7
